TPU v7x, 512 devices: a whole 4x4x16 slice. The times are simulated.
512 devices in a mesh: tm: 32 (over z, x_hi), height: 16 (over x_lo, y, core).
Axes of the slice: x: 4 (x_hi: 2, x_lo: 2; x = x_hi * 2 + x_lo), y: 4, z: 16, core: 2. Of those that a mesh axis runs over, the one named last changes fastest.
Arguments:
- clip: bfloat16 [64, 64, 32, 128], P('tm', 'height'), may hold values from -6 to 6
- first_filter: bfloat16 [3, 3, 3, 128, 256], replicated, may hold values from -0.109375 to 0.109375
- second_filter: bfloat16 [3, 3, 3, 256, 256], P(None, None, None, None, 'height'), may hold values from -0.078125 to 0.078125
- upstream: bfloat16 [32, 32, 16, 256], P('tm', 'height'), may hold values from -6 to 6
Outputs:
- grad_clip: bfloat16 [64, 64, 32, 128], P('tm', 'height')
- grad_filter: float32 [3, 3, 3, 128, 256], P(None, None, None, 'tm', 'height')
All inputs are finite; a program needn't handle non-finite values.
Results may differ from a plain program's by a relative error of at most 0.0049.
Values may be sent and summed in bfloat16 or wider, within the bound.
No kernel may reach another device: no remote copies, remote signals or barrier semaphores. Data moves between devices by JAX's collectives and lax.ppermute only.
A program may use at most 64 MiB of HBM per device.

v0:
```python
import jax
import jax.numpy as jnp
from jax import lax
from jax.sharding import PartitionSpec as P


def passed_along(value, axis, by):
    size = lax.axis_size(axis)
    pairs = [(i, i + by) for i in range(size) if 0 <= i + by < size]
    return lax.ppermute(value, axis, pairs)


def extended(block, sides, width):
    for axis, dim in sides:
        count = lax.axis_size(axis)
        forward = [(i, i + 1) for i in range(count - 1)]
        backward = [(target, source) for source, target in forward]
        low = lax.ppermute(
            lax.slice_in_dim(block, block.shape[dim] - width, None, axis=dim), axis, forward
        )
        high = lax.ppermute(lax.slice_in_dim(block, 0, width, axis=dim), axis, backward)
        block = jnp.concatenate([low, block, high], axis=dim)
    return block


def conv_taps(padded, filt, frames, rows, width):
    cin = padded.shape[3]
    total = jnp.zeros((frames * rows * width, filt.shape[4]), jnp.float32)
    for tap_a in range(3):
        for tap_b in range(3):
            for tap_c in range(3):
                piece = padded[
                    tap_a : tap_a + frames, tap_b : tap_b + rows, tap_c : tap_c + width
                ].reshape(-1, cin)
                total = total + jnp.dot(
                    piece, filt[tap_a, tap_b, tap_c], preferred_element_type=jnp.float32
                )
    return total.reshape(frames, rows, width, -1)


def body(clip, first_filter, second_filter, upstream):
    frames, rows, width, cin = clip.shape
    chans = first_filter.shape[4]
    past = passed_along(clip, "tm", 1)
    timed = jnp.concatenate([past, clip], 0)
    banded = extended(timed, (("height", 1),), 1)
    padded = jnp.pad(banded, ((0, 0), (0, 0), (1, 1), (0, 0)))
    second = lax.all_gather(second_filter, "height", axis=4, tiled=True)
    preact = conv_taps(padded, first_filter, frames, rows, width)
    later = passed_along(upstream, "tm", -1)
    ext = jnp.concatenate([upstream, later], 0)
    below = passed_along(ext[:, :1], "height", -1)
    ext = jnp.concatenate([ext, below], 1)
    out_t, out_r, out_w = (ext.shape[0], ext.shape[1], ext.shape[2])
    flat = ext.reshape(-1, ext.shape[3])
    buffer = jnp.zeros((frames + 3, rows + 3, width + 2, chans), jnp.float32)
    for tap_a in range(3):
        for tap_b in range(3):
            for tap_c in range(3):
                contrib = jnp.dot(
                    flat, second[tap_a, tap_b, tap_c].T, preferred_element_type=jnp.float32
                )
                contrib = contrib.reshape(out_t, out_r, out_w, chans)
                buffer = buffer.at[
                    tap_a : tap_a + 2 * out_t : 2,
                    tap_b : tap_b + 2 * out_r : 2,
                    tap_c : tap_c + 2 * out_w : 2,
                ].add(contrib)
    grad_act = buffer[2 : frames + 2, 1 : rows + 1, 1 : width + 1]
    sig = jax.nn.sigmoid(preact)
    grad_pre = (grad_act * sig * (1.0 + preact * (1.0 - sig))).astype(jnp.bfloat16)
    dflat = grad_pre.reshape(-1, chans)
    parts = []
    for tap_a in range(3):
        for tap_b in range(3):
            for tap_c in range(3):
                piece = padded[
                    tap_a : tap_a + frames, tap_b : tap_b + rows, tap_c : tap_c + width
                ].reshape(-1, cin)
                parts.append(
                    lax.dot_general(
                        piece, dflat, (((0,), (0,)), ((), ())), preferred_element_type=jnp.float32
                    )
                )
    partial_grad = jnp.stack(parts).reshape(3, 3, 3, cin, chans)
    summed = lax.psum_scatter(partial_grad, "height", scatter_dimension=4, tiled=True)
    summed = lax.psum_scatter(summed, "tm", scatter_dimension=3, tiled=True)
    count = frames * lax.axis_size("tm") * rows * lax.axis_size("height") * width
    grad_filter = summed * (1.0 / float(count) ** 0.5)
    following = passed_along(grad_pre, "tm", -1)
    delta = jnp.concatenate([grad_pre, following], 0)
    delta = extended(delta, (("height", 1),), 1)
    padded_grad = jnp.pad(delta, ((0, 0), (0, 0), (1, 1), (0, 0)))
    total = jnp.zeros((frames * rows * width, cin), jnp.float32)
    for tap_a in range(3):
        for tap_b in range(3):
            for tap_c in range(3):
                piece = padded_grad[
                    2 - tap_a : 2 - tap_a + frames,
                    2 - tap_b : 2 - tap_b + rows,
                    2 - tap_c : 2 - tap_c + width,
                ].reshape(-1, chans)
                total = total + jnp.dot(
                    piece, first_filter[tap_a, tap_b, tap_c].T, preferred_element_type=jnp.float32
                )
    grad_clip = total.reshape(frames, rows, width, cin).astype(jnp.bfloat16)
    return (grad_clip, grad_filter)


def solution(mesh):
    in_specs = (
        P("tm", "height", None, None),
        P(),
        P(None, None, None, None, "height"),
        P("tm", "height", None, None),
    )
    out_specs = (P("tm", "height", None, None), P(None, None, None, "tm", "height"))
    return jax.shard_map(body, mesh=mesh, in_specs=in_specs, out_specs=out_specs, check_vma=False)
```

profile of v0, /device:TPU:8, one launch (start us, length us, event | category | flops | bytes accessed | tf_op | source)
XLA Modules:
  0.0 756.2 jit_solution(15366968102378210817)
XLA Ops:
  7.9 1.3 collective-permute-start
  9.2 6.1 collective-permute-start.2
  17.9 1.3 dynamic-slice
  19.2 1.3 dynamic-slice.2
  23.4 1.9 collective-permute-start.4
  25.3 2.4 collective-permute-start.3
  27.8 7.3 collective-permute-start.1
  40.3 18.2 %all-gather.2.cloned.1.call-done = bf16[3,3,3,256,256]{3,4,2,1,0:T(8,128)(2,1)} async-done(((bf16[3,3,3,256,16]{3,4,2,1,0:T(8,128)(2,1)}), bf16[3,3,3,256,256]{3,4,2,1,0:T(8,128)(2,1)}) %all-gather.2.cloned.1.call-update) | async-done | bytes 3538960 | tf_op jit(solution)/shard_map/all_gather | solution.py:48
  59.7 7.0 scatter_fusion
  67.8 6.6 scatter_fusion.1
  75.4 6.6 scatter_fusion.2
  83.1 6.6 scatter_fusion.3
  90.7 6.6 scatter_fusion.4
  98.4 6.6 scatter_fusion.5
  106.0 6.6 scatter_fusion.6
  113.7 6.6 scatter_fusion.7
  120.3 1.0 fusion.61
  121.4 6.6 scatter_fusion.8
  129.0 6.6 scatter_fusion.9
  135.6 1.0 fusion.59
  136.7 6.6 scatter_fusion.10
  144.3 6.8 scatter_fusion.11
  152.1 6.6 scatter_fusion.12
  159.8 6.6 scatter_fusion.13
  167.5 6.6 scatter_fusion.14
  175.1 6.6 scatter_fusion.15
  182.8 6.6 scatter_fusion.16
  190.4 6.6 scatter_fusion.17
  198.1 6.6 scatter_fusion.18
  205.7 6.6 scatter_fusion.19
  213.4 6.6 scatter_fusion.20
  221.0 6.6 scatter_fusion.21
  228.7 6.8 scatter_fusion.22
  236.6 6.6 scatter_fusion.23
  244.2 6.6 scatter_fusion.24
  251.9 6.6 scatter_fusion.25
  259.5 6.6 scatter_fusion.26
  266.3 1.3 collective-permute-start.5
  273.1 1.8 copy-done.2
  274.9 6.4 copy.214
  281.3 2.6 collective-permute-start.7
  284.0 1.9 collective-permute-start.6
  285.9 3.6 collective-permute-done.6
  290.2 1.1 copy-done.1
  296.4 130.6 %all-reduce.7.cloned.1.call-done = f32[3,3,3,128,256]{3,2,1,0,4:T(4,128)} async-done(((f32[3,3,3,128,256]{3,2,1,0,4:T(4,128)}), f32[3,3,3,128,256]{3,2,1,0,4:T(4,128)}) %all-reduce.7.cloned.1.call-update) | async-done | bytes 3538960
  428.1 1.8 copy.215
  430.7 317.2 %all-reduce.9.cloned.1.call-done = f32[3,3,3,128,16]{4,3,2,1,0:T(8,128)} async-done(((f32[3,3,3,128,16]{4,3,2,1,0:T(8,128)}), f32[3,3,3,128,16]{4,3,2,1,0:T(8,128)}) %all-reduce.9.cloned.1.call-update) | async-done | bytes 221200
  747.9 1.5 dynamic-slice_multiply_fusion
  (185 shorter events, 49.1 us)
Async XLA Ops:
  7.2 51.3 %all-gather.2.cloned.1.call-start = ((), (), s32[]{:S(2)}) async-start(), calls=%async_computation | async-start | bytes 3760128 | tf_op jit(solution)/shard_map/all_gather | solution.py:48
  7.9 419.2 %all-reduce.7.cloned.1.call-start = ((), (), s32[]{:S(2)}) async-start(), calls=%async_computation.1 | async-start | bytes 9437184
  7.9 19.8 %collective-permute-start = (bf16[1,2,16,256]{3,2,1,0:T(8,128)(2,1)}, bf16[1,2,16,256]{3,2,1,0:T(8,128)(2,1)S(1)}, u32[]{:S(2)}, u32[]{:S(2)}) collective-permute-start(bf16[1,2,16,256]{3,2,1,0:T(8,128)(2,1)} %param.7), channel_id=1, source_target_pairs={{16,0},{32,16},{48,32},{64,48},{80,64},{96,80},{112,96},{128,112},... | collective-permute-start | bytes 49160 | tf_op jit(solution)/shard_map/ppermute | solution.py:10
  9.2 13.3 %collective-permute-start.2 = (bf16[2,4,32,128]{3,2,1,0:T(8,128)(2,1)}, bf16[2,4,32,128]{3,2,1,0:T(8,128)(2,1)S(1)}, u32[]{:S(2)}, u32[]{:S(2)}) collective-permute-start(bf16[2,4,32,128]{3,2,1,0:T(8,128)(2,1)} %param.4), channel_id=1, source_target_pairs={{0,16},{16,32},{32,48},{48,64},{64,80},{80,96},{96,112},{112,128},... | collective-permute-start | bytes 196616 | tf_op jit(solution)/shard_map/ppermute | solution.py:10
  15.6 19.8 %copy-start = (bf16[3,3,3,128,256]{4,3,2,1,0:T(8,128)(2,1)S(1)}, bf16[3,3,3,128,256]{4,3,2,1,0:T(8,128)(2,1)}, u32[]{:S(2)}) copy-start(bf16[3,3,3,128,256]{4,3,2,1,0:T(8,128)(2,1)} %param.5) | copy-start | bytes 5308420
  23.4 11.7 %collective-permute-start.4 = (bf16[4,1,32,128]{3,2,1,0:T(8,128)(2,1)S(1)}, bf16[4,1,32,128]{3,2,1,0:T(8,128)(2,1)S(1)}, u32[]{:S(2)}, u32[]{:S(2)}) collective-permute-start(bf16[4,1,32,128]{3,2,1,0:T(8,128)(2,1)S(1)} %get-tuple-element.59), channel_id=1, source_target_pairs={{1,0},{2,1},{3,2},{4,3},{5,4},{6,5},{7,6},{8,7},{9,8},{10,9},{11,1... | collective-permute-start | bytes 98312 | tf_op jit(solution)/shard_map/ppermute | solution.py:21
  25.3 9.8 %collective-permute-start.3 = (bf16[4,1,32,128]{3,2,1,0:T(8,128)(2,1)S(1)}, bf16[4,1,32,128]{3,2,1,0:T(8,128)(2,1)S(1)}, u32[]{:S(2)}, u32[]{:S(2)}) collective-permute-start(bf16[4,1,32,128]{3,2,1,0:T(8,128)(2,1)S(1)} %get-tuple-element.58), channel_id=1, source_target_pairs={{0,1},{1,2},{2,3},{3,4},{4,5},{5,6},{6,7},{7,8},{8,9},{9,10},{10,1... | collective-permute-start | bytes 98312 | tf_op jit(solution)/shard_map/ppermute | solution.py:18
  27.8 12.5 %collective-permute-start.1 = (bf16[2,1,16,256]{3,2,1,0:T(8,128)(2,1)S(1)}, bf16[2,1,16,256]{3,2,1,0:T(8,128)(2,1)S(1)}, u32[]{:S(2)}, u32[]{:S(2)}) collective-permute-start(bf16[2,1,16,256]{3,2,1,0:T(8,128)(2,1)S(1)} %slice.615), channel_id=1, source_target_pairs={{1,0},{2,1},{3,2},{4,3},{5,4},{6,5},{7,6},{8,7},{9,8},{10,9},{11,1... | collective-permute-start | bytes 49160 | tf_op jit(solution)/shard_map/ppermute | solution.py:10
  38.5 0.9 copy-start.3
  266.3 15.0 %collective-permute-start.5 = (bf16[2,4,32,256]{3,2,1,0:T(8,128)(2,1)S(1)}, bf16[2,4,32,256]{3,2,1,0:T(8,128)(2,1)S(1)}, u32[]{:S(2)}, u32[]{:S(2)}) collective-permute-start(bf16[2,4,32,256]{3,2,1,0:T(8,128)(2,1)S(1)} %fusion.40), channel_id=1, source_target_pairs={{16,0},{32,16},{48,32},{64,48},{80,64},{96,80},{112,96},{128,112},... | collective-permute-start | bytes 393224 | tf_op jit(solution)/shard_map/ppermute | solution.py:10
  273.1 1.8 copy-start.2
  281.3 466.6 %all-reduce.9.cloned.1.call-start = ((), (), s32[]{:S(2)}) async-start(), calls=%async_computation.2 | async-start | bytes 3538944
  281.3 4.6 collective-permute-start.7
  284.0 5.6 collective-permute-start.6
  289.8 1.5 copy-start.1
Sparse Core Ops, SparseCore 0:
  10.1 48.3 all-gather.1
  281.4 145.6 all-reduce.6
  430.0 317.8 all-reduce.8
where the time goes:
time: 760 us; the launch traced here: 756 us
  waiting for transfers between devices  470 us (62%)
  other arithmetic  181 us (24%)
  matrix products  43.9 us (6%)
  starting transfers between devices  25 us (3%)
  local copies, waits for them, and re-layouts  19.3 us (3%)
  between operations  16.3 us (2%)
    unnamed x5, waiting for transfers between devices  449 us
    scatter-add x27, other arithmetic, body(): buffer = buffer.at[tap_a:tap_a + 2 * out_t:2, tap_b:tap_b + 2 * out_r:2,...  179 us
    dot_general x27, matrix products, body(): jnp.dot(flat, second[tap_a, tap_b, tap_c].T, preferred_element_type=jnp.f...  28.3 us
    all_gather x1, waiting for transfers between devices, body(): second = lax.all_gather(second_filter, 'height', axis=4, tiled=True)  18.2 us
    ppermute x4, starting transfers between devices, passed_along(): return lax.ppermute(value, axis, pairs)  16 us
  transfers between devices with their start and end apart: 11, of which 4 were waited for; matrix products, arithmetic and copies ran while one was open for 4% of the time, Pallas kernels for 0%

commit v1 on v0

v1 whole, which is shorter than its diff:
```python
import functools

import jax
import jax.numpy as jnp
from jax import lax
from jax.experimental import pallas as pl
from jax.experimental.pallas import tpu as pltpu
from jax.sharding import PartitionSpec as P

F32, BF16 = jnp.float32, jnp.bfloat16
CORES = 2
OWN = 64
FRAMES = 4
ROWS, SPAN = 8, 10
HIGH, HALF_HIGH, HALF = ROWS + 4, ROWS // 2 + 2, SPAN // 2
MIDDLE = (1, 2, 3, 0)

LONG = {0: ((2, 0),), 1: ((0, 0), (1, 1))}
WIDE = {0: ((1, 0), (2, 1)), 1: ((0, 1),)}


def shift_classes():
    classes = []
    for t in (1, 0):
        for h in (1, 0):
            for w in (0, 1):
                taps = tuple(
                    ((a, b, c), (fp, ip, jp))
                    for a, fp in LONG[t]
                    for b, ip in LONG[h]
                    for c, jp in WIDE[w]
                )
                classes.append(((t, h, w), taps))
    return classes


CLASSES = shift_classes()
TAP_ORDER = [tap for _, taps in CLASSES for tap, _ in taps]


def mm(lhs, rhs):
    return jnp.dot(lhs, rhs, preferred_element_type=F32)


def one_hot(rows, cols, column_of):
    row = lax.broadcasted_iota(jnp.int32, (rows, cols), 0)
    col = lax.broadcasted_iota(jnp.int32, (rows, cols), 1)
    return jnp.where(column_of(row) == col, 1.0, 0.0).astype(BF16)


def call(kernel, out, args, scratch=(), fetch=(), idle=(), alias=None, flops=0, limit=16):
    n_in, n_out, n_scratch = len(args), len(out), len(scratch)

    def run(*refs):
        ins, outs = list(refs[:n_in]), refs[n_in : n_in + n_out]
        rest = refs[n_in + n_out :]
        if fetch:
            landing, sems = rest[n_scratch:-1], rest[-1]
            copies = [
                pltpu.make_async_copy(ins[i], landing[k], sems.at[k]) for k, i in enumerate(fetch)
            ]
            for copy in copies:
                copy.start()
            for copy in copies:
                copy.wait()
            for k, i in enumerate(fetch):
                ins[i] = landing[k]
        kernel(*ins, *outs, *rest[:n_scratch])

    spec = pl.BlockSpec(memory_space=pltpu.VMEM)
    far = pl.BlockSpec(memory_space=pl.ANY)
    moved = sum(x.size * x.dtype.itemsize for x in list(args) + list(out))
    extra = [pltpu.VMEM(args[i].shape, args[i].dtype) for i in fetch]
    if fetch:
        extra.append(pltpu.SemaphoreType.DMA((len(fetch),)))
    return pl.pallas_call(
        run,
        out_shape=tuple(out),
        in_specs=[far if i in fetch or i in idle else spec for i in range(n_in)],
        out_specs=tuple([far if i in (alias or {}).values() else spec for i in range(n_out)]),
        input_output_aliases=dict(alias or {}),
        scratch_shapes=list(scratch) + extra,
        compiler_params=pltpu.CompilerParams(vmem_limit_bytes=limit * 1024 * 1024),
        cost_estimate=pl.CostEstimate(flops=flops, bytes_accessed=moved, transcendentals=0),
    )(*args)


def shaped(shape, dtype):
    return jax.ShapeDtypeStruct(shape, dtype)


def own_channel(place, x, core):
    return (2 * (place // 8) + core) * 16 + 8 * x + place % 8


def filter_pieces_kernel(second, out):
    taps, depth, chans = second.shape
    x = lax.axis_index("tm") % 2
    row = lax.broadcasted_iota(jnp.int32, (chans, 2 * OWN), 0)
    col = lax.broadcasted_iota(jnp.int32, (chans, 2 * OWN), 1)
    order = jnp.where(own_channel(col % OWN, x, col // OWN) == row, 1.0, 0.0).astype(BF16)
    moved = mm(second[...].reshape(taps * depth, chans), order).astype(BF16)
    moved = moved.reshape(taps, depth, 2 * OWN)
    for place in range(0, len(TAP_ORDER), 2):
        pair = TAP_ORDER[place : place + 2]
        for core in range(CORES):
            lanes = slice(core * OWN, (core + 1) * OWN)
            piece = jnp.concatenate([moved[a * 9 + b * 3 + c, :, lanes] for a, b, c in pair], 1)
            for p in range(core, out.shape[0], CORES):
                out[p, :, place * OWN : place * OWN + piece.shape[1]] = piece


def own_filter_kernel(first, band, turned):
    chans = first.shape[1]
    x, core = lax.axis_index("tm") % 2, lax.axis_index("height") % CORES

    def source(place):
        return own_channel(place % OWN, x, core)

    row = lax.broadcasted_iota(jnp.int32, (chans, 2 * OWN), 0)
    col = lax.broadcasted_iota(jnp.int32, (chans, 2 * OWN), 1)
    pick = jnp.where(source(col) == row, 1.0, 0.0).astype(BF16)
    twice = mm(first[...], pick)
    lane = lax.broadcasted_iota(jnp.int32, (128, 2 * OWN), 1)
    for ab in range(9):
        for s in range(4):
            left = twice[(ab * 3 + s) * 128 : (ab * 3 + s + 1) * 128] if s < 3 else 0.0
            right = twice[(ab * 3 + s - 1) * 128 : (ab * 3 + s) * 128] if s > 0 else 0.0
            both = jnp.where(lane < OWN, left, right)
            band[ab, s * 128 : (s + 1) * 128] = both.astype(BF16)
    row = lax.broadcasted_iota(jnp.int32, (OWN, chans), 0)
    col = lax.broadcasted_iota(jnp.int32, (OWN, chans), 1)
    pick = jnp.where(source(row) == col, 1.0, 0.0).astype(BF16)
    flat = lax.dot_general(
        pick, first[...], (((1,), (1,)), ((), ())), preferred_element_type=F32
    ).astype(BF16)
    for ab in range(9):
        for slot, s in enumerate(MIDDLE):
            for jp in range(2):
                c = jp + 2 - s
                if 0 <= c <= 2:
                    piece = flat[:, (ab * 3 + c) * 128 : (ab * 3 + c + 1) * 128]
                else:
                    piece = jnp.zeros((OWN, 128), BF16)
                turned[ab, slot * OWN : (slot + 1) * OWN, jp * 128 : (jp + 1) * 128] = piece


def stack_kernel(clip, up, out):
    for f in range(2):
        out[4 * f : 4 * f + 4] = clip[f]
    for half in range(2):
        out[8:10, 16 * half : 16 * half + 16] = up[0, :, :, 128 * half : 128 * half + 128]


def pack_kernel(here, pair, odd, even, _, packed, edge, __):
    first = lax.axis_index("tm") % 2 == 0
    at_top = lax.axis_index("height") % CORES == 0
    one = jnp.where(first, here[...], pair[...])
    two = jnp.where(first, pair[...], here[...])
    past = jnp.where(first, odd[...], even[...])
    next_up = jnp.where(first, even[8:10], odd[8:10])
    for f in range(6):
        src = (past, one, two)[f // 2][4 * (f % 2) : 4 * (f % 2) + 4]
        packed[4 * f : 4 * f + 4] = src
        edge[2 * f : 2 * f + 2] = jnp.where(at_top, src[:2], src[2:])
    for t, src in enumerate((one[8:10], two[8:10], next_up)):
        packed[24 + 2 * t : 26 + 2 * t] = src
        edge[12 + t] = jnp.where(at_top, src[0], src[1])


def preact_kernel(own, other, near, far, filters, wide, ups, pre, band, ext):
    member = lax.axis_index("height") % CORES
    even = member == 0
    above = jnp.where(even, near[...], far[...])
    below = jnp.where(even, far[...], near[...])
    for f in range(6):
        base = f * HIGH
        band[pl.ds(base + 2 + 4 * member, 4)] = own[4 * f : 4 * f + 4]
        band[pl.ds(base + 6 - 4 * member, 4)] = other[4 * f : 4 * f + 4]
        band[base : base + 2] = above[2 * f : 2 * f + 2]
        band[base + ROWS + 2 : base + ROWS + 4] = below[2 * f : 2 * f + 2]
    for t in range(3):
        base, unit = t * HALF_HIGH, 24 + 2 * t
        for half in range(2):
            lanes = slice(128 * half, 128 * half + 128)
            subs = slice(16 * half, 16 * half + 16)
            ext[pl.ds(base + 1 + 2 * member, 2), :, lanes] = own[unit : unit + 2, subs]
            ext[pl.ds(base + 3 - 2 * member, 2), :, lanes] = other[unit : unit + 2, subs]
            ext[base, :, lanes] = above[12 + t, subs]
            ext[base + HALF_HIGH - 1, :, lanes] = below[12 + t, subs]
    units = ext.shape[0]
    flat = ext[...].reshape(units * 16, 256)
    shift = one_hot(units * 16, units * 16, lambda r: jnp.where(r % 16 == 15, -1, r + 1))
    ups[0] = flat.reshape(units, 16, 256)
    ups[1] = mm(shift, flat).astype(BF16).reshape(units, 16, 256)

    def column(r):
        s, unit, w = r // 128, (r // 16) % 8, 2 * (r % 16) + r // 128 - 1
        return jnp.where((w >= 0) & (w < 32), unit * 32 + w, -1)

    matrix = one_hot(512, 256, column)
    for g in range(band.shape[0] // 8):
        moved = mm(matrix, band[8 * g : 8 * g + 8].reshape(256, 128)).astype(BF16)
        for s in range(4):
            piece = moved[128 * s : 128 * s + 128].reshape(8, 16, 128)
            wide[8 * g : 8 * g + 8, :, s * 128 : (s + 1) * 128] = piece
    total = jnp.zeros((FRAMES * SPAN * 16, 2 * OWN), F32)
    for a in range(3):
        for b in range(3):
            tops = [(a + f) * HIGH + b for f in range(FRAMES)]
            win = jnp.concatenate([wide[x : x + SPAN] for x in tops], 0)
            total = total + mm(win.reshape(FRAMES * SPAN * 16, 512), filters[a * 3 + b])
    total = total.reshape(FRAMES, SPAN, 16, 2 * OWN)
    for f in range(FRAMES):
        for r in range(SPAN):
            pre[f % 2, r % 2, f // 2, r // 2] = total[f, r]


def gradient_kernel(second, ups, pre, wide, grad, parts):
    group = lax.axis_index("height") // CORES
    first_band = group == 0
    last_band = group == lax.axis_size("height") // CORES - 1
    even, odd = {}, {}
    offset = 0
    for (t, h, w), taps in CLASSES:
        tops = [(t + q) * HALF_HIGH + h for q in range(2)]
        lhs = jnp.concatenate([ups[w, x : x + HALF] for x in tops], 0).reshape(32 * HALF, 256)
        prod = mm(lhs, second[:, offset : offset + len(taps) * OWN])
        offset += len(taps) * OWN
        total, step = (odd, 1) if w else (even, 2)
        for k in range(0, len(taps), step):
            key = taps[k][1][:2]
            piece = prod[:, k * OWN : (k + step) * OWN]
            total[key] = total[key] + piece if key in total else piece
    blank = jnp.zeros((32 * HALF, OWN), F32)
    for (fp, ip), act in even.items():
        act = act + jnp.concatenate([blank, odd[fp, ip]], 1)
        x = pre[fp, ip].reshape(32 * HALF, 2 * OWN)
        sig = jax.nn.sigmoid(x)
        g = (act * sig * (1.0 + x * (1.0 - sig))).reshape(2, HALF, 16, 2 * OWN)
        for q in range(2):
            for p in range(HALF):
                piece, r = g[q, p], 2 * p + ip
                if r == 0:
                    piece = jnp.where(first_band, 0.0, piece)
                if r == SPAN - 1:
                    piece = jnp.where(last_band, 0.0, piece)
                grad[2 * q + fp, r] = piece.astype(BF16)
    turned = grad[:, 1 : 1 + ROWS].reshape(FRAMES * ROWS * 16, 2 * OWN).T
    strips = []
    for a in range(3):
        for b in range(3):
            tops = [(a + f) * HIGH + 1 + b for f in range(FRAMES)]
            win = jnp.concatenate([wide[x : x + ROWS] for x in tops], 0)
            prod = mm(turned, win.reshape(FRAMES * ROWS * 16, 512))
            for c in range(3):
                piece = prod[:OWN, 128 * c : 128 * c + 128]
                piece = piece + prod[OWN:, 128 * c + 128 : 128 * c + 256]
                strips.append(piece.astype(BF16))
    strips.append(jnp.zeros_like(strips[0]))
    row = lax.broadcasted_iota(jnp.int32, (256, 256), 0)
    col = lax.broadcasted_iota(jnp.int32, (256, 256), 1)
    x, tap, z, e = col // 128, (col // 64) % 2, (col // 4) % 16, col % 4
    order = jnp.where(tap * 128 + 8 * z + 4 * x + e == row, 1.0, 0.0).astype(BF16)
    blocks = OWN // 8
    for k in range(7):
        pairs = [jnp.concatenate(strips[i : i + 2], 1) for i in (4 * k, 4 * k + 2)]
        pairs = [mm(pair, order).reshape(blocks, 8, 256) for pair in pairs]
        both = jnp.concatenate(pairs, 1).astype(BF16)
        for x in range(2):
            parts[x * blocks : (x + 1) * blocks, k] = both[:, :, 128 * x : 128 * x + 128]


def sum_turn_kernel(parts, out):
    blank = jnp.zeros((16, 128), F32)
    blocks = parts.shape[0] // 2
    halves = []
    for x in range(2):
        total = parts[x * blocks].astype(F32)
        for i in range(1, blocks):
            total = total + parts[x * blocks + i].astype(F32)
        halves += [total.reshape(112, 128), blank]
    flat = jnp.concatenate(halves, 0).T
    for z in range(16):
        rows = [(tap * 64 + z * 4, x) for x in range(2) for tap in range(2)]
        block = [flat[r : r + 4, 128 * x : 128 * x + 128] for r, x in rows]
        out[z] = jnp.concatenate(block, 0).astype(BF16)


def finish_kernel(scale, parts, out):
    total = parts[0].astype(F32)
    for i in range(1, parts.shape[0]):
        total = total + parts[i].astype(F32)
    total = total * scale
    for k in range(27):
        lanes = slice(8 * (k // 2), 8 * (k // 2) + 8)
        rows = [8 * x + 4 * (k % 2) for x in range(2)]
        out[k] = jnp.concatenate([total[r : r + 4, lanes] for r in rows], 1)


def clip_kernel(grad, following, filters, _, keep, send, wide):
    lane = lax.broadcasted_iota(jnp.int32, (192, 2 * OWN), 1)
    up = one_hot(192, 192, lambda r: jnp.where(r % 16 == 15, -1, r + 1))
    down = one_hot(192, 192, lambda r: jnp.where(r % 16 == 0, -1, r - 1))
    for f in range(FRAMES + 2):
        src = grad[f] if f < FRAMES else following[f - FRAMES]
        wide[f * SPAN : (f + 1) * SPAN, :, : 2 * OWN] = src
    for g in range(0, (FRAMES + 2) * SPAN, 12):
        block = wide[g : g + 12, :, : 2 * OWN].reshape(192, 2 * OWN)
        moved = jnp.where(lane < OWN, mm(up, block), mm(down, block)).astype(BF16)
        wide[g : g + 12, :, 2 * OWN :] = moved.reshape(12, 16, 2 * OWN)
    total = jnp.zeros((FRAMES * ROWS * 16, 256), F32)
    for a in range(3):
        for b in range(3):
            tops = [(f + 2 - a) * SPAN + 2 - b for f in range(FRAMES)]
            win = jnp.concatenate([wide[x : x + ROWS] for x in tops], 0)
            total = total + mm(win.reshape(FRAMES * ROWS * 16, 4 * OWN), filters[a * 3 + b])
    total = total.reshape(FRAMES, ROWS, 16, 256)
    low, high = total[:, :4], total[:, 4:]
    even = lax.axis_index("height") % CORES == 0
    keep[...] = jnp.where(even, low, high)
    send[...] = jnp.where(even, high, low)


def halve_kernel(kept, got, keep, send):
    total = kept[...] + got[...]
    first = lax.axis_index("tm") % 2 == 0
    low, high = total[:2], total[2:]
    keep[...] = jnp.where(first, low, high)
    send[...] = jnp.where(first, high, low).astype(BF16)


def join_kernel(kept, got, out):
    total = (kept[...] + got[...].astype(F32)).astype(BF16).reshape(128, 256)
    low = one_hot(256, 128, lambda r: jnp.where(r % 2 == 0, (r // 32) * 16 + (r % 32) // 2, -1))
    high = one_hot(256, 128, lambda r: jnp.where(r % 2 == 1, (r // 32) * 16 + (r % 32) // 2, -1))
    moved = mm(low, total[:, :128]) + mm(high, total[:, 128:])
    out[...] = moved.astype(BF16).reshape(out.shape)


def inside(pairs, count):
    return [(i, k) for i, k in pairs if 0 <= k < count]


def body(clip, first_filter, second_filter, upstream):
    frames, rows, width, cin = clip.shape
    chans = first_filter.shape[4]
    tms, heights = lax.axis_size("tm"), lax.axis_size("height")
    lines = tms // 2
    siblings = [(i, i ^ 1) for i in range(heights)]
    blocks = [(t, t ^ 1) for t in range(tms)]

    (here,) = call(stack_kernel, [shaped((10, 32, 128), BF16)], [clip, upstream], fetch=(0, 1), limit=60)
    pair = lax.ppermute(here, "tm", blocks)
    odd_pairs = inside([(t, t + 1 if t % 2 else t - 1) for t in range(tms)], tms)
    even_pairs = inside([(t, t + 2 if t % 2 else t - 2) for t in range(tms)], tms)
    odd = lax.ppermute(here, "tm", odd_pairs)
    even = lax.ppermute(here, "tm", even_pairs)

    second = jnp.swapaxes(second_filter, 3, 4).reshape(27, chans // heights, chans)
    (pieces,) = call(
        filter_pieces_kernel,
        [shaped((heights, chans // heights, 27 * OWN), BF16)],
        [second],
        fetch=(0,),
        flops=2 * 27 * 16 * 256 * 128,
    )
    band, turned = call(
        own_filter_kernel,
        [shaped((9, 512, 2 * OWN), BF16), shaped((9, 4 * OWN, 2 * cin), BF16)],
        [first_filter.reshape(27 * cin, chans)],
        fetch=(0,),
        flops=4 * 27 * 128 * 256 * 128,
    )

    packed, edge, pieces = call(
        pack_kernel,
        [shaped((30, 32, 128), BF16), shaped((15, 32, 128), BF16), shaped(pieces.shape, BF16)],
        [here, pair, odd, even, pieces],
        fetch=(1, 2, 3),
        idle=(4,),
        alias={4: 2},
    )
    second = lax.all_to_all(pieces, "height", 0, 0).reshape(chans, 27 * OWN)
    near_pairs = inside([(i, i + 1 if i % 2 else i - 1) for i in range(heights)], heights)
    far_pairs = inside([(i, i + 2 if i % 2 else i - 2) for i in range(heights)], heights)
    other = lax.ppermute(packed, "height", siblings)
    near = lax.ppermute(edge, "height", near_pairs)
    far = lax.ppermute(edge, "height", far_pairs)

    units, up_units = 6 * HIGH, 3 * HALF_HIGH
    wide, ups, pre = call(
        preact_kernel,
        [
            shaped((units, 16, 512), BF16),
            shaped((2, up_units, 16, 256), BF16),
            shaped((2, 2, 2, HALF, 16, 2 * OWN), F32),
        ],
        [packed, other, near, far, band],
        scratch=[pltpu.VMEM((units, 32, 128), BF16), pltpu.VMEM((up_units, 16, 256), BF16)],
        fetch=(1, 2, 3),
        flops=2 * 640 * 9 * 512 * 128,
    )
    grad_pre, parts = call(
        gradient_kernel,
        [shaped((FRAMES, SPAN, 16, 2 * OWN), BF16), shaped((heights, 7, 16, cin), BF16)],
        [second, ups, pre, wide],
        fetch=(0,),
        flops=2 * 512 * 9 * 512 * 128,
    )

    planes = [
        [(2 * z + x) * heights + CORES * g + core for x in range(2) for g in range(heights // 2)]
        for z in range(lines)
        for core in range(CORES)
    ]
    parts = lax.all_to_all(parts, ("tm", "height"), 0, 0, axis_index_groups=planes)
    (sums,) = call(sum_turn_kernel, [shaped((lines, 16, 128), BF16)], [parts], fetch=(0,))
    columns = [[2 * z + x for z in range(lines)] for x in range(2)]
    summed = lax.all_to_all(sums, "tm", 0, 0, axis_index_groups=columns)
    count = frames * tms * rows * heights * width
    (grad_filter,) = call(
        functools.partial(finish_kernel, 1.0 / float(count) ** 0.5),
        [shaped((27, cin // tms, chans // heights), F32)],
        [summed],
        fetch=(0,),
    )
    grad_filter = grad_filter.reshape(3, 3, 3, cin // tms, chans // heights)

    back = inside([(t, t - 2) for t in range(tms)], tms)
    following = lax.ppermute(grad_pre[:2], "tm", back)
    keep, send = call(
        clip_kernel,
        [shaped((FRAMES, rows, 16, 2 * cin), F32)] * 2,
        [grad_pre, following, turned, sums],
        scratch=[pltpu.VMEM(((FRAMES + 2) * SPAN, 16, 4 * OWN), BF16)],
        fetch=(1,),
        idle=(3,),
        flops=2 * 512 * 9 * 256 * 256,
    )
    got = lax.ppermute(send, "height", siblings)
    keep, send = call(
        halve_kernel,
        [shaped((2, rows, 16, 2 * cin), F32), shaped((2, rows, 16, 2 * cin), BF16)],
        [keep, got],
        fetch=(1,),
    )
    got = lax.ppermute(send, "tm", blocks)
    (grad_clip,) = call(join_kernel, [shaped(clip.shape, BF16)], [keep, got], fetch=(1,))
    return (grad_clip, grad_filter)


def solution(mesh):
    in_specs = (
        P("tm", "height", None, None),
        P(),
        P(None, None, None, None, "height"),
        P("tm", "height", None, None),
    )
    out_specs = (P("tm", "height", None, None), P(None, None, None, "tm", "height"))
    return jax.shard_map(body, mesh=mesh, in_specs=in_specs, out_specs=out_specs, check_vma=False)
```

time: 760 us -> 97.6 us (0.13)
  the two profiles are of different devices: /device:TPU:8 before, /device:TPU:1 now
where the time goes in v1:
time: 97.6 us; the launch traced here: 96.9 us
  starting transfers between devices  55.9 us (57%)
  waiting for transfers between devices  23.3 us (24%)
  Pallas kernels  14.7 us (15%)
  local copies, waits for them, and re-layouts  1.99 us (2%)
    pallas_call x11, Pallas kernels, call(): pl.pallas_call(run, out_shape=tuple(out), in_specs=[far if i in fetch or...  14.7 us
    all_to_all x1, starting transfers between devices, body(): summed = lax.all_to_all(sums, 'tm', 0, 0, axis_index_groups=columns)  12.1 us
    all_to_all x1, starting transfers between devices, body(): second = lax.all_to_all(pieces, 'height', 0, 0).reshape(chans, 27 * OWN)  10.3 us
    all_to_all x1, waiting for transfers between devices, body(): lax.all_to_all(parts, ('tm', 'height'), 0, 0, axis_index_groups=planes)  9.89 us
    ppermute x1, starting transfers between devices, body(): pair = lax.ppermute(here, 'tm', blocks)  8.99 us
    all_to_all x1, waiting for transfers between devices, body(): summed = lax.all_to_all(sums, 'tm', 0, 0, axis_index_groups=columns)  8.88 us
    all_to_all x1, starting transfers between devices, body(): lax.all_to_all(parts, ('tm', 'height'), 0, 0, axis_index_groups=planes)  8.19 us
    ppermute x1, starting transfers between devices, body(): far = lax.ppermute(edge, 'height', far_pairs)  3.43 us
  transfers between devices with their start and end apart: 12, of which 4 were waited for; matrix products, arithmetic and copies ran while one was open for 0% of the time, Pallas kernels for 8%

profile of v1, /device:TPU:1, one launch (start us, length us, event | category | flops | bytes accessed | tf_op | source)
XLA Modules:
  0.0 96.9 jit_solution(8732431658081993734)
XLA Ops:
  0.6 1.5 %shard_map.59.refs_0_ = bf16[10,32,128]{2,1,0:T(8,128)(2,1)} custom-call(bf16[2,4,32,128]{3,2,1,0:T(8,128)(2,1)} %refs_0_.1, bf16[1,2,16,256]{3,2,1,0:T(8,128)(2,1)} %refs_1_.1), custom_call_target="tpu_custom_call" | custom-call | bytes 163840 | tf_op jit(solution)/shard_map/pallas_call | solution.py:76
  2.1 0.0 copy-start.1
  2.1 1.4 %collective-permute-start.2 = (bf16[10,32,128]{2,1,0:T(8,128)(2,1)}, bf16[10,32,128]{2,1,0:T(8,128)(2,1)S(1)}, u32[]{:S(2)}, u32[]{:S(2)}) collective-permute-start(bf16[10,32,128]{2,1,0:T(8,128)(2,1)} %shard_map.59.refs_0_), channel_id=1, source_target_pairs={{16,48},{32,0},{48,80},{64,32},{80,112},{96,64},{112,144},{128,96}... | collective-permute-start | bytes 245768 | tf_op jit(solution)/shard_map/ppermute | solution.py:358
  3.6 0.7 collective-permute-start.1
  4.2 9.0 %collective-permute-start = (bf16[10,32,128]{2,1,0:T(8,128)(2,1)}, bf16[10,32,128]{2,1,0:T(8,128)(2,1)S(1)}, u32[]{:S(2)}, u32[]{:S(2)}) collective-permute-start(bf16[10,32,128]{2,1,0:T(8,128)(2,1)} %shard_map.59.refs_0_), channel_id=1, source_target_pairs={{0,16},{16,0},{32,48},{48,32},{64,80},{80,64},{96,112},{112,96},{1... | collective-permute-start | bytes 245768 | tf_op jit(solution)/shard_map/ppermute | solution.py:354
  13.2 0.0 copy-start.2
  13.3 0.9 copy-done.2
  14.2 1.5 %shard_map.60.refs_4_ = bf16[16,16,1728]{2,1,0:T(8,128)(2,1)} custom-call(bf16[27,16,256]{2,1,0:T(8,128)(2,1)S(1)} %bitcast.8), custom_call_target="tpu_custom_call" | custom-call | flops 28311552 | bytes 1105920 | tf_op jit(solution)/shard_map/pallas_call | solution.py:76
  15.7 0.0 collective-permute-done.2.refs_3_
  15.7 0.0 collective-permute-done.1.refs_2_
  15.8 0.0 collective-permute-done.refs_1_
  15.8 0.0 copy-done.1
  15.8 0.4 shard_map.61
  16.2 0.0 copy-start
  16.2 10.3 %all-to-all-start = ((bf16[16,16,1728]{2,1,0:T(8,128)(2,1)}), bf16[16,16,1728]{2,1,0:T(8,128)(2,1)S(1)}, u32[]{:S(2)}, u32[]{:S(2)}) async-start(bf16[16,16,1728]{2,1,0:T(8,128)(2,1)} %get-tuple-element.16), calls=%async_computation | async-start | bytes 1835008 | tf_op jit(solution)/shard_map/all_to_all | solution.py:384
  26.5 2.1 %collective-permute-start.3 = (bf16[30,32,128]{2,1,0:T(8,128)(2,1)S(1)}, bf16[30,32,128]{2,1,0:T(8,128)(2,1)S(1)}, u32[]{:S(2)}, u32[]{:S(2)}) collective-permute-start(bf16[30,32,128]{2,1,0:T(8,128)(2,1)S(1)} %get-tuple-element.17.refs_0_), channel_id=1, source_target_pairs={{0,1},{1,0},{2,3},{3,2},{4,5},{5,4},{6,7},{7,6},{8,9},{9,8},{10,11... | collective-permute-start | bytes 737288 | tf_op jit(solution)/shard_map/ppermute | solution.py:387
  28.6 3.4 %collective-permute-start.5 = (bf16[15,32,128]{2,1,0:T(8,128)(2,1)S(1)}, bf16[15,32,128]{2,1,0:T(8,128)(2,1)S(1)}, u32[]{:S(2)}, u32[]{:S(2)}) collective-permute-start(bf16[15,32,128]{2,1,0:T(8,128)(2,1)S(1)} %get-tuple-element.18), channel_id=1, source_target_pairs={{1,3},{2,0},{3,5},{4,2},{5,7},{6,4},{7,9},{8,6},{9,11},{10,8},{11,... | collective-permute-start | bytes 368648 | tf_op jit(solution)/shard_map/ppermute | solution.py:389
  32.1 2.3 %collective-permute-start.4 = (bf16[15,32,128]{2,1,0:T(8,128)(2,1)S(1)}, bf16[15,32,128]{2,1,0:T(8,128)(2,1)S(1)}, u32[]{:S(2)}, u32[]{:S(2)}) collective-permute-start(bf16[15,32,128]{2,1,0:T(8,128)(2,1)S(1)} %get-tuple-element.18), channel_id=1, source_target_pairs={{1,2},{2,1},{3,4},{4,3},{5,6},{6,5},{7,8},{8,7},{9,10},{10,9},{11,... | collective-permute-start | bytes 368648 | tf_op jit(solution)/shard_map/ppermute | solution.py:388
  34.4 0.0 copy-done
  34.4 1.5 %shard_map.62 = (bf16[9,512,128]{2,1,0:T(8,128)(2,1)S(1)}, bf16[9,256,256]{2,1,0:T(8,128)(2,1)S(1)}) custom-call(bf16[3456,256]{1,0:T(8,128)(2,1)S(1)} %bitcast.7), custom_call_target="tpu_custom_call" | custom-call | flops 452984832 | bytes 4128768 | tf_op jit(solution)/shard_map/pallas_call | solution.py:76
  35.9 0.0 copy-start.3
  35.9 1.0 %copy-done.3 = bf16[9,256,256]{2,1,0:T(8,128)(2,1)} copy-done((bf16[9,256,256]{2,1,0:T(8,128)(2,1)}, bf16[9,256,256]{2,1,0:T(8,128)(2,1)S(1)}, u32[]{:S(2)}) %copy-start.3) | copy-done | bytes 1179672
  37.0 1.8 %collective-permute-done.5.refs_3_ = bf16[15,32,128]{2,1,0:T(8,128)(2,1)S(1)} collective-permute-done((bf16[15,32,128]{2,1,0:T(8,128)(2,1)S(1)}, bf16[15,32,128]{2,1,0:T(8,128)(2,1)S(1)}, u32[]{:S(2)}, u32[]{:S(2)}) %collective-permute-start.5) | collective-permute-done | bytes 122912 | tf_op jit(solution)/shard_map/ppermute | solution.py:389
  38.7 2.8 %collective-permute-done.4.refs_2_ = bf16[15,32,128]{2,1,0:T(8,128)(2,1)S(1)} collective-permute-done((bf16[15,32,128]{2,1,0:T(8,128)(2,1)S(1)}, bf16[15,32,128]{2,1,0:T(8,128)(2,1)S(1)}, u32[]{:S(2)}, u32[]{:S(2)}) %collective-permute-start.4) | collective-permute-done | bytes 122912 | tf_op jit(solution)/shard_map/ppermute | solution.py:388
  41.5 0.0 collective-permute-done.3.refs_1_
  41.5 3.1 %shard_map.63 = (bf16[72,16,512]{2,1,0:T(8,128)(2,1)S(1)}, bf16[2,18,16,256]{3,2,1,0:T(8,128)(2,1)S(1)}, f32[2,2,2,5,16,128]{5,4,3,2,1,0:T(8,128)S(1)}) custom-call(bf16[30,32,128]{2,1,0:T(8,128)(2,1)S(1)} %get-tuple-element.17.refs_0_, bf16[30,32,128]{2,1,0:T(8,128)(2,1)S(1)} %collective-permute-done.3.refs_1_, ...), custom_call_target="tpu_custom_call" | custom-call | flops 754974720 | bytes 3719168 | tf_op jit(solution)/shard_map/pallas_call | solution.py:76
  44.6 0.0 all-to-all-done
  44.7 2.6 %shard_map.64 = (bf16[4,10,16,128]{3,2,1,0:T(8,128)(2,1)S(1)}, bf16[16,7,16,128]{3,2,1,0:T(8,128)(2,1)}) custom-call(bf16[256,1728]{1,0:T(8,128)(2,1)S(1)} %bitcast.6, bf16[2,18,16,256]{3,2,1,0:T(8,128)(2,1)S(1)} %get-tuple-element.20.refs_1_, f32[2,2,2,5,16,128]{5,4,3,2,1,0:T(8,128)S(1)} %get-tuple-element.21.refs_2_, ...), custom_call_target="tpu_custom_call" | custom-call | flops 603979776 | bytes 3309568 | tf_op jit(solution)/shard_map/pallas_call | solution.py:76
  47.3 0.0 copy-start.4
  47.3 8.2 %all-to-all-start.1 = ((bf16[16,7,16,128]{3,2,1,0:T(8,128)(2,1)}), bf16[16,7,16,128]{3,2,1,0:T(8,128)(2,1)S(1)}, u32[]{:S(2)}, u32[]{:S(2)}) async-start(bf16[16,7,16,128]{3,2,1,0:T(8,128)(2,1)} %get-tuple-element.25), calls=%async_computation.1 | async-start | bytes 917504 | tf_op jit(solution)/shard_map/all_to_all | solution.py:417
  55.5 1.3 %collective-permute-start.6 = (bf16[2,10,16,128]{3,2,1,0:T(8,128)(2,1)S(1)}, bf16[2,10,16,128]{3,2,1,0:T(8,128)(2,1)S(1)}, u32[]{:S(2)}, u32[]{:S(2)}) collective-permute-start(bf16[2,10,16,128]{3,2,1,0:T(8,128)(2,1)S(1)} %slice.3), channel_id=1, source_target_pairs={{32,0},{48,16},{64,32},{80,48},{96,64},{112,80},{128,96},{144,112}... | collective-permute-start | bytes 245768 | tf_op jit(solution)/shard_map/ppermute | solution.py:431
  56.8 9.9 %all-to-all-done.1.refs_0_ = bf16[16,7,16,128]{3,2,1,0:T(8,128)(2,1)S(1)} async-done(((bf16[16,7,16,128]{3,2,1,0:T(8,128)(2,1)}), bf16[16,7,16,128]{3,2,1,0:T(8,128)(2,1)S(1)}, u32[]{:S(2)}, u32[]{:S(2)}) %all-to-all-start.1) | async-done | bytes 458784 | tf_op jit(solution)/shard_map/all_to_all | solution.py:417
  66.7 1.0 %shard_map.65.refs_3_ = bf16[16,16,128]{2,1,0:T(8,128)(2,1)} custom-call(bf16[16,7,16,128]{3,2,1,0:T(8,128)(2,1)S(1)} %all-to-all-done.1.refs_0_), custom_call_target="tpu_custom_call" | custom-call | bytes 524288 | tf_op jit(solution)/shard_map/pallas_call | solution.py:76
  67.7 0.0 collective-permute-done.6.refs_1_
  67.7 0.0 copy-done.4
  67.8 1.2 %shard_map.66 = (f32[4,4,16,256]{3,2,1,0:T(8,128)S(1)}, f32[4,4,16,256]{3,2,1,0:T(8,128)S(1)}) custom-call(bf16[4,10,16,128]{3,2,1,0:T(8,128)(2,1)S(1)} %get-tuple-element.23.refs_0_, bf16[2,10,16,128]{3,2,1,0:T(8,128)(2,1)S(1)} %collective-permute-done.6.refs_1_, bf16[9,256,256]{2,1,0:T(8,128)(2,1)S(1)} %copy-done.4, bf16[16,16,128]{2,1,0:T(8,128)(2,1)} %shard_map.65.refs_3_), custom_call_target="tpu_custom_call" | custom-call | flops 603979776 | bytes 2015232 | tf_op jit(solution)/shard_map/pallas_call | solution.py:76
  68.9 2.4 %collective-permute-start.7 = (f32[4,4,16,256]{3,2,1,0:T(8,128)S(1)}, f32[4,4,16,256]{3,2,1,0:T(8,128)S(1)}, u32[]{:S(2)}, u32[]{:S(2)}) collective-permute-start(f32[4,4,16,256]{3,2,1,0:T(8,128)S(1)} %get-tuple-element.27), channel_id=1, source_target_pairs={{0,1},{1,0},{2,3},{3,2},{4,5},{5,4},{6,7},{7,6},{8,9},{9,8},{10,11... | collective-permute-start | bytes 786440 | tf_op jit(solution)/shard_map/ppermute | solution.py:441
  71.4 12.1 %all-to-all-start.2 = ((bf16[16,16,128]{2,1,0:T(8,128)(2,1)}), bf16[16,16,128]{2,1,0:T(8,128)(2,1)S(1)}, u32[]{:S(2)}, u32[]{:S(2)}) async-start(bf16[16,16,128]{2,1,0:T(8,128)(2,1)} %shard_map.65.refs_3_), calls=%async_computation.2 | async-start | bytes 131072 | tf_op jit(solution)/shard_map/all_to_all | solution.py:420
  83.5 0.0 collective-permute-done.7.refs_1_
  83.5 0.1 shard_map.67
  83.6 2.7 %collective-permute-start.8 = (bf16[2,4,16,256]{3,2,1,0:T(8,128)(2,1)S(1)}, bf16[2,4,16,256]{3,2,1,0:T(8,128)(2,1)S(1)}, u32[]{:S(2)}, u32[]{:S(2)}) collective-permute-start(bf16[2,4,16,256]{3,2,1,0:T(8,128)(2,1)S(1)} %get-tuple-element.29), channel_id=1, source_target_pairs={{0,16},{16,0},{32,48},{48,32},{64,80},{80,64},{96,112},{112,96},{1... | collective-permute-start | bytes 196616 | tf_op jit(solution)/shard_map/ppermute | solution.py:448
  86.2 8.9 %all-to-all-done.2.refs_0_ = bf16[16,16,128]{2,1,0:T(8,128)(2,1)S(1)} async-done(((bf16[16,16,128]{2,1,0:T(8,128)(2,1)}), bf16[16,16,128]{2,1,0:T(8,128)(2,1)S(1)}, u32[]{:S(2)}, u32[]{:S(2)}) %all-to-all-start.2) | async-done | bytes 65568 | tf_op jit(solution)/shard_map/all_to_all | solution.py:420
  95.1 0.8 shard_map.69
  95.9 0.0 collective-permute-done.8.refs_1_
  95.9 0.9 shard_map.68
  (1 shorter events, 0.0 us)
Async XLA Ops:
  2.1 13.6 %copy-start.1 = (bf16[10,32,128]{2,1,0:T(8,128)(2,1)S(1)}, bf16[10,32,128]{2,1,0:T(8,128)(2,1)}, u32[]{:S(2)}) copy-start(bf16[10,32,128]{2,1,0:T(8,128)(2,1)} %shard_map.59.refs_0_) | copy-start | bytes 245764
  2.1 13.6 %collective-permute-start.2 = (bf16[10,32,128]{2,1,0:T(8,128)(2,1)}, bf16[10,32,128]{2,1,0:T(8,128)(2,1)S(1)}, u32[]{:S(2)}, u32[]{:S(2)}) collective-permute-start(bf16[10,32,128]{2,1,0:T(8,128)(2,1)} %shard_map.59.refs_0_), channel_id=1, source_target_pairs={{16,48},{32,0},{48,80},{64,32},{80,112},{96,64},{112,144},{128,96}... | collective-permute-start | bytes 245768 | tf_op jit(solution)/shard_map/ppermute | solution.py:358
  3.6 12.2 %collective-permute-start.1 = (bf16[10,32,128]{2,1,0:T(8,128)(2,1)}, bf16[10,32,128]{2,1,0:T(8,128)(2,1)S(1)}, u32[]{:S(2)}, u32[]{:S(2)}) collective-permute-start(bf16[10,32,128]{2,1,0:T(8,128)(2,1)} %shard_map.59.refs_0_), channel_id=1, source_target_pairs={{16,32},{32,16},{48,64},{64,48},{80,96},{96,80},{112,128},{128,112... | collective-permute-start | bytes 245768 | tf_op jit(solution)/shard_map/ppermute | solution.py:357
  4.2 11.5 %collective-permute-start = (bf16[10,32,128]{2,1,0:T(8,128)(2,1)}, bf16[10,32,128]{2,1,0:T(8,128)(2,1)S(1)}, u32[]{:S(2)}, u32[]{:S(2)}) collective-permute-start(bf16[10,32,128]{2,1,0:T(8,128)(2,1)} %shard_map.59.refs_0_), channel_id=1, source_target_pairs={{0,16},{16,0},{32,48},{48,32},{64,80},{80,64},{96,112},{112,96},{1... | collective-permute-start | bytes 245768 | tf_op jit(solution)/shard_map/ppermute | solution.py:354
  13.2 0.9 copy-start.2
  16.2 18.2 %copy-start = (bf16[3,3,3,128,256]{4,3,2,1,0:T(8,128)(2,1)S(1)}, bf16[3,3,3,128,256]{4,3,2,1,0:T(8,128)(2,1)}, u32[]{:S(2)}) copy-start(bf16[3,3,3,128,256]{4,3,2,1,0:T(8,128)(2,1)} %param.5) | copy-start | bytes 5308420
  16.2 28.4 %all-to-all-start = ((bf16[16,16,1728]{2,1,0:T(8,128)(2,1)}), bf16[16,16,1728]{2,1,0:T(8,128)(2,1)S(1)}, u32[]{:S(2)}, u32[]{:S(2)}) async-start(bf16[16,16,1728]{2,1,0:T(8,128)(2,1)} %get-tuple-element.16), calls=%async_computation | async-start | bytes 1835008 | tf_op jit(solution)/shard_map/all_to_all | solution.py:384
  26.5 15.0 %collective-permute-start.3 = (bf16[30,32,128]{2,1,0:T(8,128)(2,1)S(1)}, bf16[30,32,128]{2,1,0:T(8,128)(2,1)S(1)}, u32[]{:S(2)}, u32[]{:S(2)}) collective-permute-start(bf16[30,32,128]{2,1,0:T(8,128)(2,1)S(1)} %get-tuple-element.17.refs_0_), channel_id=1, source_target_pairs={{0,1},{1,0},{2,3},{3,2},{4,5},{5,4},{6,7},{7,6},{8,9},{9,8},{10,11... | collective-permute-start | bytes 737288 | tf_op jit(solution)/shard_map/ppermute | solution.py:387
  28.6 10.1 %collective-permute-start.5 = (bf16[15,32,128]{2,1,0:T(8,128)(2,1)S(1)}, bf16[15,32,128]{2,1,0:T(8,128)(2,1)S(1)}, u32[]{:S(2)}, u32[]{:S(2)}) collective-permute-start(bf16[15,32,128]{2,1,0:T(8,128)(2,1)S(1)} %get-tuple-element.18), channel_id=1, source_target_pairs={{1,3},{2,0},{3,5},{4,2},{5,7},{6,4},{7,9},{8,6},{9,11},{10,8},{11,... | collective-permute-start | bytes 368648 | tf_op jit(solution)/shard_map/ppermute | solution.py:389
  32.1 9.4 %collective-permute-start.4 = (bf16[15,32,128]{2,1,0:T(8,128)(2,1)S(1)}, bf16[15,32,128]{2,1,0:T(8,128)(2,1)S(1)}, u32[]{:S(2)}, u32[]{:S(2)}) collective-permute-start(bf16[15,32,128]{2,1,0:T(8,128)(2,1)S(1)} %get-tuple-element.18), channel_id=1, source_target_pairs={{1,2},{2,1},{3,4},{4,3},{5,6},{6,5},{7,8},{8,7},{9,10},{10,9},{11,... | collective-permute-start | bytes 368648 | tf_op jit(solution)/shard_map/ppermute | solution.py:388
  35.9 1.0 %copy-start.3 = (bf16[9,256,256]{2,1,0:T(8,128)(2,1)}, bf16[9,256,256]{2,1,0:T(8,128)(2,1)S(1)}, u32[]{:S(2)}) copy-start(bf16[9,256,256]{2,1,0:T(8,128)(2,1)S(1)} %get-tuple-element.24.refs_2_) | copy-start | bytes 3538948
  47.3 20.5 %copy-start.4 = (bf16[9,256,256]{2,1,0:T(8,128)(2,1)S(1)}, bf16[9,256,256]{2,1,0:T(8,128)(2,1)}, u32[]{:S(2)}) copy-start(bf16[9,256,256]{2,1,0:T(8,128)(2,1)} %copy-done.3) | copy-start | bytes 3538948
  47.3 19.4 %all-to-all-start.1 = ((bf16[16,7,16,128]{3,2,1,0:T(8,128)(2,1)}), bf16[16,7,16,128]{3,2,1,0:T(8,128)(2,1)S(1)}, u32[]{:S(2)}, u32[]{:S(2)}) async-start(bf16[16,7,16,128]{3,2,1,0:T(8,128)(2,1)} %get-tuple-element.25), calls=%async_computation.1 | async-start | bytes 917504 | tf_op jit(solution)/shard_map/all_to_all | solution.py:417
  55.5 12.2 %collective-permute-start.6 = (bf16[2,10,16,128]{3,2,1,0:T(8,128)(2,1)S(1)}, bf16[2,10,16,128]{3,2,1,0:T(8,128)(2,1)S(1)}, u32[]{:S(2)}, u32[]{:S(2)}) collective-permute-start(bf16[2,10,16,128]{3,2,1,0:T(8,128)(2,1)S(1)} %slice.3), channel_id=1, source_target_pairs={{32,0},{48,16},{64,32},{80,48},{96,64},{112,80},{128,96},{144,112}... | collective-permute-start | bytes 245768 | tf_op jit(solution)/shard_map/ppermute | solution.py:431
  68.9 14.6 %collective-permute-start.7 = (f32[4,4,16,256]{3,2,1,0:T(8,128)S(1)}, f32[4,4,16,256]{3,2,1,0:T(8,128)S(1)}, u32[]{:S(2)}, u32[]{:S(2)}) collective-permute-start(f32[4,4,16,256]{3,2,1,0:T(8,128)S(1)} %get-tuple-element.27), channel_id=1, source_target_pairs={{0,1},{1,0},{2,3},{3,2},{4,5},{5,4},{6,7},{7,6},{8,9},{9,8},{10,11... | collective-permute-start | bytes 786440 | tf_op jit(solution)/shard_map/ppermute | solution.py:441
  71.4 23.7 %all-to-all-start.2 = ((bf16[16,16,128]{2,1,0:T(8,128)(2,1)}), bf16[16,16,128]{2,1,0:T(8,128)(2,1)S(1)}, u32[]{:S(2)}, u32[]{:S(2)}) async-start(bf16[16,16,128]{2,1,0:T(8,128)(2,1)} %shard_map.65.refs_3_), calls=%async_computation.2 | async-start | bytes 131072 | tf_op jit(solution)/shard_map/all_to_all | solution.py:420
  83.6 12.4 %collective-permute-start.8 = (bf16[2,4,16,256]{3,2,1,0:T(8,128)(2,1)S(1)}, bf16[2,4,16,256]{3,2,1,0:T(8,128)(2,1)S(1)}, u32[]{:S(2)}, u32[]{:S(2)}) collective-permute-start(bf16[2,4,16,256]{3,2,1,0:T(8,128)(2,1)S(1)} %get-tuple-element.29), channel_id=1, source_target_pairs={{0,16},{16,0},{32,48},{48,32},{64,80},{80,64},{96,112},{112,96},{1... | collective-permute-start | bytes 196616 | tf_op jit(solution)/shard_map/ppermute | solution.py:448

commit v2 on v1

--- a/solution.py
+++ b/solution.py
@@ -48,7 +48,7 @@
     return jnp.where(column_of(row) == col, 1.0, 0.0).astype(BF16)
 
 
-def call(kernel, out, args, scratch=(), fetch=(), idle=(), alias=None, flops=0, limit=16):
+def call(kernel, out, args, scratch=(), fetch=(), idle=(), flops=0, limit=16):
     n_in, n_out, n_scratch = len(args), len(out), len(scratch)
 
     def run(*refs):
@@ -77,8 +77,7 @@
         run,
         out_shape=tuple(out),
         in_specs=[far if i in fetch or i in idle else spec for i in range(n_in)],
-        out_specs=tuple([far if i in (alias or {}).values() else spec for i in range(n_out)]),
-        input_output_aliases=dict(alias or {}),
+        out_specs=tuple([spec] * n_out),
         scratch_shapes=list(scratch) + extra,
         compiler_params=pltpu.CompilerParams(vmem_limit_bytes=limit * 1024 * 1024),
         cost_estimate=pl.CostEstimate(flops=flops, bytes_accessed=moved, transcendentals=0),
@@ -152,7 +151,7 @@
         out[8:10, 16 * half : 16 * half + 16] = up[0, :, :, 128 * half : 128 * half + 128]
 
 
-def pack_kernel(here, pair, odd, even, _, packed, edge, __):
+def pack_kernel(here, pair, odd, even, packed, edge):
     first = lax.axis_index("tm") % 2 == 0
     at_top = lax.axis_index("height") % CORES == 0
     one = jnp.where(first, here[...], pair[...])
@@ -281,13 +280,14 @@
             total = total + parts[x * blocks + i].astype(F32)
         halves += [total.reshape(112, 128), blank]
     flat = jnp.concatenate(halves, 0).T
-    for z in range(16):
+    for i in range(16):
+        z = (i + 8) % 16
         rows = [(tap * 64 + z * 4, x) for x in range(2) for tap in range(2)]
         block = [flat[r : r + 4, 128 * x : 128 * x + 128] for r, x in rows]
-        out[z] = jnp.concatenate(block, 0).astype(BF16)
-
-
-def finish_kernel(scale, parts, out):
+        out[i] = jnp.concatenate(block, 0).astype(BF16)
+
+
+def finish_kernel(scale, parts, _, out):
     total = parts[0].astype(F32)
     for i in range(1, parts.shape[0]):
         total = total + parts[i].astype(F32)
@@ -298,7 +298,7 @@
         out[k] = jnp.concatenate([total[r : r + 4, lanes] for r in rows], 1)
 
 
-def clip_kernel(grad, following, filters, _, keep, send, wide):
+def clip_kernel(grad, following, filters, _, keep, core_send, block_send, cross_send, wide):
     lane = lax.broadcasted_iota(jnp.int32, (192, 2 * OWN), 1)
     up = one_hot(192, 192, lambda r: jnp.where(r % 16 == 15, -1, r + 1))
     down = one_hot(192, 192, lambda r: jnp.where(r % 16 == 0, -1, r - 1))
@@ -318,24 +318,23 @@
     total = total.reshape(FRAMES, ROWS, 16, 256)
     low, high = total[:, :4], total[:, 4:]
     even = lax.axis_index("height") % CORES == 0
-    keep[...] = jnp.where(even, low, high)
-    send[...] = jnp.where(even, high, low)
-
-
-def halve_kernel(kept, got, keep, send):
-    total = kept[...] + got[...]
     first = lax.axis_index("tm") % 2 == 0
-    low, high = total[:2], total[2:]
-    keep[...] = jnp.where(first, low, high)
-    send[...] = jnp.where(first, high, low).astype(BF16)
-
-
-def join_kernel(kept, got, out):
-    total = (kept[...] + got[...].astype(F32)).astype(BF16).reshape(128, 256)
+    mine, other = jnp.where(even, low, high), jnp.where(even, high, low)
+    keep[...] = jnp.where(first, mine[:2], mine[2:])
+    block_send[...] = jnp.where(first, mine[2:], mine[:2]).astype(BF16)
+    core_send[...] = jnp.where(first, other[:2], other[2:]).astype(BF16)
+    cross_send[...] = jnp.where(first, other[2:], other[:2]).astype(BF16)
+
+
+def join_kernel(kept, core_got, block_got, cross_got, out, mark):
+    total = kept[...] + core_got[...].astype(F32)
+    total = total + block_got[...].astype(F32) + cross_got[...].astype(F32)
+    total = total.astype(BF16).reshape(128, 256)
     low = one_hot(256, 128, lambda r: jnp.where(r % 2 == 0, (r // 32) * 16 + (r % 32) // 2, -1))
     high = one_hot(256, 128, lambda r: jnp.where(r % 2 == 1, (r // 32) * 16 + (r % 32) // 2, -1))
     moved = mm(low, total[:, :128]) + mm(high, total[:, 128:])
     out[...] = moved.astype(BF16).reshape(out.shape)
+    mark[...] = jnp.zeros_like(mark)
 
 
 def inside(pairs, count):
@@ -350,13 +349,6 @@
     siblings = [(i, i ^ 1) for i in range(heights)]
     blocks = [(t, t ^ 1) for t in range(tms)]
 
-    (here,) = call(stack_kernel, [shaped((10, 32, 128), BF16)], [clip, upstream], fetch=(0, 1), limit=60)
-    pair = lax.ppermute(here, "tm", blocks)
-    odd_pairs = inside([(t, t + 1 if t % 2 else t - 1) for t in range(tms)], tms)
-    even_pairs = inside([(t, t + 2 if t % 2 else t - 2) for t in range(tms)], tms)
-    odd = lax.ppermute(here, "tm", odd_pairs)
-    even = lax.ppermute(here, "tm", even_pairs)
-
     second = jnp.swapaxes(second_filter, 3, 4).reshape(27, chans // heights, chans)
     (pieces,) = call(
         filter_pieces_kernel,
@@ -365,6 +357,15 @@
         fetch=(0,),
         flops=2 * 27 * 16 * 256 * 128,
     )
+    second = lax.all_to_all(pieces, "height", 0, 0).reshape(chans, 27 * OWN)
+
+    (here,) = call(stack_kernel, [shaped((10, 32, 128), BF16)], [clip, upstream], fetch=(0, 1), limit=60)
+    pair = lax.ppermute(here, "tm", blocks)
+    odd_pairs = inside([(t, t + 1 if t % 2 else t - 1) for t in range(tms)], tms)
+    even_pairs = inside([(t, t + 2 if t % 2 else t - 2) for t in range(tms)], tms)
+    odd = lax.ppermute(here, "tm", odd_pairs)
+    even = lax.ppermute(here, "tm", even_pairs)
+
     band, turned = call(
         own_filter_kernel,
         [shaped((9, 512, 2 * OWN), BF16), shaped((9, 4 * OWN, 2 * cin), BF16)],
@@ -373,15 +374,12 @@
         flops=4 * 27 * 128 * 256 * 128,
     )
 
-    packed, edge, pieces = call(
+    packed, edge = call(
         pack_kernel,
-        [shaped((30, 32, 128), BF16), shaped((15, 32, 128), BF16), shaped(pieces.shape, BF16)],
-        [here, pair, odd, even, pieces],
+        [shaped((30, 32, 128), BF16), shaped((15, 32, 128), BF16)],
+        [here, pair, odd, even],
         fetch=(1, 2, 3),
-        idle=(4,),
-        alias={4: 2},
-    )
-    second = lax.all_to_all(pieces, "height", 0, 0).reshape(chans, 27 * OWN)
+    )
     near_pairs = inside([(i, i + 1 if i % 2 else i - 1) for i in range(heights)], heights)
     far_pairs = inside([(i, i + 2 if i % 2 else i - 2) for i in range(heights)], heights)
     other = lax.ppermute(packed, "height", siblings)
@@ -416,37 +414,41 @@
     ]
     parts = lax.all_to_all(parts, ("tm", "height"), 0, 0, axis_index_groups=planes)
     (sums,) = call(sum_turn_kernel, [shaped((lines, 16, 128), BF16)], [parts], fetch=(0,))
-    columns = [[2 * z + x for z in range(lines)] for x in range(2)]
+    columns = [[2 * ((i + 8) % lines) + x for i in range(lines)] for x in range(2)]
     summed = lax.all_to_all(sums, "tm", 0, 0, axis_index_groups=columns)
-    count = frames * tms * rows * heights * width
-    (grad_filter,) = call(
-        functools.partial(finish_kernel, 1.0 / float(count) ** 0.5),
-        [shaped((27, cin // tms, chans // heights), F32)],
-        [summed],
-        fetch=(0,),
-    )
-    grad_filter = grad_filter.reshape(3, 3, 3, cin // tms, chans // heights)
 
     back = inside([(t, t - 2) for t in range(tms)], tms)
     following = lax.ppermute(grad_pre[:2], "tm", back)
-    keep, send = call(
+    part = (2, rows, 16, 2 * cin)
+    keep, core_send, block_send, cross_send = call(
         clip_kernel,
-        [shaped((FRAMES, rows, 16, 2 * cin), F32)] * 2,
+        [shaped(part, F32)] + [shaped(part, BF16)] * 3,
         [grad_pre, following, turned, sums],
         scratch=[pltpu.VMEM(((FRAMES + 2) * SPAN, 16, 4 * OWN), BF16)],
         fetch=(1,),
         idle=(3,),
         flops=2 * 512 * 9 * 256 * 256,
     )
-    got = lax.ppermute(send, "height", siblings)
-    keep, send = call(
-        halve_kernel,
-        [shaped((2, rows, 16, 2 * cin), F32), shaped((2, rows, 16, 2 * cin), BF16)],
-        [keep, got],
-        fetch=(1,),
-    )
-    got = lax.ppermute(send, "tm", blocks)
-    (grad_clip,) = call(join_kernel, [shaped(clip.shape, BF16)], [keep, got], fetch=(1,))
+    crosses = [(t * heights + h, k * heights + i) for t, k in blocks for h, i in siblings]
+    core_got = lax.ppermute(core_send, "height", siblings)
+    block_got = lax.ppermute(block_send, "tm", blocks)
+    cross_got = lax.ppermute(cross_send, ("tm", "height"), crosses)
+    grad_clip, mark = call(
+        join_kernel,
+        [shaped(clip.shape, BF16), shaped((8, 128), F32)],
+        [keep, core_got, block_got, cross_got],
+        fetch=(1, 2, 3),
+    )
+
+    count = frames * tms * rows * heights * width
+    (grad_filter,) = call(
+        functools.partial(finish_kernel, 1.0 / float(count) ** 0.5),
+        [shaped((27, cin // tms, chans // heights), F32)],
+        [summed, mark],
+        fetch=(0,),
+        idle=(1,),
+    )
+    grad_filter = grad_filter.reshape(3, 3, 3, cin // tms, chans // heights)
     return (grad_clip, grad_filter)
 
 

time: 97.6 us -> 104 us (1.066)
  blocking collectives: 0 us -> 16.2 us
  waiting for transfers between devices: 23.3 us -> 15.9 us
  starting transfers between devices: 55.9 us -> 53.9 us
    all_to_all x0 -> x1, blocking collectives: none -> 16.2 us  [body(): lax.all_to_all(parts, ('tm', 'height'), 0, 0, axis_index_groups=planes)]
    all_to_all x1 -> x0, waiting for transfers between devices: 9.89 us -> none  [body(): lax.all_to_all(parts, ('tm', 'height'), 0, 0, axis_index_groups=planes)]
    ppermute x2 -> x3, starting transfers between devices: 5.11 us -> 14.5 us  [the longest x1 7.57 us: body(): core_got = lax.ppermute(core_send, 'height', siblings)]
    all_to_all x1, waiting for transfers between devices: 8.88 us -> 0.01 us  [body(): summed = lax.all_to_all(sums, 'tm', 0, 0, axis_index_groups=columns)]
    ppermute x1, waiting for transfers between devices: 0.01 us -> 8.55 us  [body(): pair = lax.ppermute(here, 'tm', blocks)]
    all_to_all x1 -> x0, starting transfers between devices: 8.19 us -> none  [body(): lax.all_to_all(parts, ('tm', 'height'), 0, 0, axis_index_groups=planes)]
    ppermute x1, starting transfers between devices: 8.99 us -> 1.92 us  [body(): pair = lax.ppermute(here, 'tm', blocks)]
    ppermute x1, waiting for transfers between devices: 0.01 us -> 4.18 us  [body(): following = lax.ppermute(grad_pre[:2], 'tm', back)]
where the time goes in v2:
time: 104 us
  starting transfers between devices  53.9 us (52%)
  blocking collectives  16.2 us (16%)
  waiting for transfers between devices  15.9 us (15%)
  Pallas kernels  14 us (13%)
  local copies, waits for them, and re-layouts  2.85 us (3%)
    all_to_all x1, blocking collectives, body(): lax.all_to_all(parts, ('tm', 'height'), 0, 0, axis_index_groups=planes)  16.2 us
    all_to_all x1, starting transfers between devices, body(): summed = lax.all_to_all(sums, 'tm', 0, 0, axis_index_groups=columns)  14.3 us
    pallas_call x10, Pallas kernels, call(): pl.pallas_call(run, out_shape=tuple(out), in_specs=[far if i in fetch or...  14 us
    all_to_all x1, starting transfers between devices, body(): second = lax.all_to_all(pieces, 'height', 0, 0).reshape(chans, 27 * OWN)  10.4 us
    ppermute x1, waiting for transfers between devices, body(): pair = lax.ppermute(here, 'tm', blocks)  8.55 us
    ppermute x1, starting transfers between devices, body(): core_got = lax.ppermute(core_send, 'height', siblings)  7.57 us
    ppermute x1, starting transfers between devices, body(): cross_got = lax.ppermute(cross_send, ('tm', 'height'), crosses)  4.26 us
    ppermute x1, waiting for transfers between devices, body(): following = lax.ppermute(grad_pre[:2], 'tm', back)  4.18 us
  transfers between devices with their start and end apart: 12, of which 4 were waited for; matrix products, arithmetic and copies ran while one was open for 0% of the time, Pallas kernels for 8%

profile of v2, /device:TPU:1, one launch (start us, length us, event | category | flops | bytes accessed | tf_op | source)
XLA Modules:
  0.0 103.7 jit_solution(8452660190079077528)
XLA Ops:
  0.6 0.0 copy-start.2
  0.6 0.9 copy-done.2
  1.6 1.6 %shard_map.59 = bf16[16,16,1728]{2,1,0:T(8,128)(2,1)} custom-call(bf16[27,16,256]{2,1,0:T(8,128)(2,1)S(1)} %bitcast.8), custom_call_target="tpu_custom_call" | custom-call | flops 28311552 | bytes 1105920 | tf_op jit(solution)/shard_map/pallas_call | solution.py:76
  3.1 0.0 copy-start
  3.1 10.4 %all-to-all-start = ((bf16[16,16,1728]{2,1,0:T(8,128)(2,1)}), bf16[16,16,1728]{2,1,0:T(8,128)(2,1)S(1)}, u32[]{:S(2)}, u32[]{:S(2)}) async-start(bf16[16,16,1728]{2,1,0:T(8,128)(2,1)} %shard_map.59), calls=%async_computation | async-start | bytes 1835008 | tf_op jit(solution)/shard_map/all_to_all | solution.py:360
  13.6 1.5 %shard_map.60.refs_0_ = bf16[10,32,128]{2,1,0:T(8,128)(2,1)} custom-call(bf16[2,4,32,128]{3,2,1,0:T(8,128)(2,1)} %refs_0_.1, bf16[1,2,16,256]{3,2,1,0:T(8,128)(2,1)} %refs_1_.1), custom_call_target="tpu_custom_call" | custom-call | bytes 163840 | tf_op jit(solution)/shard_map/pallas_call | solution.py:76
  15.1 1.9 %collective-permute-start = (bf16[10,32,128]{2,1,0:T(8,128)(2,1)}, bf16[10,32,128]{2,1,0:T(8,128)(2,1)S(1)}, u32[]{:S(2)}, u32[]{:S(2)}) collective-permute-start(bf16[10,32,128]{2,1,0:T(8,128)(2,1)} %shard_map.60.refs_0_), channel_id=1, source_target_pairs={{0,16},{16,0},{32,48},{48,32},{64,80},{80,64},{96,112},{112,96},{1... | collective-permute-start | bytes 245768 | tf_op jit(solution)/shard_map/ppermute | solution.py:363
  17.0 0.7 collective-permute-start.1
  17.7 1.3 %collective-permute-start.2 = (bf16[10,32,128]{2,1,0:T(8,128)(2,1)}, bf16[10,32,128]{2,1,0:T(8,128)(2,1)S(1)}, u32[]{:S(2)}, u32[]{:S(2)}) collective-permute-start(bf16[10,32,128]{2,1,0:T(8,128)(2,1)} %shard_map.60.refs_0_), channel_id=1, source_target_pairs={{16,48},{32,0},{48,80},{64,32},{80,112},{96,64},{112,144},{128,96}... | collective-permute-start | bytes 245768 | tf_op jit(solution)/shard_map/ppermute | solution.py:367
  19.0 8.5 %collective-permute-done.refs_1_ = bf16[10,32,128]{2,1,0:T(8,128)(2,1)S(1)} collective-permute-done((bf16[10,32,128]{2,1,0:T(8,128)(2,1)}, bf16[10,32,128]{2,1,0:T(8,128)(2,1)S(1)}, u32[]{:S(2)}, u32[]{:S(2)}) %collective-permute-start) | collective-permute-done | bytes 81952 | tf_op jit(solution)/shard_map/ppermute | solution.py:363
  27.5 0.0 collective-permute-done.1.refs_2_
  27.5 0.0 collective-permute-done.2.refs_3_
  27.5 0.0 copy-start.1
  27.5 0.9 copy-done.1
  28.4 0.4 shard_map.61
  28.8 3.0 %collective-permute-start.3 = (bf16[30,32,128]{2,1,0:T(8,128)(2,1)S(1)}, bf16[30,32,128]{2,1,0:T(8,128)(2,1)S(1)}, u32[]{:S(2)}, u32[]{:S(2)}) collective-permute-start(bf16[30,32,128]{2,1,0:T(8,128)(2,1)S(1)} %get-tuple-element.17.refs_0_), channel_id=1, source_target_pairs={{0,1},{1,0},{2,3},{3,2},{4,5},{5,4},{6,7},{7,6},{8,9},{9,8},{10,11... | collective-permute-start | bytes 737288 | tf_op jit(solution)/shard_map/ppermute | solution.py:385
  31.8 3.3 %collective-permute-start.4 = (bf16[15,32,128]{2,1,0:T(8,128)(2,1)S(1)}, bf16[15,32,128]{2,1,0:T(8,128)(2,1)S(1)}, u32[]{:S(2)}, u32[]{:S(2)}) collective-permute-start(bf16[15,32,128]{2,1,0:T(8,128)(2,1)S(1)} %get-tuple-element.18), channel_id=1, source_target_pairs={{1,2},{2,1},{3,4},{4,3},{5,6},{6,5},{7,8},{8,7},{9,10},{10,9},{11,... | collective-permute-start | bytes 368648 | tf_op jit(solution)/shard_map/ppermute | solution.py:386
  35.2 3.1 %collective-permute-start.5 = (bf16[15,32,128]{2,1,0:T(8,128)(2,1)S(1)}, bf16[15,32,128]{2,1,0:T(8,128)(2,1)S(1)}, u32[]{:S(2)}, u32[]{:S(2)}) collective-permute-start(bf16[15,32,128]{2,1,0:T(8,128)(2,1)S(1)} %get-tuple-element.18), channel_id=1, source_target_pairs={{1,3},{2,0},{3,5},{4,2},{5,7},{6,4},{7,9},{8,6},{9,11},{10,8},{11,... | collective-permute-start | bytes 368648 | tf_op jit(solution)/shard_map/ppermute | solution.py:387
  38.3 0.0 copy-done
  38.3 1.5 %shard_map.62 = (bf16[9,512,128]{2,1,0:T(8,128)(2,1)S(1)}, bf16[9,256,256]{2,1,0:T(8,128)(2,1)S(1)}) custom-call(bf16[3456,256]{1,0:T(8,128)(2,1)S(1)} %bitcast.7), custom_call_target="tpu_custom_call" | custom-call | flops 452984832 | bytes 4128768 | tf_op jit(solution)/shard_map/pallas_call | solution.py:76
  39.8 0.0 copy-start.3
  39.9 1.0 copy-done.3
  40.9 0.0 collective-permute-done.4.refs_2_
  40.9 0.0 collective-permute-done.5.refs_3_
  40.9 0.0 collective-permute-done.3.refs_1_
  40.9 3.1 %shard_map.63 = (bf16[72,16,512]{2,1,0:T(8,128)(2,1)S(1)}, bf16[2,18,16,256]{3,2,1,0:T(8,128)(2,1)S(1)}, f32[2,2,2,5,16,128]{5,4,3,2,1,0:T(8,128)S(1)}) custom-call(bf16[30,32,128]{2,1,0:T(8,128)(2,1)S(1)} %get-tuple-element.17.refs_0_, bf16[30,32,128]{2,1,0:T(8,128)(2,1)S(1)} %collective-permute-done.3.refs_1_, ...), custom_call_target="tpu_custom_call" | custom-call | flops 754974720 | bytes 3719168 | tf_op jit(solution)/shard_map/pallas_call | solution.py:76
  44.0 0.0 all-to-all-done
  44.1 1.8 %shard_map.64 = (bf16[4,10,16,128]{3,2,1,0:T(8,128)(2,1)S(1)}, bf16[16,7,16,128]{3,2,1,0:T(8,128)(2,1)S(1)}) custom-call(bf16[256,1728]{1,0:T(8,128)(2,1)S(1)} %bitcast.6, bf16[2,18,16,256]{3,2,1,0:T(8,128)(2,1)S(1)} %get-tuple-element.20.refs_1_, f32[2,2,2,5,16,128]{5,4,3,2,1,0:T(8,128)S(1)} %get-tuple-element.21.refs_2_, ...), custom_call_target="tpu_custom_call" | custom-call | flops 603979776 | bytes 3309568 | tf_op jit(solution)/shard_map/pallas_call | solution.py:76
  45.9 0.0 copy-start.4
  45.9 16.2 %all_to_all.15.refs_0_ = bf16[16,7,16,128]{3,2,1,0:T(8,128)(2,1)S(1)} all-to-all(bf16[16,7,16,128]{3,2,1,0:T(8,128)(2,1)S(1)} %get-tuple-element.25), channel_id=1, replica_groups={{0,2,4,6,8,10,12,14,16,18,20,22,24,26,28,30},{1,3,5,7,9,11,13,15,17,19,..., dimensions={0} | all-to-all | bytes 917504 | tf_op jit(solution)/shard_map/all_to_all | solution.py:415
  62.1 1.0 %shard_map.65.refs_3_ = bf16[16,16,128]{2,1,0:T(8,128)(2,1)} custom-call(bf16[16,7,16,128]{3,2,1,0:T(8,128)(2,1)S(1)} %all_to_all.15.refs_0_), custom_call_target="tpu_custom_call" | custom-call | bytes 524288 | tf_op jit(solution)/shard_map/pallas_call | solution.py:76
  63.1 14.3 %all-to-all-start.2 = ((bf16[16,16,128]{2,1,0:T(8,128)(2,1)}), bf16[16,16,128]{2,1,0:T(8,128)(2,1)S(1)}, u32[]{:S(2)}, u32[]{:S(2)}) async-start(bf16[16,16,128]{2,1,0:T(8,128)(2,1)} %shard_map.65.refs_3_), calls=%async_computation.2 | async-start | bytes 131072 | tf_op jit(solution)/shard_map/all_to_all | solution.py:418
  77.4 1.3 %collective-permute-start.6 = (bf16[2,10,16,128]{3,2,1,0:T(8,128)(2,1)S(1)}, bf16[2,10,16,128]{3,2,1,0:T(8,128)(2,1)S(1)}, u32[]{:S(2)}, u32[]{:S(2)}) collective-permute-start(bf16[2,10,16,128]{3,2,1,0:T(8,128)(2,1)S(1)} %slice.3), channel_id=1, source_target_pairs={{32,0},{48,16},{64,32},{80,48},{96,64},{112,80},{128,96},{144,112}... | collective-permute-start | bytes 245768 | tf_op jit(solution)/shard_map/ppermute | solution.py:421
  78.7 4.2 %collective-permute-done.6.refs_1_ = bf16[2,10,16,128]{3,2,1,0:T(8,128)(2,1)S(1)} collective-permute-done((bf16[2,10,16,128]{3,2,1,0:T(8,128)(2,1)S(1)}, bf16[2,10,16,128]{3,2,1,0:T(8,128)(2,1)S(1)}, u32[]{:S(2)}, u32[]{:S(2)}) %collective-permute-start.6) | collective-permute-done | bytes 81952 | tf_op jit(solution)/shard_map/ppermute | solution.py:421
  82.9 0.0 copy-done.4
  82.9 1.1 %shard_map.66 = (f32[2,4,16,256]{3,2,1,0:T(8,128)S(1)}, bf16[2,4,16,256]{3,2,1,0:T(8,128)(2,1)S(1)}, bf16[2,4,16,256]{3,2,1,0:T(8,128)(2,1)S(1)}, bf16[2,4,16,256]{3,2,1,0:T(8,128)(2,1)S(1)}) custom-call(bf16[4,10,16,128]{3,2,1,0:T(8,128)(2,1)S(1)} %get-tuple-element.23.refs_0_, bf16[2,10,16,128]{3,2,1,0:T(8,128)(2,1)S(1)} %collective-permute-done.6.refs_1_, ...), custom_call_target="tpu_custom_call" | custom-call | flops 603979776 | bytes 1818624 | tf_op jit(solution)/shard_map/pallas_call | solution.py:76
  84.1 7.6 %collective-permute-start.7 = (bf16[2,4,16,256]{3,2,1,0:T(8,128)(2,1)S(1)}, bf16[2,4,16,256]{3,2,1,0:T(8,128)(2,1)S(1)}, u32[]{:S(2)}, u32[]{:S(2)}) collective-permute-start(bf16[2,4,16,256]{3,2,1,0:T(8,128)(2,1)S(1)} %get-tuple-element.27), channel_id=1, source_target_pairs={{0,1},{1,0},{2,3},{3,2},{4,5},{5,4},{6,7},{7,6},{8,9},{9,8},{10,11... | collective-permute-start | bytes 196616 | tf_op jit(solution)/shard_map/ppermute | solution.py:433
  91.7 2.7 %collective-permute-start.8 = (bf16[2,4,16,256]{3,2,1,0:T(8,128)(2,1)S(1)}, bf16[2,4,16,256]{3,2,1,0:T(8,128)(2,1)S(1)}, u32[]{:S(2)}, u32[]{:S(2)}) collective-permute-start(bf16[2,4,16,256]{3,2,1,0:T(8,128)(2,1)S(1)} %get-tuple-element.28), channel_id=1, source_target_pairs={{0,16},{16,0},{32,48},{48,32},{64,80},{80,64},{96,112},{112,96},{1... | collective-permute-start | bytes 196616 | tf_op jit(solution)/shard_map/ppermute | solution.py:434
  94.4 4.3 %collective-permute-start.9 = (bf16[2,4,16,256]{3,2,1,0:T(8,128)(2,1)S(1)}, bf16[2,4,16,256]{3,2,1,0:T(8,128)(2,1)S(1)}, u32[]{:S(2)}, u32[]{:S(2)}) collective-permute-start(bf16[2,4,16,256]{3,2,1,0:T(8,128)(2,1)S(1)} %get-tuple-element.29), channel_id=1, source_target_pairs={{0,17},{1,16},{2,19},{3,18},{4,21},{5,20},{6,23},{7,22},{8,25},{9,... | collective-permute-start | bytes 196616 | tf_op jit(solution)/shard_map/ppermute | solution.py:435
  98.6 0.0 collective-permute-done.7.refs_1_
  98.6 0.1 collective-permute-done.8.refs_2_
  98.8 3.0 %collective-permute-done.9.refs_3_ = bf16[2,4,16,256]{3,2,1,0:T(8,128)(2,1)S(1)} collective-permute-done((bf16[2,4,16,256]{3,2,1,0:T(8,128)(2,1)S(1)}, bf16[2,4,16,256]{3,2,1,0:T(8,128)(2,1)S(1)}, u32[]{:S(2)}, u32[]{:S(2)}) %collective-permute-start.9) | collective-permute-done | bytes 65568 | tf_op jit(solution)/shard_map/ppermute | solution.py:435
  101.8 1.1 %shard_map.67 = (bf16[2,4,32,128]{3,2,1,0:T(8,128)(2,1)}, f32[8,128]{1,0:T(8,128)S(1)}) custom-call(f32[2,4,16,256]{3,2,1,0:T(8,128)S(1)} %get-tuple-element.26.refs_0_, bf16[2,4,16,256]{3,2,1,0:T(8,128)(2,1)S(1)} %collective-permute-done.7.refs_1_, bf16[2,4,16,256]{3,2,1,0:T(8,128)(2,1)S(1)} %collective-permute-done.8.refs_2_, ...), custom_call_target="tpu_custom_call" | custom-call | bytes 397312 | tf_op jit(solution)/shard_map/pallas_call | solution.py:76
  102.9 0.0 all-to-all-done.2.refs_0_
  102.9 0.8 shard_map.68
  (1 shorter events, 0.0 us)
Async XLA Ops:
  0.6 0.9 copy-start.2
  3.1 35.2 %copy-start = (bf16[3,3,3,128,256]{4,3,2,1,0:T(8,128)(2,1)S(1)}, bf16[3,3,3,128,256]{4,3,2,1,0:T(8,128)(2,1)}, u32[]{:S(2)}) copy-start(bf16[3,3,3,128,256]{4,3,2,1,0:T(8,128)(2,1)} %param.5) | copy-start | bytes 5308420
  3.1 40.9 %all-to-all-start = ((bf16[16,16,1728]{2,1,0:T(8,128)(2,1)}), bf16[16,16,1728]{2,1,0:T(8,128)(2,1)S(1)}, u32[]{:S(2)}, u32[]{:S(2)}) async-start(bf16[16,16,1728]{2,1,0:T(8,128)(2,1)} %shard_map.59), calls=%async_computation | async-start | bytes 1835008 | tf_op jit(solution)/shard_map/all_to_all | solution.py:360
  15.1 12.4 %collective-permute-start = (bf16[10,32,128]{2,1,0:T(8,128)(2,1)}, bf16[10,32,128]{2,1,0:T(8,128)(2,1)S(1)}, u32[]{:S(2)}, u32[]{:S(2)}) collective-permute-start(bf16[10,32,128]{2,1,0:T(8,128)(2,1)} %shard_map.60.refs_0_), channel_id=1, source_target_pairs={{0,16},{16,0},{32,48},{48,32},{64,80},{80,64},{96,112},{112,96},{1... | collective-permute-start | bytes 245768 | tf_op jit(solution)/shard_map/ppermute | solution.py:363
  17.0 10.5 %collective-permute-start.1 = (bf16[10,32,128]{2,1,0:T(8,128)(2,1)}, bf16[10,32,128]{2,1,0:T(8,128)(2,1)S(1)}, u32[]{:S(2)}, u32[]{:S(2)}) collective-permute-start(bf16[10,32,128]{2,1,0:T(8,128)(2,1)} %shard_map.60.refs_0_), channel_id=1, source_target_pairs={{16,32},{32,16},{48,64},{64,48},{80,96},{96,80},{112,128},{128,112... | collective-permute-start | bytes 245768 | tf_op jit(solution)/shard_map/ppermute | solution.py:366
  17.7 9.9 %collective-permute-start.2 = (bf16[10,32,128]{2,1,0:T(8,128)(2,1)}, bf16[10,32,128]{2,1,0:T(8,128)(2,1)S(1)}, u32[]{:S(2)}, u32[]{:S(2)}) collective-permute-start(bf16[10,32,128]{2,1,0:T(8,128)(2,1)} %shard_map.60.refs_0_), channel_id=1, source_target_pairs={{16,48},{32,0},{48,80},{64,32},{80,112},{96,64},{112,144},{128,96}... | collective-permute-start | bytes 245768 | tf_op jit(solution)/shard_map/ppermute | solution.py:367
  27.5 0.9 copy-start.1
  28.8 12.1 %collective-permute-start.3 = (bf16[30,32,128]{2,1,0:T(8,128)(2,1)S(1)}, bf16[30,32,128]{2,1,0:T(8,128)(2,1)S(1)}, u32[]{:S(2)}, u32[]{:S(2)}) collective-permute-start(bf16[30,32,128]{2,1,0:T(8,128)(2,1)S(1)} %get-tuple-element.17.refs_0_), channel_id=1, source_target_pairs={{0,1},{1,0},{2,3},{3,2},{4,5},{5,4},{6,7},{7,6},{8,9},{9,8},{10,11... | collective-permute-start | bytes 737288 | tf_op jit(solution)/shard_map/ppermute | solution.py:385
  31.8 9.0 %collective-permute-start.4 = (bf16[15,32,128]{2,1,0:T(8,128)(2,1)S(1)}, bf16[15,32,128]{2,1,0:T(8,128)(2,1)S(1)}, u32[]{:S(2)}, u32[]{:S(2)}) collective-permute-start(bf16[15,32,128]{2,1,0:T(8,128)(2,1)S(1)} %get-tuple-element.18), channel_id=1, source_target_pairs={{1,2},{2,1},{3,4},{4,3},{5,6},{6,5},{7,8},{8,7},{9,10},{10,9},{11,... | collective-permute-start | bytes 368648 | tf_op jit(solution)/shard_map/ppermute | solution.py:386
  35.2 5.7 %collective-permute-start.5 = (bf16[15,32,128]{2,1,0:T(8,128)(2,1)S(1)}, bf16[15,32,128]{2,1,0:T(8,128)(2,1)S(1)}, u32[]{:S(2)}, u32[]{:S(2)}) collective-permute-start(bf16[15,32,128]{2,1,0:T(8,128)(2,1)S(1)} %get-tuple-element.18), channel_id=1, source_target_pairs={{1,3},{2,0},{3,5},{4,2},{5,7},{6,4},{7,9},{8,6},{9,11},{10,8},{11,... | collective-permute-start | bytes 368648 | tf_op jit(solution)/shard_map/ppermute | solution.py:387
  39.8 1.0 copy-start.3
  45.9 37.0 %copy-start.4 = (bf16[9,256,256]{2,1,0:T(8,128)(2,1)S(1)}, bf16[9,256,256]{2,1,0:T(8,128)(2,1)}, u32[]{:S(2)}) copy-start(bf16[9,256,256]{2,1,0:T(8,128)(2,1)} %copy-done.3) | copy-start | bytes 3538948
  63.1 39.8 %all-to-all-start.2 = ((bf16[16,16,128]{2,1,0:T(8,128)(2,1)}), bf16[16,16,128]{2,1,0:T(8,128)(2,1)S(1)}, u32[]{:S(2)}, u32[]{:S(2)}) async-start(bf16[16,16,128]{2,1,0:T(8,128)(2,1)} %shard_map.65.refs_3_), calls=%async_computation.2 | async-start | bytes 131072 | tf_op jit(solution)/shard_map/all_to_all | solution.py:418
  77.4 5.5 %collective-permute-start.6 = (bf16[2,10,16,128]{3,2,1,0:T(8,128)(2,1)S(1)}, bf16[2,10,16,128]{3,2,1,0:T(8,128)(2,1)S(1)}, u32[]{:S(2)}, u32[]{:S(2)}) collective-permute-start(bf16[2,10,16,128]{3,2,1,0:T(8,128)(2,1)S(1)} %slice.3), channel_id=1, source_target_pairs={{32,0},{48,16},{64,32},{80,48},{96,64},{112,80},{128,96},{144,112}... | collective-permute-start | bytes 245768 | tf_op jit(solution)/shard_map/ppermute | solution.py:421
  84.1 14.6 %collective-permute-start.7 = (bf16[2,4,16,256]{3,2,1,0:T(8,128)(2,1)S(1)}, bf16[2,4,16,256]{3,2,1,0:T(8,128)(2,1)S(1)}, u32[]{:S(2)}, u32[]{:S(2)}) collective-permute-start(bf16[2,4,16,256]{3,2,1,0:T(8,128)(2,1)S(1)} %get-tuple-element.27), channel_id=1, source_target_pairs={{0,1},{1,0},{2,3},{3,2},{4,5},{5,4},{6,7},{7,6},{8,9},{9,8},{10,11... | collective-permute-start | bytes 196616 | tf_op jit(solution)/shard_map/ppermute | solution.py:433
  91.7 7.1 %collective-permute-start.8 = (bf16[2,4,16,256]{3,2,1,0:T(8,128)(2,1)S(1)}, bf16[2,4,16,256]{3,2,1,0:T(8,128)(2,1)S(1)}, u32[]{:S(2)}, u32[]{:S(2)}) collective-permute-start(bf16[2,4,16,256]{3,2,1,0:T(8,128)(2,1)S(1)} %get-tuple-element.28), channel_id=1, source_target_pairs={{0,16},{16,0},{32,48},{48,32},{64,80},{80,64},{96,112},{112,96},{1... | collective-permute-start | bytes 196616 | tf_op jit(solution)/shard_map/ppermute | solution.py:434
  94.4 7.4 %collective-permute-start.9 = (bf16[2,4,16,256]{3,2,1,0:T(8,128)(2,1)S(1)}, bf16[2,4,16,256]{3,2,1,0:T(8,128)(2,1)S(1)}, u32[]{:S(2)}, u32[]{:S(2)}) collective-permute-start(bf16[2,4,16,256]{3,2,1,0:T(8,128)(2,1)S(1)} %get-tuple-element.29), channel_id=1, source_target_pairs={{0,17},{1,16},{2,19},{3,18},{4,21},{5,20},{6,23},{7,22},{8,25},{9,... | collective-permute-start | bytes 196616 | tf_op jit(solution)/shard_map/ppermute | solution.py:435

commit v3 on v1

--- a/solution.py
+++ b/solution.py
@@ -110,16 +110,12 @@
                 out[p, :, place * OWN : place * OWN + piece.shape[1]] = piece
 
 
-def own_filter_kernel(first, band, turned):
+def band_kernel(first, band):
     chans = first.shape[1]
     x, core = lax.axis_index("tm") % 2, lax.axis_index("height") % CORES
-
-    def source(place):
-        return own_channel(place % OWN, x, core)
-
     row = lax.broadcasted_iota(jnp.int32, (chans, 2 * OWN), 0)
     col = lax.broadcasted_iota(jnp.int32, (chans, 2 * OWN), 1)
-    pick = jnp.where(source(col) == row, 1.0, 0.0).astype(BF16)
+    pick = jnp.where(own_channel(col % OWN, x, core) == row, 1.0, 0.0).astype(BF16)
     twice = mm(first[...], pick)
     lane = lax.broadcasted_iota(jnp.int32, (128, 2 * OWN), 1)
     for ab in range(9):
@@ -128,9 +124,14 @@
             right = twice[(ab * 3 + s - 1) * 128 : (ab * 3 + s) * 128] if s > 0 else 0.0
             both = jnp.where(lane < OWN, left, right)
             band[ab, s * 128 : (s + 1) * 128] = both.astype(BF16)
+
+
+def turned_kernel(first, _, turned):
+    chans = first.shape[1]
+    x, core = lax.axis_index("tm") % 2, lax.axis_index("height") % CORES
     row = lax.broadcasted_iota(jnp.int32, (OWN, chans), 0)
     col = lax.broadcasted_iota(jnp.int32, (OWN, chans), 1)
-    pick = jnp.where(source(row) == col, 1.0, 0.0).astype(BF16)
+    pick = jnp.where(own_channel(row, x, core) == col, 1.0, 0.0).astype(BF16)
     flat = lax.dot_general(
         pick, first[...], (((1,), (1,)), ((), ())), preferred_element_type=F32
     ).astype(BF16)
@@ -145,34 +146,48 @@
                 turned[ab, slot * OWN : (slot + 1) * OWN, jp * 128 : (jp + 1) * 128] = piece
 
 
-def stack_kernel(clip, up, out):
+def stack_kernel(clip, up, here, edge):
+    at_top = lax.axis_index("height") % CORES == 0
     for f in range(2):
-        out[4 * f : 4 * f + 4] = clip[f]
+        here[4 * f : 4 * f + 4] = clip[f]
+        edge[2 * f : 2 * f + 2] = jnp.where(at_top, clip[f, :2], clip[f, 2:])
     for half in range(2):
-        out[8:10, 16 * half : 16 * half + 16] = up[0, :, :, 128 * half : 128 * half + 128]
-
-
-def pack_kernel(here, pair, odd, even, _, packed, edge, __):
+        subs = slice(16 * half, 16 * half + 16)
+        src = up[0, :, :, 128 * half : 128 * half + 128]
+        here[8:10, subs] = src
+        edge[4, subs] = jnp.where(at_top, src[0], src[1])
+
+
+def append_kernel(here, edge, _, out, __, sems):
+    copies = [
+        pltpu.make_async_copy(here, out.at[:10], sems.at[0]),
+        pltpu.make_async_copy(edge, out.at[10:], sems.at[1]),
+    ]
+    for copy in copies:
+        copy.start()
+    for copy in copies:
+        copy.wait()
+
+
+def pack_kernel(here, pair, odd, even, packed):
     first = lax.axis_index("tm") % 2 == 0
-    at_top = lax.axis_index("height") % CORES == 0
     one = jnp.where(first, here[...], pair[...])
     two = jnp.where(first, pair[...], here[...])
     past = jnp.where(first, odd[...], even[...])
-    next_up = jnp.where(first, even[8:10], odd[8:10])
-    for f in range(6):
-        src = (past, one, two)[f // 2][4 * (f % 2) : 4 * (f % 2) + 4]
-        packed[4 * f : 4 * f + 4] = src
-        edge[2 * f : 2 * f + 2] = jnp.where(at_top, src[:2], src[2:])
-    for t, src in enumerate((one[8:10], two[8:10], next_up)):
-        packed[24 + 2 * t : 26 + 2 * t] = src
-        edge[12 + t] = jnp.where(at_top, src[0], src[1])
-
-
-def preact_kernel(own, other, near, far, filters, wide, ups, pre, band, ext):
+    after = jnp.where(first, even[...], odd[...])
+    for k, src in enumerate((past, one, two)):
+        packed[8 * k : 8 * k + 8] = src[:8]
+        packed[30 + 4 * k : 34 + 4 * k] = src[10:14]
+    for t, src in enumerate((one, two, after)):
+        packed[24 + 2 * t : 26 + 2 * t] = src[8:10]
+        packed[42 + t] = src[14]
+
+
+def preact_kernel(own, other, filters, wide, ups, pre, band, ext):
     member = lax.axis_index("height") % CORES
     even = member == 0
-    above = jnp.where(even, near[...], far[...])
-    below = jnp.where(even, far[...], near[...])
+    above = jnp.where(even, own[30:45], other[30:45])
+    below = jnp.where(even, other[30:45], own[30:45])
     for f in range(6):
         base = f * HIGH
         band[pl.ds(base + 2 + 4 * member, 4)] = own[4 * f : 4 * f + 4]
@@ -271,7 +286,7 @@
             parts[x * blocks : (x + 1) * blocks, k] = both[:, :, 128 * x : 128 * x + 128]
 
 
-def sum_turn_kernel(parts, out):
+def sum_turn_kernel(parts, _, out):
     blank = jnp.zeros((16, 128), F32)
     blocks = parts.shape[0] // 2
     halves = []
@@ -281,13 +296,14 @@
             total = total + parts[x * blocks + i].astype(F32)
         halves += [total.reshape(112, 128), blank]
     flat = jnp.concatenate(halves, 0).T
-    for z in range(16):
+    for i in range(16):
+        z = (i + 8) % 16
         rows = [(tap * 64 + z * 4, x) for x in range(2) for tap in range(2)]
         block = [flat[r : r + 4, 128 * x : 128 * x + 128] for r, x in rows]
-        out[z] = jnp.concatenate(block, 0).astype(BF16)
-
-
-def finish_kernel(scale, parts, out):
+        out[i] = jnp.concatenate(block, 0).astype(BF16)
+
+
+def finish_kernel(scale, parts, out, mark):
     total = parts[0].astype(F32)
     for i in range(1, parts.shape[0]):
         total = total + parts[i].astype(F32)
@@ -296,9 +312,10 @@
         lanes = slice(8 * (k // 2), 8 * (k // 2) + 8)
         rows = [8 * x + 4 * (k % 2) for x in range(2)]
         out[k] = jnp.concatenate([total[r : r + 4, lanes] for r in rows], 1)
-
-
-def clip_kernel(grad, following, filters, _, keep, send, wide):
+    mark[...] = jnp.zeros_like(mark)
+
+
+def clip_kernel(grad, following, filters, keep, send, wide):
     lane = lax.broadcasted_iota(jnp.int32, (192, 2 * OWN), 1)
     up = one_hot(192, 192, lambda r: jnp.where(r % 16 == 15, -1, r + 1))
     down = one_hot(192, 192, lambda r: jnp.where(r % 16 == 0, -1, r - 1))
@@ -330,7 +347,7 @@
     send[...] = jnp.where(first, high, low).astype(BF16)
 
 
-def join_kernel(kept, got, out):
+def join_kernel(kept, got, _, out):
     total = (kept[...] + got[...].astype(F32)).astype(BF16).reshape(128, 256)
     low = one_hot(256, 128, lambda r: jnp.where(r % 2 == 0, (r // 32) * 16 + (r % 32) // 2, -1))
     high = one_hot(256, 128, lambda r: jnp.where(r % 2 == 1, (r // 32) * 16 + (r % 32) // 2, -1))
@@ -350,12 +367,15 @@
     siblings = [(i, i ^ 1) for i in range(heights)]
     blocks = [(t, t ^ 1) for t in range(tms)]
 
-    (here,) = call(stack_kernel, [shaped((10, 32, 128), BF16)], [clip, upstream], fetch=(0, 1), limit=60)
-    pair = lax.ppermute(here, "tm", blocks)
-    odd_pairs = inside([(t, t + 1 if t % 2 else t - 1) for t in range(tms)], tms)
-    even_pairs = inside([(t, t + 2 if t % 2 else t - 2) for t in range(tms)], tms)
-    odd = lax.ppermute(here, "tm", odd_pairs)
-    even = lax.ppermute(here, "tm", even_pairs)
+    here, edge = call(
+        stack_kernel,
+        [shaped((10, 32, 128), BF16), shaped((5, 32, 128), BF16)],
+        [clip, upstream],
+        fetch=(0, 1),
+        limit=60,
+    )
+    near_pairs = inside([(i, i + 1 if i % 2 else i - 1) for i in range(heights)], heights)
+    edge = lax.ppermute(edge, "height", near_pairs)
 
     second = jnp.swapaxes(second_filter, 3, 4).reshape(27, chans // heights, chans)
     (pieces,) = call(
@@ -365,28 +385,35 @@
         fetch=(0,),
         flops=2 * 27 * 16 * 256 * 128,
     )
-    band, turned = call(
-        own_filter_kernel,
-        [shaped((9, 512, 2 * OWN), BF16), shaped((9, 4 * OWN, 2 * cin), BF16)],
-        [first_filter.reshape(27 * cin, chans)],
+    here, pieces = call(
+        append_kernel,
+        [shaped((15, 32, 128), BF16), shaped(pieces.shape, BF16)],
+        [here, edge, pieces],
+        scratch=[pltpu.SemaphoreType.DMA((2,))],
+        idle=(0, 1, 2),
+        alias={2: 1},
+    )
+    second = lax.all_to_all(pieces, "height", 0, 0).reshape(chans, 27 * OWN)
+
+    pair = lax.ppermute(here, "tm", blocks)
+    odd_pairs = inside([(t, t + 1 if t % 2 else t - 1) for t in range(tms)], tms)
+    even_pairs = inside([(t, t + 2 if t % 2 else t - 2) for t in range(tms)], tms)
+    odd = lax.ppermute(here, "tm", odd_pairs)
+    even = lax.ppermute(here, "tm", even_pairs)
+
+    first = first_filter.reshape(27 * cin, chans)
+    (band,) = call(
+        band_kernel,
+        [shaped((9, 512, 2 * OWN), BF16)],
+        [first],
         fetch=(0,),
-        flops=4 * 27 * 128 * 256 * 128,
-    )
-
-    packed, edge, pieces = call(
-        pack_kernel,
-        [shaped((30, 32, 128), BF16), shaped((15, 32, 128), BF16), shaped(pieces.shape, BF16)],
-        [here, pair, odd, even, pieces],
-        fetch=(1, 2, 3),
-        idle=(4,),
-        alias={4: 2},
-    )
-    second = lax.all_to_all(pieces, "height", 0, 0).reshape(chans, 27 * OWN)
-    near_pairs = inside([(i, i + 1 if i % 2 else i - 1) for i in range(heights)], heights)
-    far_pairs = inside([(i, i + 2 if i % 2 else i - 2) for i in range(heights)], heights)
+        flops=2 * 27 * 128 * 256 * 128,
+    )
+
+    (packed,) = call(
+        pack_kernel, [shaped((45, 32, 128), BF16)], [here, pair, odd, even], fetch=(1, 2, 3)
+    )
     other = lax.ppermute(packed, "height", siblings)
-    near = lax.ppermute(edge, "height", near_pairs)
-    far = lax.ppermute(edge, "height", far_pairs)
 
     units, up_units = 6 * HIGH, 3 * HALF_HIGH
     wide, ups, pre = call(
@@ -396,9 +423,9 @@
             shaped((2, up_units, 16, 256), BF16),
             shaped((2, 2, 2, HALF, 16, 2 * OWN), F32),
         ],
-        [packed, other, near, far, band],
+        [packed, other, band],
         scratch=[pltpu.VMEM((units, 32, 128), BF16), pltpu.VMEM((up_units, 16, 256), BF16)],
-        fetch=(1, 2, 3),
+        fetch=(0, 1),
         flops=2 * 640 * 9 * 512 * 128,
     )
     grad_pre, parts = call(
@@ -415,29 +442,34 @@
         for core in range(CORES)
     ]
     parts = lax.all_to_all(parts, ("tm", "height"), 0, 0, axis_index_groups=planes)
-    (sums,) = call(sum_turn_kernel, [shaped((lines, 16, 128), BF16)], [parts], fetch=(0,))
-    columns = [[2 * z + x for z in range(lines)] for x in range(2)]
-    summed = lax.all_to_all(sums, "tm", 0, 0, axis_index_groups=columns)
-    count = frames * tms * rows * heights * width
-    (grad_filter,) = call(
-        functools.partial(finish_kernel, 1.0 / float(count) ** 0.5),
-        [shaped((27, cin // tms, chans // heights), F32)],
-        [summed],
-        fetch=(0,),
-    )
-    grad_filter = grad_filter.reshape(3, 3, 3, cin // tms, chans // heights)
-
     back = inside([(t, t - 2) for t in range(tms)], tms)
     following = lax.ppermute(grad_pre[:2], "tm", back)
+    (turned,) = call(
+        turned_kernel,
+        [shaped((9, 4 * OWN, 2 * cin), BF16)],
+        [first, grad_pre],
+        fetch=(0,),
+        idle=(1,),
+        flops=2 * 27 * 128 * 256 * 64,
+    )
     keep, send = call(
         clip_kernel,
         [shaped((FRAMES, rows, 16, 2 * cin), F32)] * 2,
-        [grad_pre, following, turned, sums],
+        [grad_pre, following, turned],
         scratch=[pltpu.VMEM(((FRAMES + 2) * SPAN, 16, 4 * OWN), BF16)],
         fetch=(1,),
-        idle=(3,),
         flops=2 * 512 * 9 * 256 * 256,
     )
+
+    (sums,) = call(
+        sum_turn_kernel,
+        [shaped((lines, 16, 128), BF16)],
+        [parts, send],
+        fetch=(0,),
+        idle=(1,),
+    )
+    columns = [[2 * ((i + 8) % lines) + x for i in range(lines)] for x in range(2)]
+    summed = lax.all_to_all(sums, "tm", 0, 0, axis_index_groups=columns)
     got = lax.ppermute(send, "height", siblings)
     keep, send = call(
         halve_kernel,
@@ -446,7 +478,21 @@
         fetch=(1,),
     )
     got = lax.ppermute(send, "tm", blocks)
-    (grad_clip,) = call(join_kernel, [shaped(clip.shape, BF16)], [keep, got], fetch=(1,))
+    count = frames * tms * rows * heights * width
+    grad_filter, mark = call(
+        functools.partial(finish_kernel, 1.0 / float(count) ** 0.5),
+        [shaped((27, cin // tms, chans // heights), F32), shaped((8, 128), F32)],
+        [summed],
+        fetch=(0,),
+    )
+    (grad_clip,) = call(
+        join_kernel,
+        [shaped(clip.shape, BF16)],
+        [keep, got, mark],
+        fetch=(1,),
+        idle=(2,),
+    )
+    grad_filter = grad_filter.reshape(3, 3, 3, cin // tms, chans // heights)
     return (grad_clip, grad_filter)
 
 

time: 97.6 us -> 89.6 us (0.918)
  waiting for transfers between devices: 23.3 us -> 10.2 us
  starting transfers between devices: 55.9 us -> 58.5 us
  local copies, waits for them, and re-layouts: 1.99 us -> 3.25 us
    all_to_all x1, waiting for transfers between devices: 9.89 us -> 0.01 us  [body(): lax.all_to_all(parts, ('tm', 'height'), 0, 0, axis_index_groups=planes)]
    all_to_all x1, waiting for transfers between devices: 8.88 us -> 0.01 us  [body(): summed = lax.all_to_all(sums, 'tm', 0, 0, axis_index_groups=columns)]
    ppermute x1, waiting for transfers between devices: 0.01 us -> 6.02 us  [body(): pair = lax.ppermute(here, 'tm', blocks)]
    all_to_all x1, starting transfers between devices: 12.1 us -> 17.1 us  [body(): summed = lax.all_to_all(sums, 'tm', 0, 0, axis_index_groups=columns)]
    ppermute x2 -> x1, waiting for transfers between devices: 4.55 us -> 0.01 us  [body(): edge = lax.ppermute(edge, 'height', near_pairs)]
    all_to_all x1, starting transfers between devices: 10.3 us -> 6.51 us  [body(): second = lax.all_to_all(pieces, 'height', 0, 0).reshape(chans, 27 * OWN)]
    ppermute x1, waiting for transfers between devices: 0.01 us -> 3.13 us  [body(): following = lax.ppermute(grad_pre[:2], 'tm', back)]
    ppermute x1, starting transfers between devices: 2.66 us -> 5.06 us  [body(): got = lax.ppermute(send, 'tm', blocks)]
  transfers between devices with their start and end apart: 12 -> 11, of which waited for: 4 -> 4; matrix products, arithmetic and copies ran while one was open for 0% -> 0% of each run, Pallas kernels for 8% -> 11%
where the time goes in v3:
time: 89.6 us; the launch traced here: 88.1 us
  starting transfers between devices  58.5 us (65%)
  Pallas kernels  15.2 us (17%)
  waiting for transfers between devices  10.2 us (11%)
  local copies, waits for them, and re-layouts  3.25 us (4%)
    all_to_all x1, starting transfers between devices, body(): summed = lax.all_to_all(sums, 'tm', 0, 0, axis_index_groups=columns)  17.1 us
    pallas_call x13, Pallas kernels, call(): pl.pallas_call(run, out_shape=tuple(out), in_specs=[far if i in fetch or...  15.2 us
    all_to_all x1, starting transfers between devices, body(): lax.all_to_all(parts, ('tm', 'height'), 0, 0, axis_index_groups=planes)  8.12 us
    ppermute x1, starting transfers between devices, body(): pair = lax.ppermute(here, 'tm', blocks)  7.92 us
    all_to_all x1, starting transfers between devices, body(): second = lax.all_to_all(pieces, 'height', 0, 0).reshape(chans, 27 * OWN)  6.51 us
    ppermute x1, waiting for transfers between devices, body(): pair = lax.ppermute(here, 'tm', blocks)  6.02 us
    ppermute x1, starting transfers between devices, body(): got = lax.ppermute(send, 'tm', blocks)  5.06 us
    ppermute x1, starting transfers between devices, body(): edge = lax.ppermute(edge, 'height', near_pairs)  4.59 us
  transfers between devices with their start and end apart: 11, of which 4 were waited for; matrix products, arithmetic and copies ran while one was open for 0% of the time, Pallas kernels for 11%

profile of v3, /device:TPU:1, one launch (start us, length us, event | category | flops | bytes accessed | tf_op | source)
XLA Modules:
  0.0 88.1 jit_solution(1216841198543223755)
XLA Ops:
  0.6 1.5 %shard_map.59 = (bf16[10,32,128]{2,1,0:T(8,128)(2,1)}, bf16[5,32,128]{2,1,0:T(8,128)(2,1)}) custom-call(bf16[2,4,32,128]{3,2,1,0:T(8,128)(2,1)} %refs_0_.1, bf16[1,2,16,256]{3,2,1,0:T(8,128)(2,1)} %refs_1_.1), custom_call_target="tpu_custom_call" | custom-call | bytes 204800 | tf_op jit(solution)/shard_map/pallas_call | solution.py:76
  2.2 4.6 %collective-permute-start = (bf16[5,32,128]{2,1,0:T(8,128)(2,1)}, bf16[5,32,128]{2,1,0:T(8,128)(2,1)S(1)}, u32[]{:S(2)}, u32[]{:S(2)}) collective-permute-start(bf16[5,32,128]{2,1,0:T(8,128)(2,1)} %get-tuple-element.18), channel_id=1, source_target_pairs={{1,2},{2,1},{3,4},{4,3},{5,6},{6,5},{7,8},{8,7},{9,10},{10,9},{11,... | collective-permute-start | bytes 122888 | tf_op jit(solution)/shard_map/ppermute | solution.py:378
  6.8 0.0 copy-start.3
  6.8 0.9 %copy-done.3 = bf16[3,3,3,256,16]{3,4,2,1,0:T(8,128)(2,1)S(1)} copy-done((bf16[3,3,3,256,16]{3,4,2,1,0:T(8,128)(2,1)S(1)}, bf16[3,3,3,256,16]{3,4,2,1,0:T(8,128)(2,1)}, u32[]{:S(2)}) %copy-start.3) | copy-done | bytes 221208
  7.7 0.0 copy-start.4
  7.7 1.6 %shard_map.60.refs_2_ = bf16[16,16,1728]{2,1,0:T(8,128)(2,1)} custom-call(bf16[27,16,256]{2,1,0:T(8,128)(2,1)S(1)} %bitcast.9), custom_call_target="tpu_custom_call" | custom-call | flops 28311552 | bytes 1105920 | tf_op jit(solution)/shard_map/pallas_call | solution.py:76
  9.3 0.0 collective-permute-done.refs_1_
  9.3 0.0 copy-done.4
  9.3 0.2 shard_map.61
  9.5 0.0 copy-start
  9.5 6.5 %all-to-all-start = ((bf16[16,16,1728]{2,1,0:T(8,128)(2,1)}), bf16[16,16,1728]{2,1,0:T(8,128)(2,1)S(1)}, u32[]{:S(2)}, u32[]{:S(2)}) async-start(bf16[16,16,1728]{2,1,0:T(8,128)(2,1)} %get-tuple-element.19), calls=%async_computation | async-start | bytes 1835008 | tf_op jit(solution)/shard_map/all_to_all | solution.py:396
  16.0 1.3 %collective-permute-start.3 = (bf16[15,32,128]{2,1,0:T(8,128)(2,1)S(1)}, bf16[15,32,128]{2,1,0:T(8,128)(2,1)S(1)}, u32[]{:S(2)}, u32[]{:S(2)}) collective-permute-start(bf16[15,32,128]{2,1,0:T(8,128)(2,1)S(1)} %get-tuple-element.20.refs_0_), channel_id=1, source_target_pairs={{16,48},{32,0},{48,80},{64,32},{80,112},{96,64},{112,144},{128,96}... | collective-permute-start | bytes 368648 | tf_op jit(solution)/shard_map/ppermute | solution.py:402
  17.3 0.7 collective-permute-start.2
  18.0 7.9 %collective-permute-start.1 = (bf16[15,32,128]{2,1,0:T(8,128)(2,1)S(1)}, bf16[15,32,128]{2,1,0:T(8,128)(2,1)S(1)}, u32[]{:S(2)}, u32[]{:S(2)}) collective-permute-start(bf16[15,32,128]{2,1,0:T(8,128)(2,1)S(1)} %get-tuple-element.20.refs_0_), channel_id=1, source_target_pairs={{0,16},{16,0},{32,48},{48,32},{64,80},{80,64},{96,112},{112,96},{1... | collective-permute-start | bytes 368648 | tf_op jit(solution)/shard_map/ppermute | solution.py:398
  25.9 0.0 collective-permute-done.3.refs_3_
  25.9 0.0 collective-permute-done.2.refs_2_
  25.9 6.0 %collective-permute-done.1.refs_1_ = bf16[15,32,128]{2,1,0:T(8,128)(2,1)S(1)} collective-permute-done((bf16[15,32,128]{2,1,0:T(8,128)(2,1)S(1)}, bf16[15,32,128]{2,1,0:T(8,128)(2,1)S(1)}, u32[]{:S(2)}, u32[]{:S(2)}) %collective-permute-start.1) | collective-permute-done | bytes 122912 | tf_op jit(solution)/shard_map/ppermute | solution.py:398
  31.9 0.6 shard_map.62.refs_0_
  32.5 2.5 %collective-permute-start.4 = (bf16[45,32,128]{2,1,0:T(8,128)(2,1)S(1)}, bf16[45,32,128]{2,1,0:T(8,128)(2,1)S(1)}, u32[]{:S(2)}, u32[]{:S(2)}) collective-permute-start(bf16[45,32,128]{2,1,0:T(8,128)(2,1)S(1)} %shard_map.62.refs_0_), channel_id=1, source_target_pairs={{0,1},{1,0},{2,3},{3,2},{4,5},{5,4},{6,7},{7,6},{8,9},{9,8},{10,11... | collective-permute-start | bytes 1105928 | tf_op jit(solution)/shard_map/ppermute | solution.py:416
  35.0 0.0 copy-done
  35.0 1.0 %shard_map.63.refs_2_ = bf16[9,512,128]{2,1,0:T(8,128)(2,1)S(1)} custom-call(bf16[3456,256]{1,0:T(8,128)(2,1)S(1)} %bitcast.6), custom_call_target="tpu_custom_call" | custom-call | flops 226492416 | bytes 2949120 | tf_op jit(solution)/shard_map/pallas_call | solution.py:76
  36.0 0.3 collective-permute-done.4.refs_1_
  36.3 2.8 %shard_map.64 = (bf16[72,16,512]{2,1,0:T(8,128)(2,1)S(1)}, bf16[2,18,16,256]{3,2,1,0:T(8,128)(2,1)S(1)}, f32[2,2,2,5,16,128]{5,4,3,2,1,0:T(8,128)S(1)}) custom-call(bf16[45,32,128]{2,1,0:T(8,128)(2,1)S(1)} %shard_map.62.refs_0_, bf16[45,32,128]{2,1,0:T(8,128)(2,1)S(1)} %collective-permute-done.4.refs_1_, bf16[9,512,128]{2,1,0:T(8,128)(2,1)S(1)} %shard_map.63.refs_2_), custom_call_target="tpu_custom_call" | custom-call | flops 754974720 | bytes 3719168 | tf_op jit(solution)/shard_map/pallas_call | solution.py:76
  39.1 0.0 copy-start.1
  39.1 1.0 %copy-done.1 = bf16[72,16,512]{2,1,0:T(8,128)(2,1)} copy-done((bf16[72,16,512]{2,1,0:T(8,128)(2,1)}, bf16[72,16,512]{2,1,0:T(8,128)(2,1)S(1)}, u32[]{:S(2)}) %copy-start.1) | copy-done | bytes 1179672
  40.1 0.0 all-to-all-done
  40.1 0.0 copy-start.2
  40.1 1.3 %copy-done.2 = bf16[72,16,512]{2,1,0:T(8,128)(2,1)S(1)} copy-done((bf16[72,16,512]{2,1,0:T(8,128)(2,1)S(1)}, bf16[72,16,512]{2,1,0:T(8,128)(2,1)}, u32[]{:S(2)}) %copy-start.2) | copy-done | bytes 1179672
  41.4 2.6 %shard_map.65 = (bf16[4,10,16,128]{3,2,1,0:T(8,128)(2,1)S(1)}, bf16[16,7,16,128]{3,2,1,0:T(8,128)(2,1)}) custom-call(bf16[256,1728]{1,0:T(8,128)(2,1)S(1)} %bitcast.8, bf16[2,18,16,256]{3,2,1,0:T(8,128)(2,1)S(1)} %get-tuple-element.21.refs_1_, f32[2,2,2,5,16,128]{5,4,3,2,1,0:T(8,128)S(1)} %get-tuple-element.22.refs_2_, bf16[72,16,512]{2,1,0:T(8,128)(2,1)S(1)} %copy-done.2), custom_call_target="tpu_custom_call" | custom-call | flops 603979776 | bytes 3309568 | tf_op jit(solution)/shard_map/pallas_call | solution.py:76
  44.0 8.1 %all-to-all-start.1 = ((bf16[16,7,16,128]{3,2,1,0:T(8,128)(2,1)}), bf16[16,7,16,128]{3,2,1,0:T(8,128)(2,1)S(1)}, u32[]{:S(2)}, u32[]{:S(2)}) async-start(bf16[16,7,16,128]{3,2,1,0:T(8,128)(2,1)} %get-tuple-element.29), calls=%async_computation.1 | async-start | bytes 917504 | tf_op jit(solution)/shard_map/all_to_all | solution.py:444
  52.2 1.3 %collective-permute-start.5 = (bf16[2,10,16,128]{3,2,1,0:T(8,128)(2,1)S(1)}, bf16[2,10,16,128]{3,2,1,0:T(8,128)(2,1)S(1)}, u32[]{:S(2)}, u32[]{:S(2)}) collective-permute-start(bf16[2,10,16,128]{3,2,1,0:T(8,128)(2,1)S(1)} %slice.3), channel_id=1, source_target_pairs={{32,0},{48,16},{64,32},{80,48},{96,64},{112,80},{128,96},{144,112}... | collective-permute-start | bytes 245768 | tf_op jit(solution)/shard_map/ppermute | solution.py:446
  53.5 1.0 %shard_map.66.refs_2_ = bf16[9,256,256]{2,1,0:T(8,128)(2,1)S(1)} custom-call(bf16[3456,256]{1,0:T(8,128)(2,1)S(1)} %bitcast.7, bf16[4,10,16,128]{3,2,1,0:T(8,128)(2,1)S(1)} %get-tuple-element.24.refs_1_.refs_0_), custom_call_target="tpu_custom_call" | custom-call | flops 113246208 | bytes 3112960 | tf_op jit(solution)/shard_map/pallas_call | solution.py:76
  54.5 3.1 %collective-permute-done.5.refs_1_ = bf16[2,10,16,128]{3,2,1,0:T(8,128)(2,1)S(1)} collective-permute-done((bf16[2,10,16,128]{3,2,1,0:T(8,128)(2,1)S(1)}, bf16[2,10,16,128]{3,2,1,0:T(8,128)(2,1)S(1)}, u32[]{:S(2)}, u32[]{:S(2)}) %collective-permute-start.5) | collective-permute-done | bytes 81952 | tf_op jit(solution)/shard_map/ppermute | solution.py:446
  57.6 1.1 %shard_map.67 = (f32[4,4,16,256]{3,2,1,0:T(8,128)S(1)}, f32[4,4,16,256]{3,2,1,0:T(8,128)S(1)}) custom-call(bf16[4,10,16,128]{3,2,1,0:T(8,128)(2,1)S(1)} %get-tuple-element.24.refs_1_.refs_0_, bf16[2,10,16,128]{3,2,1,0:T(8,128)(2,1)S(1)} %collective-permute-done.5.refs_1_, bf16[9,256,256]{2,1,0:T(8,128)(2,1)S(1)} %shard_map.66.refs_2_), custom_call_target="tpu_custom_call" | custom-call | flops 603979776 | bytes 1949696 | tf_op jit(solution)/shard_map/pallas_call | solution.py:76
  58.8 3.4 %collective-permute-start.6 = (f32[4,4,16,256]{3,2,1,0:T(8,128)S(1)}, f32[4,4,16,256]{3,2,1,0:T(8,128)S(1)}, u32[]{:S(2)}, u32[]{:S(2)}) collective-permute-start(f32[4,4,16,256]{3,2,1,0:T(8,128)S(1)} %get-tuple-element.26.refs_1_), channel_id=1, source_target_pairs={{0,1},{1,0},{2,3},{3,2},{4,5},{5,4},{6,7},{7,6},{8,9},{9,8},{10,11... | collective-permute-start | bytes 786440 | tf_op jit(solution)/shard_map/ppermute | solution.py:473
  62.2 0.0 all-to-all-done.1.refs_0_
  62.2 1.0 %shard_map.69 = bf16[16,16,128]{2,1,0:T(8,128)(2,1)} custom-call(bf16[16,7,16,128]{3,2,1,0:T(8,128)(2,1)S(1)} %all-to-all-done.1.refs_0_, f32[4,4,16,256]{3,2,1,0:T(8,128)S(1)} %get-tuple-element.26.refs_1_), custom_call_target="tpu_custom_call" | custom-call | bytes 786432 | tf_op jit(solution)/shard_map/pallas_call | solution.py:76
  63.3 17.1 %all-to-all-start.2 = ((bf16[16,16,128]{2,1,0:T(8,128)(2,1)}), bf16[16,16,128]{2,1,0:T(8,128)(2,1)S(1)}, u32[]{:S(2)}, u32[]{:S(2)}) async-start(bf16[16,16,128]{2,1,0:T(8,128)(2,1)} %shard_map.69), calls=%async_computation.2 | async-start | bytes 131072 | tf_op jit(solution)/shard_map/all_to_all | solution.py:472
  80.4 0.0 collective-permute-done.6.refs_1_
  80.4 0.1 shard_map.68
  80.5 5.1 %collective-permute-start.7 = (bf16[2,4,16,256]{3,2,1,0:T(8,128)(2,1)S(1)}, bf16[2,4,16,256]{3,2,1,0:T(8,128)(2,1)S(1)}, u32[]{:S(2)}, u32[]{:S(2)}) collective-permute-start(bf16[2,4,16,256]{3,2,1,0:T(8,128)(2,1)S(1)} %get-tuple-element.28), channel_id=1, source_target_pairs={{0,16},{16,0},{32,48},{48,32},{64,80},{80,64},{96,112},{112,96},{1... | collective-permute-start | bytes 196616 | tf_op jit(solution)/shard_map/ppermute | solution.py:480
  85.6 0.0 all-to-all-done.2.refs_0_
  85.6 0.8 shard_map.70
  86.4 0.8 collective-permute-done.7.refs_1_
  87.2 0.9 %shard_map.71 = bf16[2,4,32,128]{3,2,1,0:T(8,128)(2,1)} custom-call(f32[2,4,16,256]{3,2,1,0:T(8,128)S(1)} %get-tuple-element.27.refs_0_, bf16[2,4,16,256]{3,2,1,0:T(8,128)(2,1)S(1)} %collective-permute-done.7.refs_1_, f32[8,128]{1,0:T(8,128)S(1)} %get-tuple-element.30.refs_2_), custom_call_target="tpu_custom_call" | custom-call | bytes 266240 | tf_op jit(solution)/shard_map/pallas_call | solution.py:76
  (1 shorter events, 0.0 us)
Async XLA Ops:
  2.2 7.1 %collective-permute-start = (bf16[5,32,128]{2,1,0:T(8,128)(2,1)}, bf16[5,32,128]{2,1,0:T(8,128)(2,1)S(1)}, u32[]{:S(2)}, u32[]{:S(2)}) collective-permute-start(bf16[5,32,128]{2,1,0:T(8,128)(2,1)} %get-tuple-element.18), channel_id=1, source_target_pairs={{1,2},{2,1},{3,4},{4,3},{5,6},{6,5},{7,8},{8,7},{9,10},{10,9},{11,... | collective-permute-start | bytes 122888 | tf_op jit(solution)/shard_map/ppermute | solution.py:378
  6.8 0.9 %copy-start.3 = (bf16[3,3,3,256,16]{3,4,2,1,0:T(8,128)(2,1)S(1)}, bf16[3,3,3,256,16]{3,4,2,1,0:T(8,128)(2,1)}, u32[]{:S(2)}) copy-start(bf16[3,3,3,256,16]{3,4,2,1,0:T(8,128)(2,1)} %param.6) | copy-start | bytes 663556
  7.7 1.6 %copy-start.4 = (bf16[10,32,128]{2,1,0:T(8,128)(2,1)S(1)}, bf16[10,32,128]{2,1,0:T(8,128)(2,1)}, u32[]{:S(2)}) copy-start(bf16[10,32,128]{2,1,0:T(8,128)(2,1)} %get-tuple-element.17.refs_0_) | copy-start | bytes 245764
  9.5 25.5 %copy-start = (bf16[3,3,3,128,256]{4,3,2,1,0:T(8,128)(2,1)S(1)}, bf16[3,3,3,128,256]{4,3,2,1,0:T(8,128)(2,1)}, u32[]{:S(2)}) copy-start(bf16[3,3,3,128,256]{4,3,2,1,0:T(8,128)(2,1)} %param.5) | copy-start | bytes 5308420
  9.5 30.7 %all-to-all-start = ((bf16[16,16,1728]{2,1,0:T(8,128)(2,1)}), bf16[16,16,1728]{2,1,0:T(8,128)(2,1)S(1)}, u32[]{:S(2)}, u32[]{:S(2)}) async-start(bf16[16,16,1728]{2,1,0:T(8,128)(2,1)} %get-tuple-element.19), calls=%async_computation | async-start | bytes 1835008 | tf_op jit(solution)/shard_map/all_to_all | solution.py:396
  16.0 9.9 %collective-permute-start.3 = (bf16[15,32,128]{2,1,0:T(8,128)(2,1)S(1)}, bf16[15,32,128]{2,1,0:T(8,128)(2,1)S(1)}, u32[]{:S(2)}, u32[]{:S(2)}) collective-permute-start(bf16[15,32,128]{2,1,0:T(8,128)(2,1)S(1)} %get-tuple-element.20.refs_0_), channel_id=1, source_target_pairs={{16,48},{32,0},{48,80},{64,32},{80,112},{96,64},{112,144},{128,96}... | collective-permute-start | bytes 368648 | tf_op jit(solution)/shard_map/ppermute | solution.py:402
  17.3 8.6 %collective-permute-start.2 = (bf16[15,32,128]{2,1,0:T(8,128)(2,1)S(1)}, bf16[15,32,128]{2,1,0:T(8,128)(2,1)S(1)}, u32[]{:S(2)}, u32[]{:S(2)}) collective-permute-start(bf16[15,32,128]{2,1,0:T(8,128)(2,1)S(1)} %get-tuple-element.20.refs_0_), channel_id=1, source_target_pairs={{16,32},{32,16},{48,64},{64,48},{80,96},{96,80},{112,128},{128,112... | collective-permute-start | bytes 368648 | tf_op jit(solution)/shard_map/ppermute | solution.py:401
  18.0 14.0 %collective-permute-start.1 = (bf16[15,32,128]{2,1,0:T(8,128)(2,1)S(1)}, bf16[15,32,128]{2,1,0:T(8,128)(2,1)S(1)}, u32[]{:S(2)}, u32[]{:S(2)}) collective-permute-start(bf16[15,32,128]{2,1,0:T(8,128)(2,1)S(1)} %get-tuple-element.20.refs_0_), channel_id=1, source_target_pairs={{0,16},{16,0},{32,48},{48,32},{64,80},{80,64},{96,112},{112,96},{1... | collective-permute-start | bytes 368648 | tf_op jit(solution)/shard_map/ppermute | solution.py:398
  32.5 3.8 %collective-permute-start.4 = (bf16[45,32,128]{2,1,0:T(8,128)(2,1)S(1)}, bf16[45,32,128]{2,1,0:T(8,128)(2,1)S(1)}, u32[]{:S(2)}, u32[]{:S(2)}) collective-permute-start(bf16[45,32,128]{2,1,0:T(8,128)(2,1)S(1)} %shard_map.62.refs_0_), channel_id=1, source_target_pairs={{0,1},{1,0},{2,3},{3,2},{4,5},{5,4},{6,7},{7,6},{8,9},{9,8},{10,11... | collective-permute-start | bytes 1105928 | tf_op jit(solution)/shard_map/ppermute | solution.py:416
  39.1 1.0 %copy-start.1 = (bf16[72,16,512]{2,1,0:T(8,128)(2,1)}, bf16[72,16,512]{2,1,0:T(8,128)(2,1)S(1)}, u32[]{:S(2)}) copy-start(bf16[72,16,512]{2,1,0:T(8,128)(2,1)S(1)} %get-tuple-element.23.refs_3_) | copy-start | bytes 3538948
  40.1 1.3 %copy-start.2 = (bf16[72,16,512]{2,1,0:T(8,128)(2,1)S(1)}, bf16[72,16,512]{2,1,0:T(8,128)(2,1)}, u32[]{:S(2)}) copy-start(bf16[72,16,512]{2,1,0:T(8,128)(2,1)} %copy-done.1) | copy-start | bytes 3538948
  44.0 18.2 %all-to-all-start.1 = ((bf16[16,7,16,128]{3,2,1,0:T(8,128)(2,1)}), bf16[16,7,16,128]{3,2,1,0:T(8,128)(2,1)S(1)}, u32[]{:S(2)}, u32[]{:S(2)}) async-start(bf16[16,7,16,128]{3,2,1,0:T(8,128)(2,1)} %get-tuple-element.29), calls=%async_computation.1 | async-start | bytes 917504 | tf_op jit(solution)/shard_map/all_to_all | solution.py:444
  52.2 5.5 %collective-permute-start.5 = (bf16[2,10,16,128]{3,2,1,0:T(8,128)(2,1)S(1)}, bf16[2,10,16,128]{3,2,1,0:T(8,128)(2,1)S(1)}, u32[]{:S(2)}, u32[]{:S(2)}) collective-permute-start(bf16[2,10,16,128]{3,2,1,0:T(8,128)(2,1)S(1)} %slice.3), channel_id=1, source_target_pairs={{32,0},{48,16},{64,32},{80,48},{96,64},{112,80},{128,96},{144,112}... | collective-permute-start | bytes 245768 | tf_op jit(solution)/shard_map/ppermute | solution.py:446
  58.8 21.6 %collective-permute-start.6 = (f32[4,4,16,256]{3,2,1,0:T(8,128)S(1)}, f32[4,4,16,256]{3,2,1,0:T(8,128)S(1)}, u32[]{:S(2)}, u32[]{:S(2)}) collective-permute-start(f32[4,4,16,256]{3,2,1,0:T(8,128)S(1)} %get-tuple-element.26.refs_1_), channel_id=1, source_target_pairs={{0,1},{1,0},{2,3},{3,2},{4,5},{5,4},{6,7},{7,6},{8,9},{9,8},{10,11... | collective-permute-start | bytes 786440 | tf_op jit(solution)/shard_map/ppermute | solution.py:473
  63.3 22.3 %all-to-all-start.2 = ((bf16[16,16,128]{2,1,0:T(8,128)(2,1)}), bf16[16,16,128]{2,1,0:T(8,128)(2,1)S(1)}, u32[]{:S(2)}, u32[]{:S(2)}) async-start(bf16[16,16,128]{2,1,0:T(8,128)(2,1)} %shard_map.69), calls=%async_computation.2 | async-start | bytes 131072 | tf_op jit(solution)/shard_map/all_to_all | solution.py:472
  80.5 6.7 %collective-permute-start.7 = (bf16[2,4,16,256]{3,2,1,0:T(8,128)(2,1)S(1)}, bf16[2,4,16,256]{3,2,1,0:T(8,128)(2,1)S(1)}, u32[]{:S(2)}, u32[]{:S(2)}) collective-permute-start(bf16[2,4,16,256]{3,2,1,0:T(8,128)(2,1)S(1)} %get-tuple-element.28), channel_id=1, source_target_pairs={{0,16},{16,0},{32,48},{48,32},{64,80},{80,64},{96,112},{112,96},{1... | collective-permute-start | bytes 196616 | tf_op jit(solution)/shard_map/ppermute | solution.py:480

commit v4 on v3

--- a/solution.py
+++ b/solution.py
@@ -169,18 +169,27 @@
         copy.wait()
 
 
-def pack_kernel(here, pair, odd, even, packed):
+def choose_kernel(here, pair, _, forward, backward, __):
+    first = lax.axis_index("tm") % 2 == 0
+    forward[:8] = jnp.where(first, pair[:8], here[:8])
+    forward[8:12] = jnp.where(first, pair[10:14], here[10:14])
+    backward[:2] = jnp.where(first, here[8:10], pair[8:10])
+    backward[2] = jnp.where(first, here[14], pair[14])
+
+
+def pack_kernel(here, pair, before, after, packed):
     first = lax.axis_index("tm") % 2 == 0
     one = jnp.where(first, here[...], pair[...])
     two = jnp.where(first, pair[...], here[...])
-    past = jnp.where(first, odd[...], even[...])
-    after = jnp.where(first, even[...], odd[...])
-    for k, src in enumerate((past, one, two)):
+    packed[:8] = before[:8]
+    packed[30:34] = before[8:12]
+    for k, src in ((1, one), (2, two)):
         packed[8 * k : 8 * k + 8] = src[:8]
         packed[30 + 4 * k : 34 + 4 * k] = src[10:14]
-    for t, src in enumerate((one, two, after)):
-        packed[24 + 2 * t : 26 + 2 * t] = src[8:10]
-        packed[42 + t] = src[14]
+    for t, src in enumerate((one[8:10], two[8:10], after[:2])):
+        packed[24 + 2 * t : 26 + 2 * t] = src
+    for t, src in enumerate((one[14], two[14], after[2])):
+        packed[42 + t] = src
 
 
 def preact_kernel(own, other, filters, wide, ups, pre, band, ext):
@@ -286,6 +295,11 @@
             parts[x * blocks : (x + 1) * blocks, k] = both[:, :, 128 * x : 128 * x + 128]
 
 
+def middle_kernel(own, other, filters, second, grad, parts, wide, ups, pre, band, ext):
+    preact_kernel(own, other, filters, wide, ups, pre, band, ext)
+    gradient_kernel(second, ups, pre, wide, grad, parts)
+
+
 def sum_turn_kernel(parts, _, out):
     blank = jnp.zeros((16, 128), F32)
     blocks = parts.shape[0] // 2
@@ -372,7 +386,6 @@
         [shaped((10, 32, 128), BF16), shaped((5, 32, 128), BF16)],
         [clip, upstream],
         fetch=(0, 1),
-        limit=60,
     )
     near_pairs = inside([(i, i + 1 if i % 2 else i - 1) for i in range(heights)], heights)
     edge = lax.ppermute(edge, "height", near_pairs)
@@ -385,6 +398,7 @@
         fetch=(0,),
         flops=2 * 27 * 16 * 256 * 128,
     )
+
     here, pieces = call(
         append_kernel,
         [shaped((15, 32, 128), BF16), shaped(pieces.shape, BF16)],
@@ -393,13 +407,20 @@
         idle=(0, 1, 2),
         alias={2: 1},
     )
+    pair = lax.ppermute(here, "tm", blocks)
+    forward, backward, pieces = call(
+        choose_kernel,
+        [shaped((12, 32, 128), BF16), shaped((3, 32, 128), BF16), shaped(pieces.shape, BF16)],
+        [here, pair, pieces],
+        fetch=(1,),
+        idle=(2,),
+        alias={2: 2},
+    )
     second = lax.all_to_all(pieces, "height", 0, 0).reshape(chans, 27 * OWN)
-
-    pair = lax.ppermute(here, "tm", blocks)
-    odd_pairs = inside([(t, t + 1 if t % 2 else t - 1) for t in range(tms)], tms)
-    even_pairs = inside([(t, t + 2 if t % 2 else t - 2) for t in range(tms)], tms)
-    odd = lax.ppermute(here, "tm", odd_pairs)
-    even = lax.ppermute(here, "tm", even_pairs)
+    forth = inside([(t, t + 2) for t in range(tms)], tms)
+    back = inside([(t, t - 2) for t in range(tms)], tms)
+    before = lax.ppermute(forward, "tm", forth)
+    after = lax.ppermute(backward, "tm", back)
 
     first = first_filter.reshape(27 * cin, chans)
     (band,) = call(
@@ -411,29 +432,24 @@
     )
 
     (packed,) = call(
-        pack_kernel, [shaped((45, 32, 128), BF16)], [here, pair, odd, even], fetch=(1, 2, 3)
+        pack_kernel, [shaped((45, 32, 128), BF16)], [here, pair, before, after], fetch=(1, 2, 3)
     )
     other = lax.ppermute(packed, "height", siblings)
 
     units, up_units = 6 * HIGH, 3 * HALF_HIGH
-    wide, ups, pre = call(
-        preact_kernel,
-        [
-            shaped((units, 16, 512), BF16),
-            shaped((2, up_units, 16, 256), BF16),
-            shaped((2, 2, 2, HALF, 16, 2 * OWN), F32),
+    grad_pre, parts = call(
+        middle_kernel,
+        [shaped((FRAMES, SPAN, 16, 2 * OWN), BF16), shaped((heights, 7, 16, cin), BF16)],
+        [packed, other, band, second],
+        scratch=[
+            pltpu.VMEM((units, 16, 512), BF16),
+            pltpu.VMEM((2, up_units, 16, 256), BF16),
+            pltpu.VMEM((2, 2, 2, HALF, 16, 2 * OWN), F32),
+            pltpu.VMEM((units, 32, 128), BF16),
+            pltpu.VMEM((up_units, 16, 256), BF16),
         ],
-        [packed, other, band],
-        scratch=[pltpu.VMEM((units, 32, 128), BF16), pltpu.VMEM((up_units, 16, 256), BF16)],
-        fetch=(0, 1),
-        flops=2 * 640 * 9 * 512 * 128,
-    )
-    grad_pre, parts = call(
-        gradient_kernel,
-        [shaped((FRAMES, SPAN, 16, 2 * OWN), BF16), shaped((heights, 7, 16, cin), BF16)],
-        [second, ups, pre, wide],
-        fetch=(0,),
-        flops=2 * 512 * 9 * 512 * 128,
+        fetch=(0, 1, 3),
+        flops=2 * 640 * 9 * 512 * 128 * 2,
     )
 
     planes = [
@@ -442,7 +458,6 @@
         for core in range(CORES)
     ]
     parts = lax.all_to_all(parts, ("tm", "height"), 0, 0, axis_index_groups=planes)
-    back = inside([(t, t - 2) for t in range(tms)], tms)
     following = lax.ppermute(grad_pre[:2], "tm", back)
     (turned,) = call(
         turned_kernel,

time: 89.6 us -> 92 us (1.027)
  waiting for transfers between devices: 10.2 us -> 12.6 us
  starting transfers between devices: 58.5 us -> 56.9 us
  Pallas kernels: 15.2 us -> 16.2 us
  local copies, waits for them, and re-layouts: 3.25 us -> 4.23 us
    ppermute x2, waiting for transfers between devices: 0.01 us -> 3.85 us  [the longest x1 3.85 us: body(): after = lax.ppermute(backward, 'tm', back)]
    ppermute x1, starting transfers between devices: 7.92 us -> 4.66 us  [body(): pair = lax.ppermute(here, 'tm', blocks)]
    ppermute x1, waiting for transfers between devices: 6.02 us -> 2.82 us  [body(): pair = lax.ppermute(here, 'tm', blocks)]
    all_to_all x1, starting transfers between devices: 8.12 us -> 5.13 us  [body(): lax.all_to_all(parts, ('tm', 'height'), 0, 0, axis_index_groups=planes)]
    ppermute x2, starting transfers between devices: 1.95 us -> 3.82 us  [the longest x1 2.53 us: body(): before = lax.ppermute(forward, 'tm', forth)]
    all_to_all x1, waiting for transfers between devices: 0.01 us -> 1.52 us  [body(): second = lax.all_to_all(pieces, 'height', 0, 0).reshape(chans, 27 * OWN)]
    all_to_all x1, starting transfers between devices: 6.51 us -> 7.92 us  [body(): second = lax.all_to_all(pieces, 'height', 0, 0).reshape(chans, 27 * OWN)]
    all_to_all x1, starting transfers between devices: 17.1 us -> 18.3 us  [body(): summed = lax.all_to_all(sums, 'tm', 0, 0, axis_index_groups=columns)]
  transfers between devices with their start and end apart: 11 -> 11, of which waited for: 4 -> 6; matrix products, arithmetic and copies ran while one was open for 0% -> 0% of each run, Pallas kernels for 11% -> 8%
where the time goes in v4:
time: 92 us; the launch traced here: 90.8 us
  starting transfers between devices  56.9 us (62%)
  Pallas kernels  16.2 us (18%)
  waiting for transfers between devices  12.6 us (14%)
  local copies, waits for them, and re-layouts  4.23 us (5%)
    all_to_all x1, starting transfers between devices, body(): summed = lax.all_to_all(sums, 'tm', 0, 0, axis_index_groups=columns)  18.3 us
    pallas_call x13, Pallas kernels, call(): pl.pallas_call(run, out_shape=tuple(out), in_specs=[far if i in fetch or...  16.2 us
    all_to_all x1, starting transfers between devices, body(): second = lax.all_to_all(pieces, 'height', 0, 0).reshape(chans, 27 * OWN)  7.92 us
    all_to_all x1, starting transfers between devices, body(): lax.all_to_all(parts, ('tm', 'height'), 0, 0, axis_index_groups=planes)  5.13 us
    ppermute x1, starting transfers between devices, body(): got = lax.ppermute(send, 'tm', blocks)  5.06 us
    ppermute x1, starting transfers between devices, body(): pair = lax.ppermute(here, 'tm', blocks)  4.66 us
    ppermute x1, starting transfers between devices, body(): edge = lax.ppermute(edge, 'height', near_pairs)  4.59 us
    unnamed x12, local copies, waits for them, and re-layouts  4.22 us
  transfers between devices with their start and end apart: 11, of which 6 were waited for; matrix products, arithmetic and copies ran while one was open for 0% of the time, Pallas kernels for 8%

profile of v4, /device:TPU:1, one launch (start us, length us, event | category | flops | bytes accessed | tf_op | source)
XLA Modules:
  0.0 90.8 jit_solution(15608038257255817935)
XLA Ops:
  0.6 0.0 copy-start.2
  0.6 0.8 copy-done.2
  1.5 0.0 copy-start.3
  1.5 0.7 copy-done.3
  2.2 0.1 shard_map.59
  2.3 4.6 %collective-permute-start = (bf16[5,32,128]{2,1,0:T(8,128)(2,1)S(1)}, bf16[5,32,128]{2,1,0:T(8,128)(2,1)S(1)}, u32[]{:S(2)}, u32[]{:S(2)}) collective-permute-start(bf16[5,32,128]{2,1,0:T(8,128)(2,1)S(1)} %get-tuple-element.18), channel_id=1, source_target_pairs={{1,2},{2,1},{3,4},{4,3},{5,6},{6,5},{7,8},{8,7},{9,10},{10,9},{11,... | collective-permute-start | bytes 122888 | tf_op jit(solution)/shard_map/ppermute | solution.py:391
  6.9 0.0 copy-start.1
  6.9 0.9 %copy-done.1 = bf16[3,3,3,256,16]{3,4,2,1,0:T(8,128)(2,1)S(1)} copy-done((bf16[3,3,3,256,16]{3,4,2,1,0:T(8,128)(2,1)S(1)}, bf16[3,3,3,256,16]{3,4,2,1,0:T(8,128)(2,1)}, u32[]{:S(2)}) %copy-start.1) | copy-done | bytes 221208
  7.9 1.6 %shard_map.60.refs_2_ = bf16[16,16,1728]{2,1,0:T(8,128)(2,1)} custom-call(bf16[27,16,256]{2,1,0:T(8,128)(2,1)S(1)} %bitcast.8), custom_call_target="tpu_custom_call" | custom-call | flops 28311552 | bytes 1105920 | tf_op jit(solution)/shard_map/pallas_call | solution.py:76
  9.4 0.0 collective-permute-done.refs_1_
  9.5 0.2 shard_map.61
  9.6 4.7 %collective-permute-start.1 = (bf16[15,32,128]{2,1,0:T(8,128)(2,1)S(1)}, bf16[15,32,128]{2,1,0:T(8,128)(2,1)S(1)}, u32[]{:S(2)}, u32[]{:S(2)}) collective-permute-start(bf16[15,32,128]{2,1,0:T(8,128)(2,1)S(1)} %get-tuple-element.19.refs_0_), channel_id=1, source_target_pairs={{0,16},{16,0},{32,48},{48,32},{64,80},{80,64},{96,112},{112,96},{1... | collective-permute-start | bytes 368648 | tf_op jit(solution)/shard_map/ppermute | solution.py:410
  14.3 2.8 %collective-permute-done.1.refs_1_ = bf16[15,32,128]{2,1,0:T(8,128)(2,1)S(1)} collective-permute-done((bf16[15,32,128]{2,1,0:T(8,128)(2,1)S(1)}, bf16[15,32,128]{2,1,0:T(8,128)(2,1)S(1)}, u32[]{:S(2)}, u32[]{:S(2)}) %collective-permute-start.1) | collective-permute-done | bytes 122912 | tf_op jit(solution)/shard_map/ppermute | solution.py:410
  17.1 0.2 shard_map.62
  17.3 0.0 copy-start
  17.3 7.9 %all-to-all-start = ((bf16[16,16,1728]{2,1,0:T(8,128)(2,1)}), bf16[16,16,1728]{2,1,0:T(8,128)(2,1)}, u32[]{:S(2)}, u32[]{:S(2)}) async-start(bf16[16,16,1728]{2,1,0:T(8,128)(2,1)} %get-tuple-element.23), calls=%async_computation | async-start | bytes 1835008 | tf_op jit(solution)/shard_map/all_to_all | solution.py:419
  25.2 2.5 %collective-permute-start.2 = (bf16[12,32,128]{2,1,0:T(8,128)(2,1)S(1)}, bf16[12,32,128]{2,1,0:T(8,128)(2,1)S(1)}, u32[]{:S(2)}, u32[]{:S(2)}) collective-permute-start(bf16[12,32,128]{2,1,0:T(8,128)(2,1)S(1)} %get-tuple-element.21), channel_id=1, source_target_pairs={{0,32},{16,48},{32,64},{48,80},{64,96},{80,112},{96,128},{112,144}... | collective-permute-start | bytes 294920 | tf_op jit(solution)/shard_map/ppermute | solution.py:422
  27.8 1.3 %collective-permute-start.3 = (bf16[3,32,128]{2,1,0:T(8,128)(2,1)S(1)}, bf16[3,32,128]{2,1,0:T(8,128)(2,1)S(1)}, u32[]{:S(2)}, u32[]{:S(2)}) collective-permute-start(bf16[3,32,128]{2,1,0:T(8,128)(2,1)S(1)} %get-tuple-element.22), channel_id=1, source_target_pairs={{32,0},{48,16},{64,32},{80,48},{96,64},{112,80},{128,96},{144,112}... | collective-permute-start | bytes 73736 | tf_op jit(solution)/shard_map/ppermute | solution.py:423
  29.1 3.8 %collective-permute-done.3.refs_3_ = bf16[3,32,128]{2,1,0:T(8,128)(2,1)S(1)} collective-permute-done((bf16[3,32,128]{2,1,0:T(8,128)(2,1)S(1)}, bf16[3,32,128]{2,1,0:T(8,128)(2,1)S(1)}, u32[]{:S(2)}, u32[]{:S(2)}) %collective-permute-start.3) | collective-permute-done | bytes 24608 | tf_op jit(solution)/shard_map/ppermute | solution.py:423
  32.9 0.0 collective-permute-done.2.refs_2_
  32.9 0.4 shard_map.63.refs_0_
  33.3 2.9 %collective-permute-start.4 = (bf16[45,32,128]{2,1,0:T(8,128)(2,1)S(1)}, bf16[45,32,128]{2,1,0:T(8,128)(2,1)S(1)}, u32[]{:S(2)}, u32[]{:S(2)}) collective-permute-start(bf16[45,32,128]{2,1,0:T(8,128)(2,1)S(1)} %shard_map.63.refs_0_), channel_id=1, source_target_pairs={{0,1},{1,0},{2,3},{3,2},{4,5},{5,4},{6,7},{7,6},{8,9},{9,8},{10,11... | collective-permute-start | bytes 1105928 | tf_op jit(solution)/shard_map/ppermute | solution.py:437
  36.3 0.0 copy-done
  36.3 1.0 %shard_map.64.refs_2_ = bf16[9,512,128]{2,1,0:T(8,128)(2,1)S(1)} custom-call(bf16[3456,256]{1,0:T(8,128)(2,1)S(1)} %bitcast.6), custom_call_target="tpu_custom_call" | custom-call | flops 226492416 | bytes 2949120 | tf_op jit(solution)/shard_map/pallas_call | solution.py:76
  37.3 0.3 collective-permute-done.4.refs_1_
  37.6 0.0 copy-start.4
  37.6 0.7 copy-done.4
  38.3 1.5 %all-to-all-done = bf16[16,16,1728]{2,1,0:T(8,128)(2,1)} async-done(((bf16[16,16,1728]{2,1,0:T(8,128)(2,1)}), bf16[16,16,1728]{2,1,0:T(8,128)(2,1)}, u32[]{:S(2)}, u32[]{:S(2)}) %all-to-all-start) | async-done | bytes 884768 | tf_op jit(solution)/shard_map/all_to_all | solution.py:419
  39.8 0.0 copy-start.5
  39.8 1.0 %copy-done.5 = bf16[45,32,128]{2,1,0:T(8,128)(2,1)S(1)} copy-done((bf16[45,32,128]{2,1,0:T(8,128)(2,1)S(1)}, bf16[45,32,128]{2,1,0:T(8,128)(2,1)}, u32[]{:S(2)}) %copy-start.5) | copy-done | bytes 368664
  40.8 7.7 %shard_map.65 = (bf16[4,10,16,128]{3,2,1,0:T(8,128)(2,1)S(1)}, bf16[16,7,16,128]{3,2,1,0:T(8,128)(2,1)}) custom-call(bf16[45,32,128]{2,1,0:T(8,128)(2,1)S(1)} %shard_map.63.refs_0_, bf16[45,32,128]{2,1,0:T(8,128)(2,1)S(1)} %copy-done.5, bf16[9,512,128]{2,1,0:T(8,128)(2,1)S(1)} %shard_map.64.refs_2_, bf16[256,1728]{1,0:T(8,128)(2,1)} %bitcast.3.refs_3_), custom_call_target="tpu_custom_call" | custom-call | flops 1509949440 | bytes 3424256 | tf_op jit(solution)/shard_map/pallas_call | solution.py:76
  48.6 5.1 %all-to-all-start.1 = ((bf16[16,7,16,128]{3,2,1,0:T(8,128)(2,1)}), bf16[16,7,16,128]{3,2,1,0:T(8,128)(2,1)S(1)}, u32[]{:S(2)}, u32[]{:S(2)}) async-start(bf16[16,7,16,128]{3,2,1,0:T(8,128)(2,1)} %get-tuple-element.29), calls=%async_computation.1 | async-start | bytes 917504 | tf_op jit(solution)/shard_map/all_to_all | solution.py:460
  53.7 1.3 %collective-permute-start.5 = (bf16[2,10,16,128]{3,2,1,0:T(8,128)(2,1)S(1)}, bf16[2,10,16,128]{3,2,1,0:T(8,128)(2,1)S(1)}, u32[]{:S(2)}, u32[]{:S(2)}) collective-permute-start(bf16[2,10,16,128]{3,2,1,0:T(8,128)(2,1)S(1)} %slice.3), channel_id=1, source_target_pairs={{32,0},{48,16},{64,32},{80,48},{96,64},{112,80},{128,96},{144,112}... | collective-permute-start | bytes 245768 | tf_op jit(solution)/shard_map/ppermute | solution.py:461
  55.0 1.0 %shard_map.66.refs_2_ = bf16[9,256,256]{2,1,0:T(8,128)(2,1)S(1)} custom-call(bf16[3456,256]{1,0:T(8,128)(2,1)S(1)} %bitcast.7, bf16[4,10,16,128]{3,2,1,0:T(8,128)(2,1)S(1)} %get-tuple-element.24.refs_1_.refs_0_), custom_call_target="tpu_custom_call" | custom-call | flops 113246208 | bytes 3112960 | tf_op jit(solution)/shard_map/pallas_call | solution.py:76
  56.1 3.3 %collective-permute-done.5.refs_1_ = bf16[2,10,16,128]{3,2,1,0:T(8,128)(2,1)S(1)} collective-permute-done((bf16[2,10,16,128]{3,2,1,0:T(8,128)(2,1)S(1)}, bf16[2,10,16,128]{3,2,1,0:T(8,128)(2,1)S(1)}, u32[]{:S(2)}, u32[]{:S(2)}) %collective-permute-start.5) | collective-permute-done | bytes 81952 | tf_op jit(solution)/shard_map/ppermute | solution.py:461
  59.4 1.1 %shard_map.67 = (f32[4,4,16,256]{3,2,1,0:T(8,128)S(1)}, f32[4,4,16,256]{3,2,1,0:T(8,128)S(1)}) custom-call(bf16[4,10,16,128]{3,2,1,0:T(8,128)(2,1)S(1)} %get-tuple-element.24.refs_1_.refs_0_, bf16[2,10,16,128]{3,2,1,0:T(8,128)(2,1)S(1)} %collective-permute-done.5.refs_1_, bf16[9,256,256]{2,1,0:T(8,128)(2,1)S(1)} %shard_map.66.refs_2_), custom_call_target="tpu_custom_call" | custom-call | flops 603979776 | bytes 1949696 | tf_op jit(solution)/shard_map/pallas_call | solution.py:76
  60.5 3.2 %collective-permute-start.6 = (f32[4,4,16,256]{3,2,1,0:T(8,128)S(1)}, f32[4,4,16,256]{3,2,1,0:T(8,128)S(1)}, u32[]{:S(2)}, u32[]{:S(2)}) collective-permute-start(f32[4,4,16,256]{3,2,1,0:T(8,128)S(1)} %get-tuple-element.26.refs_1_), channel_id=1, source_target_pairs={{0,1},{1,0},{2,3},{3,2},{4,5},{5,4},{6,7},{7,6},{8,9},{9,8},{10,11... | collective-permute-start | bytes 786440 | tf_op jit(solution)/shard_map/ppermute | solution.py:488
  63.8 0.0 all-to-all-done.1.refs_0_
  63.8 1.0 %shard_map.69 = bf16[16,16,128]{2,1,0:T(8,128)(2,1)} custom-call(bf16[16,7,16,128]{3,2,1,0:T(8,128)(2,1)S(1)} %all-to-all-done.1.refs_0_, f32[4,4,16,256]{3,2,1,0:T(8,128)S(1)} %get-tuple-element.26.refs_1_), custom_call_target="tpu_custom_call" | custom-call | bytes 786432 | tf_op jit(solution)/shard_map/pallas_call | solution.py:76
  64.8 18.3 %all-to-all-start.2 = ((bf16[16,16,128]{2,1,0:T(8,128)(2,1)}), bf16[16,16,128]{2,1,0:T(8,128)(2,1)S(1)}, u32[]{:S(2)}, u32[]{:S(2)}) async-start(bf16[16,16,128]{2,1,0:T(8,128)(2,1)} %shard_map.69), calls=%async_computation.2 | async-start | bytes 131072 | tf_op jit(solution)/shard_map/all_to_all | solution.py:487
  83.1 0.0 collective-permute-done.6.refs_1_
  83.1 0.1 shard_map.68
  83.2 5.1 %collective-permute-start.7 = (bf16[2,4,16,256]{3,2,1,0:T(8,128)(2,1)S(1)}, bf16[2,4,16,256]{3,2,1,0:T(8,128)(2,1)S(1)}, u32[]{:S(2)}, u32[]{:S(2)}) collective-permute-start(bf16[2,4,16,256]{3,2,1,0:T(8,128)(2,1)S(1)} %get-tuple-element.28), channel_id=1, source_target_pairs={{0,16},{16,0},{32,48},{48,32},{64,80},{80,64},{96,112},{112,96},{1... | collective-permute-start | bytes 196616 | tf_op jit(solution)/shard_map/ppermute | solution.py:495
  88.3 0.0 all-to-all-done.2.refs_0_
  88.3 0.8 shard_map.70
  89.1 0.8 collective-permute-done.7.refs_1_
  89.9 0.9 shard_map.71
  (1 shorter events, 0.0 us)
Async XLA Ops:
  0.6 0.8 copy-start.2
  1.5 0.7 copy-start.3
  2.3 7.1 %collective-permute-start = (bf16[5,32,128]{2,1,0:T(8,128)(2,1)S(1)}, bf16[5,32,128]{2,1,0:T(8,128)(2,1)S(1)}, u32[]{:S(2)}, u32[]{:S(2)}) collective-permute-start(bf16[5,32,128]{2,1,0:T(8,128)(2,1)S(1)} %get-tuple-element.18), channel_id=1, source_target_pairs={{1,2},{2,1},{3,4},{4,3},{5,6},{6,5},{7,8},{8,7},{9,10},{10,9},{11,... | collective-permute-start | bytes 122888 | tf_op jit(solution)/shard_map/ppermute | solution.py:391
  6.9 0.9 %copy-start.1 = (bf16[3,3,3,256,16]{3,4,2,1,0:T(8,128)(2,1)S(1)}, bf16[3,3,3,256,16]{3,4,2,1,0:T(8,128)(2,1)}, u32[]{:S(2)}) copy-start(bf16[3,3,3,256,16]{3,4,2,1,0:T(8,128)(2,1)} %param.6) | copy-start | bytes 663556
  9.6 7.5 %collective-permute-start.1 = (bf16[15,32,128]{2,1,0:T(8,128)(2,1)S(1)}, bf16[15,32,128]{2,1,0:T(8,128)(2,1)S(1)}, u32[]{:S(2)}, u32[]{:S(2)}) collective-permute-start(bf16[15,32,128]{2,1,0:T(8,128)(2,1)S(1)} %get-tuple-element.19.refs_0_), channel_id=1, source_target_pairs={{0,16},{16,0},{32,48},{48,32},{64,80},{80,64},{96,112},{112,96},{1... | collective-permute-start | bytes 368648 | tf_op jit(solution)/shard_map/ppermute | solution.py:410
  17.3 19.0 %copy-start = (bf16[3,3,3,128,256]{4,3,2,1,0:T(8,128)(2,1)S(1)}, bf16[3,3,3,128,256]{4,3,2,1,0:T(8,128)(2,1)}, u32[]{:S(2)}) copy-start(bf16[3,3,3,128,256]{4,3,2,1,0:T(8,128)(2,1)} %param.5) | copy-start | bytes 5308420
  17.3 22.5 %all-to-all-start = ((bf16[16,16,1728]{2,1,0:T(8,128)(2,1)}), bf16[16,16,1728]{2,1,0:T(8,128)(2,1)}, u32[]{:S(2)}, u32[]{:S(2)}) async-start(bf16[16,16,1728]{2,1,0:T(8,128)(2,1)} %get-tuple-element.23), calls=%async_computation | async-start | bytes 1835008 | tf_op jit(solution)/shard_map/all_to_all | solution.py:419
  25.2 7.7 %collective-permute-start.2 = (bf16[12,32,128]{2,1,0:T(8,128)(2,1)S(1)}, bf16[12,32,128]{2,1,0:T(8,128)(2,1)S(1)}, u32[]{:S(2)}, u32[]{:S(2)}) collective-permute-start(bf16[12,32,128]{2,1,0:T(8,128)(2,1)S(1)} %get-tuple-element.21), channel_id=1, source_target_pairs={{0,32},{16,48},{32,64},{48,80},{64,96},{80,112},{96,128},{112,144}... | collective-permute-start | bytes 294920 | tf_op jit(solution)/shard_map/ppermute | solution.py:422
  27.8 5.1 %collective-permute-start.3 = (bf16[3,32,128]{2,1,0:T(8,128)(2,1)S(1)}, bf16[3,32,128]{2,1,0:T(8,128)(2,1)S(1)}, u32[]{:S(2)}, u32[]{:S(2)}) collective-permute-start(bf16[3,32,128]{2,1,0:T(8,128)(2,1)S(1)} %get-tuple-element.22), channel_id=1, source_target_pairs={{32,0},{48,16},{64,32},{80,48},{96,64},{112,80},{128,96},{144,112}... | collective-permute-start | bytes 73736 | tf_op jit(solution)/shard_map/ppermute | solution.py:423
  33.3 4.2 %collective-permute-start.4 = (bf16[45,32,128]{2,1,0:T(8,128)(2,1)S(1)}, bf16[45,32,128]{2,1,0:T(8,128)(2,1)S(1)}, u32[]{:S(2)}, u32[]{:S(2)}) collective-permute-start(bf16[45,32,128]{2,1,0:T(8,128)(2,1)S(1)} %shard_map.63.refs_0_), channel_id=1, source_target_pairs={{0,1},{1,0},{2,3},{3,2},{4,5},{5,4},{6,7},{7,6},{8,9},{9,8},{10,11... | collective-permute-start | bytes 1105928 | tf_op jit(solution)/shard_map/ppermute | solution.py:437
  37.6 0.7 copy-start.4
  39.8 1.0 %copy-start.5 = (bf16[45,32,128]{2,1,0:T(8,128)(2,1)S(1)}, bf16[45,32,128]{2,1,0:T(8,128)(2,1)}, u32[]{:S(2)}) copy-start(bf16[45,32,128]{2,1,0:T(8,128)(2,1)} %copy-done.4) | copy-start | bytes 1105924
  48.6 15.2 %all-to-all-start.1 = ((bf16[16,7,16,128]{3,2,1,0:T(8,128)(2,1)}), bf16[16,7,16,128]{3,2,1,0:T(8,128)(2,1)S(1)}, u32[]{:S(2)}, u32[]{:S(2)}) async-start(bf16[16,7,16,128]{3,2,1,0:T(8,128)(2,1)} %get-tuple-element.29), calls=%async_computation.1 | async-start | bytes 917504 | tf_op jit(solution)/shard_map/all_to_all | solution.py:460
  53.7 5.7 %collective-permute-start.5 = (bf16[2,10,16,128]{3,2,1,0:T(8,128)(2,1)S(1)}, bf16[2,10,16,128]{3,2,1,0:T(8,128)(2,1)S(1)}, u32[]{:S(2)}, u32[]{:S(2)}) collective-permute-start(bf16[2,10,16,128]{3,2,1,0:T(8,128)(2,1)S(1)} %slice.3), channel_id=1, source_target_pairs={{32,0},{48,16},{64,32},{80,48},{96,64},{112,80},{128,96},{144,112}... | collective-permute-start | bytes 245768 | tf_op jit(solution)/shard_map/ppermute | solution.py:461
  60.5 22.6 %collective-permute-start.6 = (f32[4,4,16,256]{3,2,1,0:T(8,128)S(1)}, f32[4,4,16,256]{3,2,1,0:T(8,128)S(1)}, u32[]{:S(2)}, u32[]{:S(2)}) collective-permute-start(f32[4,4,16,256]{3,2,1,0:T(8,128)S(1)} %get-tuple-element.26.refs_1_), channel_id=1, source_target_pairs={{0,1},{1,0},{2,3},{3,2},{4,5},{5,4},{6,7},{7,6},{8,9},{9,8},{10,11... | collective-permute-start | bytes 786440 | tf_op jit(solution)/shard_map/ppermute | solution.py:488
  64.8 23.4 %all-to-all-start.2 = ((bf16[16,16,128]{2,1,0:T(8,128)(2,1)}), bf16[16,16,128]{2,1,0:T(8,128)(2,1)S(1)}, u32[]{:S(2)}, u32[]{:S(2)}) async-start(bf16[16,16,128]{2,1,0:T(8,128)(2,1)} %shard_map.69), calls=%async_computation.2 | async-start | bytes 131072 | tf_op jit(solution)/shard_map/all_to_all | solution.py:487
  83.2 6.7 %collective-permute-start.7 = (bf16[2,4,16,256]{3,2,1,0:T(8,128)(2,1)S(1)}, bf16[2,4,16,256]{3,2,1,0:T(8,128)(2,1)S(1)}, u32[]{:S(2)}, u32[]{:S(2)}) collective-permute-start(bf16[2,4,16,256]{3,2,1,0:T(8,128)(2,1)S(1)} %get-tuple-element.28), channel_id=1, source_target_pairs={{0,16},{16,0},{32,48},{48,32},{64,80},{80,64},{96,112},{112,96},{1... | collective-permute-start | bytes 196616 | tf_op jit(solution)/shard_map/ppermute | solution.py:495

commit v5 on v4

--- a/solution.py
+++ b/solution.py
@@ -110,7 +110,7 @@
                 out[p, :, place * OWN : place * OWN + piece.shape[1]] = piece
 
 
-def band_kernel(first, band):
+def own_filter_kernel(first, band, flat):
     chans = first.shape[1]
     x, core = lax.axis_index("tm") % 2, lax.axis_index("height") % CORES
     row = lax.broadcasted_iota(jnp.int32, (chans, 2 * OWN), 0)
@@ -119,31 +119,18 @@
     twice = mm(first[...], pick)
     lane = lax.broadcasted_iota(jnp.int32, (128, 2 * OWN), 1)
     for ab in range(9):
+        lanes = slice((ab % 3) * 128, (ab % 3 + 1) * 128)
         for s in range(4):
             left = twice[(ab * 3 + s) * 128 : (ab * 3 + s + 1) * 128] if s < 3 else 0.0
             right = twice[(ab * 3 + s - 1) * 128 : (ab * 3 + s) * 128] if s > 0 else 0.0
             both = jnp.where(lane < OWN, left, right)
-            band[ab, s * 128 : (s + 1) * 128] = both.astype(BF16)
-
-
-def turned_kernel(first, _, turned):
-    chans = first.shape[1]
-    x, core = lax.axis_index("tm") % 2, lax.axis_index("height") % CORES
+            band[ab // 3, s * 128 : (s + 1) * 128, lanes] = both.astype(BF16)
     row = lax.broadcasted_iota(jnp.int32, (OWN, chans), 0)
     col = lax.broadcasted_iota(jnp.int32, (OWN, chans), 1)
     pick = jnp.where(own_channel(row, x, core) == col, 1.0, 0.0).astype(BF16)
-    flat = lax.dot_general(
+    flat[...] = lax.dot_general(
         pick, first[...], (((1,), (1,)), ((), ())), preferred_element_type=F32
     ).astype(BF16)
-    for ab in range(9):
-        for slot, s in enumerate(MIDDLE):
-            for jp in range(2):
-                c = jp + 2 - s
-                if 0 <= c <= 2:
-                    piece = flat[:, (ab * 3 + c) * 128 : (ab * 3 + c + 1) * 128]
-                else:
-                    piece = jnp.zeros((OWN, 128), BF16)
-                turned[ab, slot * OWN : (slot + 1) * OWN, jp * 128 : (jp + 1) * 128] = piece
 
 
 def stack_kernel(clip, up, here, edge):
@@ -228,13 +215,16 @@
         for s in range(4):
             piece = moved[128 * s : 128 * s + 128].reshape(8, 16, 128)
             wide[8 * g : 8 * g + 8, :, s * 128 : (s + 1) * 128] = piece
-    total = jnp.zeros((FRAMES * SPAN * 16, 2 * OWN), F32)
+    total = jnp.zeros((FRAMES, SPAN, 16, 2 * OWN), F32)
     for a in range(3):
-        for b in range(3):
-            tops = [(a + f) * HIGH + b for f in range(FRAMES)]
-            win = jnp.concatenate([wide[x : x + SPAN] for x in tops], 0)
-            total = total + mm(win.reshape(FRAMES * SPAN * 16, 512), filters[a * 3 + b])
-    total = total.reshape(FRAMES, SPAN, 16, 2 * OWN)
+        tops = [(a + f) * HIGH for f in range(FRAMES)]
+        win = jnp.concatenate([wide[x : x + SPAN + 1] for x in tops], 0)
+        prod = mm(win.reshape(FRAMES * (SPAN + 1) * 16, 512), filters[a, :, : 4 * OWN])
+        prod = prod.reshape(FRAMES, SPAN + 1, 16, 4 * OWN)
+        total = total + prod[:, :SPAN, :, : 2 * OWN] + prod[:, 1:, :, 2 * OWN :]
+        win = jnp.concatenate([wide[x + 2 : x + 2 + SPAN] for x in tops], 0)
+        prod = mm(win.reshape(FRAMES * SPAN * 16, 512), filters[a, :, 4 * OWN :])
+        total = total + prod.reshape(FRAMES, SPAN, 16, 2 * OWN)
     for f in range(FRAMES):
         for r in range(SPAN):
             pre[f % 2, r % 2, f // 2, r // 2] = total[f, r]
@@ -295,11 +285,6 @@
             parts[x * blocks : (x + 1) * blocks, k] = both[:, :, 128 * x : 128 * x + 128]
 
 
-def middle_kernel(own, other, filters, second, grad, parts, wide, ups, pre, band, ext):
-    preact_kernel(own, other, filters, wide, ups, pre, band, ext)
-    gradient_kernel(second, ups, pre, wide, grad, parts)
-
-
 def sum_turn_kernel(parts, _, out):
     blank = jnp.zeros((16, 128), F32)
     blocks = parts.shape[0] // 2
@@ -329,7 +314,16 @@
     mark[...] = jnp.zeros_like(mark)
 
 
-def clip_kernel(grad, following, filters, keep, send, wide):
+def clip_kernel(grad, following, flat, keep, send, wide, filters):
+    for ab in range(9):
+        for slot, s in enumerate(MIDDLE):
+            for jp in range(2):
+                c = jp + 2 - s
+                if 0 <= c <= 2:
+                    piece = flat[:, (ab * 3 + c) * 128 : (ab * 3 + c + 1) * 128]
+                else:
+                    piece = jnp.zeros((OWN, 128), BF16)
+                filters[ab, slot * OWN : (slot + 1) * OWN, jp * 128 : (jp + 1) * 128] = piece
     lane = lax.broadcasted_iota(jnp.int32, (192, 2 * OWN), 1)
     up = one_hot(192, 192, lambda r: jnp.where(r % 16 == 15, -1, r + 1))
     down = one_hot(192, 192, lambda r: jnp.where(r % 16 == 0, -1, r - 1))
@@ -347,22 +341,20 @@
             win = jnp.concatenate([wide[x : x + ROWS] for x in tops], 0)
             total = total + mm(win.reshape(FRAMES * ROWS * 16, 4 * OWN), filters[a * 3 + b])
     total = total.reshape(FRAMES, ROWS, 16, 256)
-    low, high = total[:, :4], total[:, 4:]
+    first = lax.axis_index("tm") % 2 == 0
+    keep[...] = jnp.where(first, total[:2], total[2:])
+    send[...] = jnp.where(first, total[2:], total[:2]).astype(BF16)
+
+
+def halve_kernel(kept, got, keep, send):
+    total = kept[...] + got[...].astype(F32)
     even = lax.axis_index("height") % CORES == 0
-    keep[...] = jnp.where(even, low, high)
-    send[...] = jnp.where(even, high, low)
-
-
-def halve_kernel(kept, got, keep, send):
-    total = kept[...] + got[...]
-    first = lax.axis_index("tm") % 2 == 0
-    low, high = total[:2], total[2:]
-    keep[...] = jnp.where(first, low, high)
-    send[...] = jnp.where(first, high, low).astype(BF16)
+    keep[...] = jnp.where(even, total[:, :4], total[:, 4:])
+    send[...] = jnp.where(even, total[:, 4:], total[:, :4])
 
 
 def join_kernel(kept, got, _, out):
-    total = (kept[...] + got[...].astype(F32)).astype(BF16).reshape(128, 256)
+    total = (kept[...] + got[...]).astype(BF16).reshape(128, 256)
     low = one_hot(256, 128, lambda r: jnp.where(r % 2 == 0, (r // 32) * 16 + (r % 32) // 2, -1))
     high = one_hot(256, 128, lambda r: jnp.where(r % 2 == 1, (r // 32) * 16 + (r % 32) // 2, -1))
     moved = mm(low, total[:, :128]) + mm(high, total[:, 128:])
@@ -423,12 +415,12 @@
     after = lax.ppermute(backward, "tm", back)
 
     first = first_filter.reshape(27 * cin, chans)
-    (band,) = call(
-        band_kernel,
-        [shaped((9, 512, 2 * OWN), BF16)],
+    band, flat = call(
+        own_filter_kernel,
+        [shaped((3, 512, 6 * OWN), BF16), shaped((OWN, 27 * cin), BF16)],
         [first],
         fetch=(0,),
-        flops=2 * 27 * 128 * 256 * 128,
+        flops=3 * 27 * 128 * 256 * 128,
     )
 
     (packed,) = call(
@@ -437,19 +429,24 @@
     other = lax.ppermute(packed, "height", siblings)
 
     units, up_units = 6 * HIGH, 3 * HALF_HIGH
+    wide, ups, pre = call(
+        preact_kernel,
+        [
+            shaped((units, 16, 512), BF16),
+            shaped((2, up_units, 16, 256), BF16),
+            shaped((2, 2, 2, HALF, 16, 2 * OWN), F32),
+        ],
+        [packed, other, band],
+        scratch=[pltpu.VMEM((units, 32, 128), BF16), pltpu.VMEM((up_units, 16, 256), BF16)],
+        fetch=(1,),
+        flops=2 * 640 * 9 * 512 * 128,
+    )
     grad_pre, parts = call(
-        middle_kernel,
+        gradient_kernel,
         [shaped((FRAMES, SPAN, 16, 2 * OWN), BF16), shaped((heights, 7, 16, cin), BF16)],
-        [packed, other, band, second],
-        scratch=[
-            pltpu.VMEM((units, 16, 512), BF16),
-            pltpu.VMEM((2, up_units, 16, 256), BF16),
-            pltpu.VMEM((2, 2, 2, HALF, 16, 2 * OWN), F32),
-            pltpu.VMEM((units, 32, 128), BF16),
-            pltpu.VMEM((up_units, 16, 256), BF16),
-        ],
-        fetch=(0, 1, 3),
-        flops=2 * 640 * 9 * 512 * 128 * 2,
+        [second, ups, pre, wide],
+        fetch=(0,),
+        flops=2 * 512 * 9 * 512 * 128,
     )
 
     planes = [
@@ -459,19 +456,14 @@
     ]
     parts = lax.all_to_all(parts, ("tm", "height"), 0, 0, axis_index_groups=planes)
     following = lax.ppermute(grad_pre[:2], "tm", back)
-    (turned,) = call(
-        turned_kernel,
-        [shaped((9, 4 * OWN, 2 * cin), BF16)],
-        [first, grad_pre],
-        fetch=(0,),
-        idle=(1,),
-        flops=2 * 27 * 128 * 256 * 64,
-    )
     keep, send = call(
         clip_kernel,
-        [shaped((FRAMES, rows, 16, 2 * cin), F32)] * 2,
-        [grad_pre, following, turned],
-        scratch=[pltpu.VMEM(((FRAMES + 2) * SPAN, 16, 4 * OWN), BF16)],
+        [shaped((2, ROWS, 16, 2 * cin), F32), shaped((2, ROWS, 16, 2 * cin), BF16)],
+        [grad_pre, following, flat],
+        scratch=[
+            pltpu.VMEM(((FRAMES + 2) * SPAN, 16, 4 * OWN), BF16),
+            pltpu.VMEM((9, 4 * OWN, 2 * cin), BF16),
+        ],
         fetch=(1,),
         flops=2 * 512 * 9 * 256 * 256,
     )
@@ -485,14 +477,14 @@
     )
     columns = [[2 * ((i + 8) % lines) + x for i in range(lines)] for x in range(2)]
     summed = lax.all_to_all(sums, "tm", 0, 0, axis_index_groups=columns)
-    got = lax.ppermute(send, "height", siblings)
+    got = lax.ppermute(send, "tm", blocks)
     keep, send = call(
         halve_kernel,
-        [shaped((2, rows, 16, 2 * cin), F32), shaped((2, rows, 16, 2 * cin), BF16)],
+        [shaped((2, rows, 16, 2 * cin), F32)] * 2,
         [keep, got],
         fetch=(1,),
     )
-    got = lax.ppermute(send, "tm", blocks)
+    got = lax.ppermute(send, "height", siblings)
     count = frames * tms * rows * heights * width
     grad_filter, mark = call(
         functools.partial(finish_kernel, 1.0 / float(count) ** 0.5),

time: 92 us -> 87.3 us (0.949)
  Pallas kernels: 16.2 us -> 13 us
  starting transfers between devices: 56.9 us -> 58.9 us
  local copies, waits for them, and re-layouts: 4.23 us -> 2.49 us
  waiting for transfers between devices: 12.6 us -> 11.3 us
    pallas_call x13, Pallas kernels: 16.2 us -> 13 us  [call(): pl.pallas_call(run, out_shape=tuple(out), in_specs=[far if i in fetch or...]
    unnamed x12 -> x8, local copies, waits for them, and re-layouts: 4.22 us -> 2.49 us
    all_to_all x1, starting transfers between devices: 5.13 us -> 6.7 us  [body(): lax.all_to_all(parts, ('tm', 'height'), 0, 0, axis_index_groups=planes)]
    all_to_all x1, waiting for transfers between devices: 1.52 us -> 0.01 us  [body(): second = lax.all_to_all(pieces, 'height', 0, 0).reshape(chans, 27 * OWN)]
    ppermute x1, waiting for transfers between devices: 3.32 us -> 4.59 us  [body(): following = lax.ppermute(grad_pre[:2], 'tm', back)]
    ppermute x1, starting transfers between devices: 3.23 us -> 4.31 us  [body(): got = lax.ppermute(send, 'height', siblings)]
  transfers between devices with their start and end apart: 11 -> 11, of which waited for: 6 -> 4; matrix products, arithmetic and copies ran while one was open for 0% -> 0% of each run, Pallas kernels for 8% -> 10%
where the time goes in v5:
time: 87.3 us; the launch traced here: 86.6 us
  starting transfers between devices  58.9 us (67%)
  Pallas kernels  13 us (15%)
  waiting for transfers between devices  11.3 us (13%)
  local copies, waits for them, and re-layouts  2.49 us (3%)
  between operations  0.88 us (1%)
    all_to_all x1, starting transfers between devices, body(): summed = lax.all_to_all(sums, 'tm', 0, 0, axis_index_groups=columns)  18.1 us
    pallas_call x13, Pallas kernels, call(): pl.pallas_call(run, out_shape=tuple(out), in_specs=[far if i in fetch or...  13 us
    all_to_all x1, starting transfers between devices, body(): second = lax.all_to_all(pieces, 'height', 0, 0).reshape(chans, 27 * OWN)  7.31 us
    all_to_all x1, starting transfers between devices, body(): lax.all_to_all(parts, ('tm', 'height'), 0, 0, axis_index_groups=planes)  6.7 us
    ppermute x1, starting transfers between devices, body(): pair = lax.ppermute(here, 'tm', blocks)  4.66 us
    ppermute x1, starting transfers between devices, body(): edge = lax.ppermute(edge, 'height', near_pairs)  4.59 us
    ppermute x1, waiting for transfers between devices, body(): following = lax.ppermute(grad_pre[:2], 'tm', back)  4.59 us
    ppermute x1, starting transfers between devices, body(): got = lax.ppermute(send, 'tm', blocks)  4.56 us
  transfers between devices with their start and end apart: 11, of which 4 were waited for; matrix products, arithmetic and copies ran while one was open for 0% of the time, Pallas kernels for 10%

profile of v5, /device:TPU:1, one launch (start us, length us, event | category | flops | bytes accessed | tf_op | source)
XLA Modules:
  0.0 86.6 jit_solution(2261247049055994580)
XLA Ops:
  0.6 0.0 copy-start.2
  0.6 0.8 copy-done.2
  1.5 0.0 copy-start.3
  1.5 0.7 copy-done.3
  2.2 0.1 shard_map.59
  2.3 4.6 %collective-permute-start = (bf16[5,32,128]{2,1,0:T(8,128)(2,1)S(1)}, bf16[5,32,128]{2,1,0:T(8,128)(2,1)S(1)}, u32[]{:S(2)}, u32[]{:S(2)}) collective-permute-start(bf16[5,32,128]{2,1,0:T(8,128)(2,1)S(1)} %get-tuple-element.23), channel_id=1, source_target_pairs={{1,2},{2,1},{3,4},{4,3},{5,6},{6,5},{7,8},{8,7},{9,10},{10,9},{11,... | collective-permute-start | bytes 122888 | tf_op jit(solution)/shard_map/ppermute | solution.py:383
  6.9 0.0 copy-start.1
  6.9 0.9 %copy-done.1 = bf16[3,3,3,256,16]{3,4,2,1,0:T(8,128)(2,1)S(1)} copy-done((bf16[3,3,3,256,16]{3,4,2,1,0:T(8,128)(2,1)S(1)}, bf16[3,3,3,256,16]{3,4,2,1,0:T(8,128)(2,1)}, u32[]{:S(2)}) %copy-start.1) | copy-done | bytes 221208
  7.9 1.6 %shard_map.60.refs_2_ = bf16[16,16,1728]{2,1,0:T(8,128)(2,1)} custom-call(bf16[27,16,256]{2,1,0:T(8,128)(2,1)S(1)} %bitcast.8), custom_call_target="tpu_custom_call" | custom-call | flops 28311552 | bytes 1105920 | tf_op jit(solution)/shard_map/pallas_call | solution.py:76
  9.4 0.0 collective-permute-done.refs_1_
  9.4 0.2 shard_map.61
  9.6 4.7 %collective-permute-start.1 = (bf16[15,32,128]{2,1,0:T(8,128)(2,1)S(1)}, bf16[15,32,128]{2,1,0:T(8,128)(2,1)S(1)}, u32[]{:S(2)}, u32[]{:S(2)}) collective-permute-start(bf16[15,32,128]{2,1,0:T(8,128)(2,1)S(1)} %get-tuple-element.24.refs_0_), channel_id=1, source_target_pairs={{0,16},{16,0},{32,48},{48,32},{64,80},{80,64},{96,112},{112,96},{1... | collective-permute-start | bytes 368648 | tf_op jit(solution)/shard_map/ppermute | solution.py:402
  14.3 2.8 %collective-permute-done.1.refs_1_ = bf16[15,32,128]{2,1,0:T(8,128)(2,1)S(1)} collective-permute-done((bf16[15,32,128]{2,1,0:T(8,128)(2,1)S(1)}, bf16[15,32,128]{2,1,0:T(8,128)(2,1)S(1)}, u32[]{:S(2)}, u32[]{:S(2)}) %collective-permute-start.1) | collective-permute-done | bytes 122912 | tf_op jit(solution)/shard_map/ppermute | solution.py:402
  17.1 0.2 shard_map.62
  17.3 0.0 copy-start
  17.3 7.3 %all-to-all-start = ((bf16[16,16,1728]{2,1,0:T(8,128)(2,1)}), bf16[16,16,1728]{2,1,0:T(8,128)(2,1)S(1)}, u32[]{:S(2)}, u32[]{:S(2)}) async-start(bf16[16,16,1728]{2,1,0:T(8,128)(2,1)} %get-tuple-element.26), calls=%async_computation | async-start | bytes 1835008 | tf_op jit(solution)/shard_map/all_to_all | solution.py:411
  24.6 3.2 %collective-permute-start.2 = (bf16[12,32,128]{2,1,0:T(8,128)(2,1)S(1)}, bf16[12,32,128]{2,1,0:T(8,128)(2,1)S(1)}, u32[]{:S(2)}, u32[]{:S(2)}) collective-permute-start(bf16[12,32,128]{2,1,0:T(8,128)(2,1)S(1)} %get-tuple-element.27), channel_id=1, source_target_pairs={{0,32},{16,48},{32,64},{48,80},{64,96},{80,112},{96,128},{112,144}... | collective-permute-start | bytes 294920 | tf_op jit(solution)/shard_map/ppermute | solution.py:414
  27.8 1.3 %collective-permute-start.3 = (bf16[3,32,128]{2,1,0:T(8,128)(2,1)S(1)}, bf16[3,32,128]{2,1,0:T(8,128)(2,1)S(1)}, u32[]{:S(2)}, u32[]{:S(2)}) collective-permute-start(bf16[3,32,128]{2,1,0:T(8,128)(2,1)S(1)} %get-tuple-element.28), channel_id=1, source_target_pairs={{32,0},{48,16},{64,32},{80,48},{96,64},{112,80},{128,96},{144,112}... | collective-permute-start | bytes 73736 | tf_op jit(solution)/shard_map/ppermute | solution.py:415
  29.1 3.7 %collective-permute-done.3.refs_3_ = bf16[3,32,128]{2,1,0:T(8,128)(2,1)S(1)} collective-permute-done((bf16[3,32,128]{2,1,0:T(8,128)(2,1)S(1)}, bf16[3,32,128]{2,1,0:T(8,128)(2,1)S(1)}, u32[]{:S(2)}, u32[]{:S(2)}) %collective-permute-start.3) | collective-permute-done | bytes 24608 | tf_op jit(solution)/shard_map/ppermute | solution.py:415
  32.8 0.0 collective-permute-done.2.refs_2_
  32.8 0.4 shard_map.63.refs_0_
  33.2 2.9 %collective-permute-start.4 = (bf16[45,32,128]{2,1,0:T(8,128)(2,1)S(1)}, bf16[45,32,128]{2,1,0:T(8,128)(2,1)S(1)}, u32[]{:S(2)}, u32[]{:S(2)}) collective-permute-start(bf16[45,32,128]{2,1,0:T(8,128)(2,1)S(1)} %shard_map.63.refs_0_), channel_id=1, source_target_pairs={{0,1},{1,0},{2,3},{3,2},{4,5},{5,4},{6,7},{7,6},{8,9},{9,8},{10,11... | collective-permute-start | bytes 1105928 | tf_op jit(solution)/shard_map/ppermute | solution.py:429
  36.2 0.0 copy-done
  36.2 1.5 %shard_map.64 = (bf16[3,512,384]{2,1,0:T(8,128)(2,1)S(1)}, bf16[64,3456]{1,0:T(8,128)(2,1)S(1)}) custom-call(bf16[3456,256]{1,0:T(8,128)(2,1)S(1)} %bitcast.7), custom_call_target="tpu_custom_call" | custom-call | flops 339738624 | bytes 3391488 | tf_op jit(solution)/shard_map/pallas_call | solution.py:76
  37.7 0.0 collective-permute-done.4.refs_1_
  37.7 2.2 %shard_map.65 = (bf16[72,16,512]{2,1,0:T(8,128)(2,1)S(1)}, bf16[2,18,16,256]{3,2,1,0:T(8,128)(2,1)S(1)}, f32[2,2,2,5,16,128]{5,4,3,2,1,0:T(8,128)S(1)}) custom-call(bf16[45,32,128]{2,1,0:T(8,128)(2,1)S(1)} %shard_map.63.refs_0_, bf16[45,32,128]{2,1,0:T(8,128)(2,1)S(1)} %collective-permute-done.4.refs_1_, bf16[3,512,384]{2,1,0:T(8,128)(2,1)S(1)} %get-tuple-element.29.refs_2_), custom_call_target="tpu_custom_call" | custom-call | flops 754974720 | bytes 3719168 | tf_op jit(solution)/shard_map/pallas_call | solution.py:76
  40.0 0.0 all-to-all-done
  40.0 2.6 %shard_map.66 = (bf16[4,10,16,128]{3,2,1,0:T(8,128)(2,1)S(1)}, bf16[16,7,16,128]{3,2,1,0:T(8,128)(2,1)}) custom-call(bf16[256,1728]{1,0:T(8,128)(2,1)S(1)} %bitcast.6, bf16[2,18,16,256]{3,2,1,0:T(8,128)(2,1)S(1)} %get-tuple-element.30.refs_1_, f32[2,2,2,5,16,128]{5,4,3,2,1,0:T(8,128)S(1)} %get-tuple-element.31.refs_2_, ...), custom_call_target="tpu_custom_call" | custom-call | flops 603979776 | bytes 3309568 | tf_op jit(solution)/shard_map/pallas_call | solution.py:76
  42.6 6.7 %all-to-all-start.1 = ((bf16[16,7,16,128]{3,2,1,0:T(8,128)(2,1)}), bf16[16,7,16,128]{3,2,1,0:T(8,128)(2,1)S(1)}, u32[]{:S(2)}, u32[]{:S(2)}) async-start(bf16[16,7,16,128]{3,2,1,0:T(8,128)(2,1)} %get-tuple-element.39), calls=%async_computation.1 | async-start | bytes 917504 | tf_op jit(solution)/shard_map/all_to_all | solution.py:457
  49.3 1.3 %collective-permute-start.5 = (bf16[2,10,16,128]{3,2,1,0:T(8,128)(2,1)S(1)}, bf16[2,10,16,128]{3,2,1,0:T(8,128)(2,1)S(1)}, u32[]{:S(2)}, u32[]{:S(2)}) collective-permute-start(bf16[2,10,16,128]{3,2,1,0:T(8,128)(2,1)S(1)} %slice.3), channel_id=1, source_target_pairs={{32,0},{48,16},{64,32},{80,48},{96,64},{112,80},{128,96},{144,112}... | collective-permute-start | bytes 245768 | tf_op jit(solution)/shard_map/ppermute | solution.py:458
  50.6 4.6 %collective-permute-done.5.refs_1_ = bf16[2,10,16,128]{3,2,1,0:T(8,128)(2,1)S(1)} collective-permute-done((bf16[2,10,16,128]{3,2,1,0:T(8,128)(2,1)S(1)}, bf16[2,10,16,128]{3,2,1,0:T(8,128)(2,1)S(1)}, u32[]{:S(2)}, u32[]{:S(2)}) %collective-permute-start.5) | collective-permute-done | bytes 81952 | tf_op jit(solution)/shard_map/ppermute | solution.py:458
  55.2 1.2 %shard_map.67 = (f32[2,8,16,256]{3,2,1,0:T(8,128)S(1)}, bf16[2,8,16,256]{3,2,1,0:T(8,128)(2,1)S(1)}) custom-call(bf16[4,10,16,128]{3,2,1,0:T(8,128)(2,1)S(1)} %get-tuple-element.33.refs_0_, bf16[2,10,16,128]{3,2,1,0:T(8,128)(2,1)S(1)} %collective-permute-done.5.refs_1_, bf16[64,3456]{1,0:T(8,128)(2,1)S(1)} %get-tuple-element.34.refs_2_), custom_call_target="tpu_custom_call" | custom-call | flops 603979776 | bytes 1081344 | tf_op jit(solution)/shard_map/pallas_call | solution.py:76
  56.4 4.6 %collective-permute-start.6 = (bf16[2,8,16,256]{3,2,1,0:T(8,128)(2,1)S(1)}, bf16[2,8,16,256]{3,2,1,0:T(8,128)(2,1)S(1)}, u32[]{:S(2)}, u32[]{:S(2)}) collective-permute-start(bf16[2,8,16,256]{3,2,1,0:T(8,128)(2,1)S(1)} %get-tuple-element.36.refs_1_), channel_id=1, source_target_pairs={{0,16},{16,0},{32,48},{48,32},{64,80},{80,64},{96,112},{112,96},{1... | collective-permute-start | bytes 393224 | tf_op jit(solution)/shard_map/ppermute | solution.py:480
  61.0 0.0 all-to-all-done.1.refs_0_
  61.0 1.0 %shard_map.69 = bf16[16,16,128]{2,1,0:T(8,128)(2,1)} custom-call(bf16[16,7,16,128]{3,2,1,0:T(8,128)(2,1)S(1)} %all-to-all-done.1.refs_0_, bf16[2,8,16,256]{3,2,1,0:T(8,128)(2,1)S(1)} %get-tuple-element.36.refs_1_), custom_call_target="tpu_custom_call" | custom-call | bytes 655360 | tf_op jit(solution)/shard_map/pallas_call | solution.py:76
  62.0 18.1 %all-to-all-start.2 = ((bf16[16,16,128]{2,1,0:T(8,128)(2,1)}), bf16[16,16,128]{2,1,0:T(8,128)(2,1)S(1)}, u32[]{:S(2)}, u32[]{:S(2)}) async-start(bf16[16,16,128]{2,1,0:T(8,128)(2,1)} %shard_map.69), calls=%async_computation.2 | async-start | bytes 131072 | tf_op jit(solution)/shard_map/all_to_all | solution.py:479
  80.1 0.0 collective-permute-done.6.refs_1_
  80.2 0.2 shard_map.68
  80.4 4.3 %collective-permute-start.7 = (f32[2,4,16,256]{3,2,1,0:T(8,128)S(1)}, f32[2,4,16,256]{3,2,1,0:T(8,128)S(1)}, u32[]{:S(2)}, u32[]{:S(2)}) collective-permute-start(f32[2,4,16,256]{3,2,1,0:T(8,128)S(1)} %get-tuple-element.38), channel_id=1, source_target_pairs={{0,1},{1,0},{2,3},{3,2},{4,5},{5,4},{6,7},{7,6},{8,9},{9,8},{10,11... | collective-permute-start | bytes 393224 | tf_op jit(solution)/shard_map/ppermute | solution.py:487
  84.7 0.0 all-to-all-done.2.refs_0_
  84.7 0.8 shard_map.70
  85.5 0.1 collective-permute-done.7.refs_1_
  85.7 1.0 %shard_map.71 = bf16[2,4,32,128]{3,2,1,0:T(8,128)(2,1)} custom-call(f32[2,4,16,256]{3,2,1,0:T(8,128)S(1)} %get-tuple-element.37.refs_0_, f32[2,4,16,256]{3,2,1,0:T(8,128)S(1)} %collective-permute-done.7.refs_1_, f32[8,128]{1,0:T(8,128)S(1)} %get-tuple-element.40.refs_2_), custom_call_target="tpu_custom_call" | custom-call | bytes 331776 | tf_op jit(solution)/shard_map/pallas_call | solution.py:76
  (1 shorter events, 0.0 us)
Async XLA Ops:
  0.6 0.8 copy-start.2
  1.5 0.7 copy-start.3
  2.3 7.1 %collective-permute-start = (bf16[5,32,128]{2,1,0:T(8,128)(2,1)S(1)}, bf16[5,32,128]{2,1,0:T(8,128)(2,1)S(1)}, u32[]{:S(2)}, u32[]{:S(2)}) collective-permute-start(bf16[5,32,128]{2,1,0:T(8,128)(2,1)S(1)} %get-tuple-element.23), channel_id=1, source_target_pairs={{1,2},{2,1},{3,4},{4,3},{5,6},{6,5},{7,8},{8,7},{9,10},{10,9},{11,... | collective-permute-start | bytes 122888 | tf_op jit(solution)/shard_map/ppermute | solution.py:383
  6.9 0.9 %copy-start.1 = (bf16[3,3,3,256,16]{3,4,2,1,0:T(8,128)(2,1)S(1)}, bf16[3,3,3,256,16]{3,4,2,1,0:T(8,128)(2,1)}, u32[]{:S(2)}) copy-start(bf16[3,3,3,256,16]{3,4,2,1,0:T(8,128)(2,1)} %param.6) | copy-start | bytes 663556
  9.6 7.5 %collective-permute-start.1 = (bf16[15,32,128]{2,1,0:T(8,128)(2,1)S(1)}, bf16[15,32,128]{2,1,0:T(8,128)(2,1)S(1)}, u32[]{:S(2)}, u32[]{:S(2)}) collective-permute-start(bf16[15,32,128]{2,1,0:T(8,128)(2,1)S(1)} %get-tuple-element.24.refs_0_), channel_id=1, source_target_pairs={{0,16},{16,0},{32,48},{48,32},{64,80},{80,64},{96,112},{112,96},{1... | collective-permute-start | bytes 368648 | tf_op jit(solution)/shard_map/ppermute | solution.py:402
  17.3 18.9 %copy-start = (bf16[3,3,3,128,256]{4,3,2,1,0:T(8,128)(2,1)S(1)}, bf16[3,3,3,128,256]{4,3,2,1,0:T(8,128)(2,1)}, u32[]{:S(2)}) copy-start(bf16[3,3,3,128,256]{4,3,2,1,0:T(8,128)(2,1)} %param.5) | copy-start | bytes 5308420
  17.3 22.6 %all-to-all-start = ((bf16[16,16,1728]{2,1,0:T(8,128)(2,1)}), bf16[16,16,1728]{2,1,0:T(8,128)(2,1)S(1)}, u32[]{:S(2)}, u32[]{:S(2)}) async-start(bf16[16,16,1728]{2,1,0:T(8,128)(2,1)} %get-tuple-element.26), calls=%async_computation | async-start | bytes 1835008 | tf_op jit(solution)/shard_map/all_to_all | solution.py:411
  24.6 8.2 %collective-permute-start.2 = (bf16[12,32,128]{2,1,0:T(8,128)(2,1)S(1)}, bf16[12,32,128]{2,1,0:T(8,128)(2,1)S(1)}, u32[]{:S(2)}, u32[]{:S(2)}) collective-permute-start(bf16[12,32,128]{2,1,0:T(8,128)(2,1)S(1)} %get-tuple-element.27), channel_id=1, source_target_pairs={{0,32},{16,48},{32,64},{48,80},{64,96},{80,112},{96,128},{112,144}... | collective-permute-start | bytes 294920 | tf_op jit(solution)/shard_map/ppermute | solution.py:414
  27.8 5.0 %collective-permute-start.3 = (bf16[3,32,128]{2,1,0:T(8,128)(2,1)S(1)}, bf16[3,32,128]{2,1,0:T(8,128)(2,1)S(1)}, u32[]{:S(2)}, u32[]{:S(2)}) collective-permute-start(bf16[3,32,128]{2,1,0:T(8,128)(2,1)S(1)} %get-tuple-element.28), channel_id=1, source_target_pairs={{32,0},{48,16},{64,32},{80,48},{96,64},{112,80},{128,96},{144,112}... | collective-permute-start | bytes 73736 | tf_op jit(solution)/shard_map/ppermute | solution.py:415
  33.2 4.5 %collective-permute-start.4 = (bf16[45,32,128]{2,1,0:T(8,128)(2,1)S(1)}, bf16[45,32,128]{2,1,0:T(8,128)(2,1)S(1)}, u32[]{:S(2)}, u32[]{:S(2)}) collective-permute-start(bf16[45,32,128]{2,1,0:T(8,128)(2,1)S(1)} %shard_map.63.refs_0_), channel_id=1, source_target_pairs={{0,1},{1,0},{2,3},{3,2},{4,5},{5,4},{6,7},{7,6},{8,9},{9,8},{10,11... | collective-permute-start | bytes 1105928 | tf_op jit(solution)/shard_map/ppermute | solution.py:429
  42.6 18.4 %all-to-all-start.1 = ((bf16[16,7,16,128]{3,2,1,0:T(8,128)(2,1)}), bf16[16,7,16,128]{3,2,1,0:T(8,128)(2,1)S(1)}, u32[]{:S(2)}, u32[]{:S(2)}) async-start(bf16[16,7,16,128]{3,2,1,0:T(8,128)(2,1)} %get-tuple-element.39), calls=%async_computation.1 | async-start | bytes 917504 | tf_op jit(solution)/shard_map/all_to_all | solution.py:457
  49.3 5.9 %collective-permute-start.5 = (bf16[2,10,16,128]{3,2,1,0:T(8,128)(2,1)S(1)}, bf16[2,10,16,128]{3,2,1,0:T(8,128)(2,1)S(1)}, u32[]{:S(2)}, u32[]{:S(2)}) collective-permute-start(bf16[2,10,16,128]{3,2,1,0:T(8,128)(2,1)S(1)} %slice.3), channel_id=1, source_target_pairs={{32,0},{48,16},{64,32},{80,48},{96,64},{112,80},{128,96},{144,112}... | collective-permute-start | bytes 245768 | tf_op jit(solution)/shard_map/ppermute | solution.py:458
  56.4 23.7 %collective-permute-start.6 = (bf16[2,8,16,256]{3,2,1,0:T(8,128)(2,1)S(1)}, bf16[2,8,16,256]{3,2,1,0:T(8,128)(2,1)S(1)}, u32[]{:S(2)}, u32[]{:S(2)}) collective-permute-start(bf16[2,8,16,256]{3,2,1,0:T(8,128)(2,1)S(1)} %get-tuple-element.36.refs_1_), channel_id=1, source_target_pairs={{0,16},{16,0},{32,48},{48,32},{64,80},{80,64},{96,112},{112,96},{1... | collective-permute-start | bytes 393224 | tf_op jit(solution)/shard_map/ppermute | solution.py:480
  62.0 22.7 %all-to-all-start.2 = ((bf16[16,16,128]{2,1,0:T(8,128)(2,1)}), bf16[16,16,128]{2,1,0:T(8,128)(2,1)S(1)}, u32[]{:S(2)}, u32[]{:S(2)}) async-start(bf16[16,16,128]{2,1,0:T(8,128)(2,1)} %shard_map.69), calls=%async_computation.2 | async-start | bytes 131072 | tf_op jit(solution)/shard_map/all_to_all | solution.py:479
  80.4 5.3 %collective-permute-start.7 = (f32[2,4,16,256]{3,2,1,0:T(8,128)S(1)}, f32[2,4,16,256]{3,2,1,0:T(8,128)S(1)}, u32[]{:S(2)}, u32[]{:S(2)}) collective-permute-start(f32[2,4,16,256]{3,2,1,0:T(8,128)S(1)} %get-tuple-element.38), channel_id=1, source_target_pairs={{0,1},{1,0},{2,3},{3,2},{4,5},{5,4},{6,7},{7,6},{8,9},{9,8},{10,11... | collective-permute-start | bytes 393224 | tf_op jit(solution)/shard_map/ppermute | solution.py:487

commit v6 on v5

--- a/solution.py
+++ b/solution.py
@@ -48,38 +48,17 @@
     return jnp.where(column_of(row) == col, 1.0, 0.0).astype(BF16)
 
 
-def call(kernel, out, args, scratch=(), fetch=(), idle=(), alias=None, flops=0, limit=16):
-    n_in, n_out, n_scratch = len(args), len(out), len(scratch)
-
-    def run(*refs):
-        ins, outs = list(refs[:n_in]), refs[n_in : n_in + n_out]
-        rest = refs[n_in + n_out :]
-        if fetch:
-            landing, sems = rest[n_scratch:-1], rest[-1]
-            copies = [
-                pltpu.make_async_copy(ins[i], landing[k], sems.at[k]) for k, i in enumerate(fetch)
-            ]
-            for copy in copies:
-                copy.start()
-            for copy in copies:
-                copy.wait()
-            for k, i in enumerate(fetch):
-                ins[i] = landing[k]
-        kernel(*ins, *outs, *rest[:n_scratch])
-
+def call(kernel, out, args, scratch=(), idle=(), alias=None, flops=0, limit=16):
     spec = pl.BlockSpec(memory_space=pltpu.VMEM)
     far = pl.BlockSpec(memory_space=pl.ANY)
     moved = sum(x.size * x.dtype.itemsize for x in list(args) + list(out))
-    extra = [pltpu.VMEM(args[i].shape, args[i].dtype) for i in fetch]
-    if fetch:
-        extra.append(pltpu.SemaphoreType.DMA((len(fetch),)))
     return pl.pallas_call(
-        run,
+        kernel,
         out_shape=tuple(out),
-        in_specs=[far if i in fetch or i in idle else spec for i in range(n_in)],
-        out_specs=tuple([far if i in (alias or {}).values() else spec for i in range(n_out)]),
+        in_specs=[far if i in idle else spec for i in range(len(args))],
+        out_specs=tuple([far if i in (alias or {}).values() else spec for i in range(len(out))]),
         input_output_aliases=dict(alias or {}),
-        scratch_shapes=list(scratch) + extra,
+        scratch_shapes=list(scratch),
         compiler_params=pltpu.CompilerParams(vmem_limit_bytes=limit * 1024 * 1024),
         cost_estimate=pl.CostEstimate(flops=flops, bytes_accessed=moved, transcendentals=0),
     )(*args)
@@ -302,7 +281,7 @@
         out[i] = jnp.concatenate(block, 0).astype(BF16)
 
 
-def finish_kernel(scale, parts, out, mark):
+def finish_kernel(scale, parts, _, out):
     total = parts[0].astype(F32)
     for i in range(1, parts.shape[0]):
         total = total + parts[i].astype(F32)
@@ -311,7 +290,6 @@
         lanes = slice(8 * (k // 2), 8 * (k // 2) + 8)
         rows = [8 * x + 4 * (k % 2) for x in range(2)]
         out[k] = jnp.concatenate([total[r : r + 4, lanes] for r in rows], 1)
-    mark[...] = jnp.zeros_like(mark)
 
 
 def clip_kernel(grad, following, flat, keep, send, wide, filters):
@@ -353,12 +331,13 @@
     send[...] = jnp.where(even, total[:, 4:], total[:, :4])
 
 
-def join_kernel(kept, got, _, out):
+def join_kernel(kept, got, out, mark):
     total = (kept[...] + got[...]).astype(BF16).reshape(128, 256)
     low = one_hot(256, 128, lambda r: jnp.where(r % 2 == 0, (r // 32) * 16 + (r % 32) // 2, -1))
     high = one_hot(256, 128, lambda r: jnp.where(r % 2 == 1, (r // 32) * 16 + (r % 32) // 2, -1))
     moved = mm(low, total[:, :128]) + mm(high, total[:, 128:])
     out[...] = moved.astype(BF16).reshape(out.shape)
+    mark[...] = jnp.zeros_like(mark)
 
 
 def inside(pairs, count):
@@ -377,7 +356,6 @@
         stack_kernel,
         [shaped((10, 32, 128), BF16), shaped((5, 32, 128), BF16)],
         [clip, upstream],
-        fetch=(0, 1),
     )
     near_pairs = inside([(i, i + 1 if i % 2 else i - 1) for i in range(heights)], heights)
     edge = lax.ppermute(edge, "height", near_pairs)
@@ -387,7 +365,6 @@
         filter_pieces_kernel,
         [shaped((heights, chans // heights, 27 * OWN), BF16)],
         [second],
-        fetch=(0,),
         flops=2 * 27 * 16 * 256 * 128,
     )
 
@@ -404,7 +381,6 @@
         choose_kernel,
         [shaped((12, 32, 128), BF16), shaped((3, 32, 128), BF16), shaped(pieces.shape, BF16)],
         [here, pair, pieces],
-        fetch=(1,),
         idle=(2,),
         alias={2: 2},
     )
@@ -419,12 +395,11 @@
         own_filter_kernel,
         [shaped((3, 512, 6 * OWN), BF16), shaped((OWN, 27 * cin), BF16)],
         [first],
-        fetch=(0,),
         flops=3 * 27 * 128 * 256 * 128,
     )
 
     (packed,) = call(
-        pack_kernel, [shaped((45, 32, 128), BF16)], [here, pair, before, after], fetch=(1, 2, 3)
+        pack_kernel, [shaped((45, 32, 128), BF16)], [here, pair, before, after]
     )
     other = lax.ppermute(packed, "height", siblings)
 
@@ -438,14 +413,12 @@
         ],
         [packed, other, band],
         scratch=[pltpu.VMEM((units, 32, 128), BF16), pltpu.VMEM((up_units, 16, 256), BF16)],
-        fetch=(1,),
         flops=2 * 640 * 9 * 512 * 128,
     )
     grad_pre, parts = call(
         gradient_kernel,
         [shaped((FRAMES, SPAN, 16, 2 * OWN), BF16), shaped((heights, 7, 16, cin), BF16)],
         [second, ups, pre, wide],
-        fetch=(0,),
         flops=2 * 512 * 9 * 512 * 128,
     )
 
@@ -464,7 +437,6 @@
             pltpu.VMEM(((FRAMES + 2) * SPAN, 16, 4 * OWN), BF16),
             pltpu.VMEM((9, 4 * OWN, 2 * cin), BF16),
         ],
-        fetch=(1,),
         flops=2 * 512 * 9 * 256 * 256,
     )
 
@@ -472,7 +444,6 @@
         sum_turn_kernel,
         [shaped((lines, 16, 128), BF16)],
         [parts, send],
-        fetch=(0,),
         idle=(1,),
     )
     columns = [[2 * ((i + 8) % lines) + x for i in range(lines)] for x in range(2)]
@@ -482,22 +453,17 @@
         halve_kernel,
         [shaped((2, rows, 16, 2 * cin), F32)] * 2,
         [keep, got],
-        fetch=(1,),
     )
     got = lax.ppermute(send, "height", siblings)
+    grad_clip, mark = call(
+        join_kernel, [shaped(clip.shape, BF16), shaped((8, 128), F32)], [keep, got]
+    )
     count = frames * tms * rows * heights * width
-    grad_filter, mark = call(
+    (grad_filter,) = call(
         functools.partial(finish_kernel, 1.0 / float(count) ** 0.5),
-        [shaped((27, cin // tms, chans // heights), F32), shaped((8, 128), F32)],
-        [summed],
-        fetch=(0,),
-    )
-    (grad_clip,) = call(
-        join_kernel,
-        [shaped(clip.shape, BF16)],
-        [keep, got, mark],
-        fetch=(1,),
-        idle=(2,),
+        [shaped((27, cin // tms, chans // heights), F32)],
+        [summed, mark],
+        idle=(1,),
     )
     grad_filter = grad_filter.reshape(3, 3, 3, cin // tms, chans // heights)
     return (grad_clip, grad_filter)

time: 87.3 us -> 86 us (0.985)
  Pallas kernels: 13 us -> 10.6 us
    pallas_call x13, Pallas kernels: 13 us -> 10.6 us  [call(): pl.pallas_call(kernel, out_shape=tuple(out), in_specs=[far if i in idle e...]
  transfers between devices with their start and end apart: 11 -> 11, of which waited for: 4 -> 5; matrix products, arithmetic and copies ran while one was open for 0% -> 0% of each run, Pallas kernels for 10% -> 9%
where the time goes in v6:
time: 86 us; the launch traced here: 85.4 us
  starting transfers between devices  59.4 us (69%)
  waiting for transfers between devices  12.1 us (14%)
  Pallas kernels  10.6 us (12%)
  local copies, waits for them, and re-layouts  2.49 us (3%)
    all_to_all x1, starting transfers between devices, body(): summed = lax.all_to_all(sums, 'tm', 0, 0, axis_index_groups=columns)  18.1 us
    pallas_call x13, Pallas kernels, call(): pl.pallas_call(kernel, out_shape=tuple(out), in_specs=[far if i in idle e...  10.6 us
    all_to_all x1, starting transfers between devices, body(): second = lax.all_to_all(pieces, 'height', 0, 0).reshape(chans, 27 * OWN)  7.31 us
    all_to_all x1, starting transfers between devices, body(): lax.all_to_all(parts, ('tm', 'height'), 0, 0, axis_index_groups=planes)  6.69 us
    ppermute x1, starting transfers between devices, body(): got = lax.ppermute(send, 'tm', blocks)  4.78 us
    ppermute x1, starting transfers between devices, body(): pair = lax.ppermute(here, 'tm', blocks)  4.66 us
    ppermute x1, starting transfers between devices, body(): edge = lax.ppermute(edge, 'height', near_pairs)  4.59 us
    ppermute x1, starting transfers between devices, body(): got = lax.ppermute(send, 'height', siblings)  4.53 us
  transfers between devices with their start and end apart: 11, of which 5 were waited for; matrix products, arithmetic and copies ran while one was open for 0% of the time, Pallas kernels for 9%

profile of v6, /device:TPU:1, one launch (start us, length us, event | category | flops | bytes accessed | tf_op | source)
XLA Modules:
  0.0 85.4 jit_solution(416498175090213673)
XLA Ops:
  0.6 0.0 copy-start.2
  0.6 0.8 copy-done.2
  1.5 0.0 copy-start.3
  1.5 0.7 copy-done.3
  2.2 4.6 %collective-permute-start = (bf16[5,32,128]{2,1,0:T(8,128)(2,1)S(1)}, bf16[5,32,128]{2,1,0:T(8,128)(2,1)S(1)}, u32[]{:S(2)}, u32[]{:S(2)}) collective-permute-start(bf16[5,32,128]{2,1,0:T(8,128)(2,1)S(1)} %get-tuple-element.23), channel_id=1, source_target_pairs={{1,2},{2,1},{3,4},{4,3},{5,6},{6,5},{7,8},{8,7},{9,10},{10,9},{11,... | collective-permute-start | bytes 122888 | tf_op jit(solution)/shard_map/ppermute | solution.py:361
  6.8 0.0 copy-start.1
  6.8 0.9 %copy-done.1 = bf16[3,3,3,256,16]{3,4,2,1,0:T(8,128)(2,1)S(1)} copy-done((bf16[3,3,3,256,16]{3,4,2,1,0:T(8,128)(2,1)S(1)}, bf16[3,3,3,256,16]{3,4,2,1,0:T(8,128)(2,1)}, u32[]{:S(2)}) %copy-start.1) | copy-done | bytes 221208
  7.8 1.3 %shard_map.60._ = bf16[16,16,1728]{2,1,0:T(8,128)(2,1)} custom-call(bf16[27,16,256]{2,1,0:T(8,128)(2,1)S(1)} %bitcast.8), custom_call_target="tpu_custom_call" | custom-call | flops 28311552 | bytes 1105920 | tf_op jit(solution)/shard_map/pallas_call | solution.py:55
  9.1 0.0 collective-permute-done.edge
  9.1 0.2 shard_map.61
  9.2 4.7 %collective-permute-start.1 = (bf16[15,32,128]{2,1,0:T(8,128)(2,1)S(1)}, bf16[15,32,128]{2,1,0:T(8,128)(2,1)S(1)}, u32[]{:S(2)}, u32[]{:S(2)}) collective-permute-start(bf16[15,32,128]{2,1,0:T(8,128)(2,1)S(1)} %get-tuple-element.24.here), channel_id=1, source_target_pairs={{0,16},{16,0},{32,48},{48,32},{64,80},{80,64},{96,112},{112,96},{1... | collective-permute-start | bytes 368648 | tf_op jit(solution)/shard_map/ppermute | solution.py:379
  13.9 2.8 %collective-permute-done.1.pair = bf16[15,32,128]{2,1,0:T(8,128)(2,1)S(1)} collective-permute-done((bf16[15,32,128]{2,1,0:T(8,128)(2,1)S(1)}, bf16[15,32,128]{2,1,0:T(8,128)(2,1)S(1)}, u32[]{:S(2)}, u32[]{:S(2)}) %collective-permute-start.1) | collective-permute-done | bytes 122912 | tf_op jit(solution)/shard_map/ppermute | solution.py:379
  16.8 0.0 copy-start
  16.8 7.3 %all-to-all-start = ((bf16[16,16,1728]{2,1,0:T(8,128)(2,1)}), bf16[16,16,1728]{2,1,0:T(8,128)(2,1)S(1)}, u32[]{:S(2)}, u32[]{:S(2)}) async-start(bf16[16,16,1728]{2,1,0:T(8,128)(2,1)} %get-tuple-element.26), calls=%async_computation | async-start | bytes 1835008 | tf_op jit(solution)/shard_map/all_to_all | solution.py:387
  24.1 3.2 %collective-permute-start.2 = (bf16[12,32,128]{2,1,0:T(8,128)(2,1)S(1)}, bf16[12,32,128]{2,1,0:T(8,128)(2,1)S(1)}, u32[]{:S(2)}, u32[]{:S(2)}) collective-permute-start(bf16[12,32,128]{2,1,0:T(8,128)(2,1)S(1)} %get-tuple-element.27), channel_id=1, source_target_pairs={{0,32},{16,48},{32,64},{48,80},{64,96},{80,112},{96,128},{112,144}... | collective-permute-start | bytes 294920 | tf_op jit(solution)/shard_map/ppermute | solution.py:390
  27.3 1.3 %collective-permute-start.3 = (bf16[3,32,128]{2,1,0:T(8,128)(2,1)S(1)}, bf16[3,32,128]{2,1,0:T(8,128)(2,1)S(1)}, u32[]{:S(2)}, u32[]{:S(2)}) collective-permute-start(bf16[3,32,128]{2,1,0:T(8,128)(2,1)S(1)} %get-tuple-element.28), channel_id=1, source_target_pairs={{32,0},{48,16},{64,32},{80,48},{96,64},{112,80},{128,96},{144,112}... | collective-permute-start | bytes 73736 | tf_op jit(solution)/shard_map/ppermute | solution.py:391
  28.6 3.7 %collective-permute-done.3.after = bf16[3,32,128]{2,1,0:T(8,128)(2,1)S(1)} collective-permute-done((bf16[3,32,128]{2,1,0:T(8,128)(2,1)S(1)}, bf16[3,32,128]{2,1,0:T(8,128)(2,1)S(1)}, u32[]{:S(2)}, u32[]{:S(2)}) %collective-permute-start.3) | collective-permute-done | bytes 24608 | tf_op jit(solution)/shard_map/ppermute | solution.py:391
  32.3 0.0 collective-permute-done.2.before
  32.3 0.1 shard_map.63.own
  32.4 2.9 %collective-permute-start.4 = (bf16[45,32,128]{2,1,0:T(8,128)(2,1)S(1)}, bf16[45,32,128]{2,1,0:T(8,128)(2,1)S(1)}, u32[]{:S(2)}, u32[]{:S(2)}) collective-permute-start(bf16[45,32,128]{2,1,0:T(8,128)(2,1)S(1)} %shard_map.63.own), channel_id=1, source_target_pairs={{0,1},{1,0},{2,3},{3,2},{4,5},{5,4},{6,7},{7,6},{8,9},{9,8},{10,11... | collective-permute-start | bytes 1105928 | tf_op jit(solution)/shard_map/ppermute | solution.py:404
  35.3 0.0 copy-done
  35.3 1.1 %shard_map.64 = (bf16[3,512,384]{2,1,0:T(8,128)(2,1)S(1)}, bf16[64,3456]{1,0:T(8,128)(2,1)S(1)}) custom-call(bf16[3456,256]{1,0:T(8,128)(2,1)S(1)} %bitcast.7), custom_call_target="tpu_custom_call" | custom-call | flops 339738624 | bytes 3391488 | tf_op jit(solution)/shard_map/pallas_call | solution.py:55
  36.5 0.1 collective-permute-done.4.other
  36.6 2.0 %shard_map.65 = (bf16[72,16,512]{2,1,0:T(8,128)(2,1)S(1)}, bf16[2,18,16,256]{3,2,1,0:T(8,128)(2,1)S(1)}, f32[2,2,2,5,16,128]{5,4,3,2,1,0:T(8,128)S(1)}) custom-call(bf16[45,32,128]{2,1,0:T(8,128)(2,1)S(1)} %shard_map.63.own, bf16[45,32,128]{2,1,0:T(8,128)(2,1)S(1)} %collective-permute-done.4.other, bf16[3,512,384]{2,1,0:T(8,128)(2,1)S(1)} %get-tuple-element.29.filters), custom_call_target="tpu_custom_call" | custom-call | flops 754974720 | bytes 3719168 | tf_op jit(solution)/shard_map/pallas_call | solution.py:55
  38.7 0.0 all-to-all-done
  38.7 2.4 %shard_map.66 = (bf16[4,10,16,128]{3,2,1,0:T(8,128)(2,1)S(1)}, bf16[16,7,16,128]{3,2,1,0:T(8,128)(2,1)}) custom-call(bf16[256,1728]{1,0:T(8,128)(2,1)S(1)} %bitcast.6, bf16[2,18,16,256]{3,2,1,0:T(8,128)(2,1)S(1)} %get-tuple-element.30.ups, f32[2,2,2,5,16,128]{5,4,3,2,1,0:T(8,128)S(1)} %get-tuple-element.31.pre, bf16[72,16,512]{2,1,0:T(8,128)(2,1)S(1)} %get-tuple-element.32.wide), custom_call_target="tpu_custom_call" | custom-call | flops 603979776 | bytes 3309568 | tf_op jit(solution)/shard_map/pallas_call | solution.py:55
  41.1 6.7 %all-to-all-start.1 = ((bf16[16,7,16,128]{3,2,1,0:T(8,128)(2,1)}), bf16[16,7,16,128]{3,2,1,0:T(8,128)(2,1)S(1)}, u32[]{:S(2)}, u32[]{:S(2)}) async-start(bf16[16,7,16,128]{3,2,1,0:T(8,128)(2,1)} %get-tuple-element.40), calls=%async_computation.1 | async-start | bytes 917504 | tf_op jit(solution)/shard_map/all_to_all | solution.py:430
  47.8 1.3 %collective-permute-start.5 = (bf16[2,10,16,128]{3,2,1,0:T(8,128)(2,1)S(1)}, bf16[2,10,16,128]{3,2,1,0:T(8,128)(2,1)S(1)}, u32[]{:S(2)}, u32[]{:S(2)}) collective-permute-start(bf16[2,10,16,128]{3,2,1,0:T(8,128)(2,1)S(1)} %slice.3), channel_id=1, source_target_pairs={{32,0},{48,16},{64,32},{80,48},{96,64},{112,80},{128,96},{144,112}... | collective-permute-start | bytes 245768 | tf_op jit(solution)/shard_map/ppermute | solution.py:431
  49.1 4.4 %collective-permute-done.5.following = bf16[2,10,16,128]{3,2,1,0:T(8,128)(2,1)S(1)} collective-permute-done((bf16[2,10,16,128]{3,2,1,0:T(8,128)(2,1)S(1)}, bf16[2,10,16,128]{3,2,1,0:T(8,128)(2,1)S(1)}, u32[]{:S(2)}, u32[]{:S(2)}) %collective-permute-start.5) | collective-permute-done | bytes 81952 | tf_op jit(solution)/shard_map/ppermute | solution.py:431
  53.4 1.1 %shard_map.67 = (f32[2,8,16,256]{3,2,1,0:T(8,128)S(1)}, bf16[2,8,16,256]{3,2,1,0:T(8,128)(2,1)S(1)}) custom-call(bf16[4,10,16,128]{3,2,1,0:T(8,128)(2,1)S(1)} %get-tuple-element.33.grad, bf16[2,10,16,128]{3,2,1,0:T(8,128)(2,1)S(1)} %collective-permute-done.5.following, bf16[64,3456]{1,0:T(8,128)(2,1)S(1)} %get-tuple-element.34.flat), custom_call_target="tpu_custom_call" | custom-call | flops 603979776 | bytes 1081344 | tf_op jit(solution)/shard_map/pallas_call | solution.py:55
  54.6 4.8 %collective-permute-start.6 = (bf16[2,8,16,256]{3,2,1,0:T(8,128)(2,1)S(1)}, bf16[2,8,16,256]{3,2,1,0:T(8,128)(2,1)S(1)}, u32[]{:S(2)}, u32[]{:S(2)}) collective-permute-start(bf16[2,8,16,256]{3,2,1,0:T(8,128)(2,1)S(1)} %get-tuple-element.36._), channel_id=1, source_target_pairs={{0,16},{16,0},{32,48},{48,32},{64,80},{80,64},{96,112},{112,96},{1... | collective-permute-start | bytes 393224 | tf_op jit(solution)/shard_map/ppermute | solution.py:451
  59.3 0.0 all-to-all-done.1.parts
  59.4 0.8 shard_map.70
  60.1 18.1 %all-to-all-start.2 = ((bf16[16,16,128]{2,1,0:T(8,128)(2,1)}), bf16[16,16,128]{2,1,0:T(8,128)(2,1)S(1)}, u32[]{:S(2)}, u32[]{:S(2)}) async-start(bf16[16,16,128]{2,1,0:T(8,128)(2,1)} %shard_map.70), calls=%async_computation.2 | async-start | bytes 131072 | tf_op jit(solution)/shard_map/all_to_all | solution.py:450
  78.2 0.0 collective-permute-done.6.got
  78.3 4.5 %collective-permute-start.7 = (f32[2,4,16,256]{3,2,1,0:T(8,128)S(1)}, f32[2,4,16,256]{3,2,1,0:T(8,128)S(1)}, u32[]{:S(2)}, u32[]{:S(2)}) collective-permute-start(f32[2,4,16,256]{3,2,1,0:T(8,128)S(1)} %get-tuple-element.38), channel_id=1, source_target_pairs={{0,1},{1,0},{2,3},{3,2},{4,5},{5,4},{6,7},{7,6},{8,9},{9,8},{10,11... | collective-permute-start | bytes 393224 | tf_op jit(solution)/shard_map/ppermute | solution.py:457
  82.8 1.0 %collective-permute-done.7.got = f32[2,4,16,256]{3,2,1,0:T(8,128)S(1)} collective-permute-done((f32[2,4,16,256]{3,2,1,0:T(8,128)S(1)}, f32[2,4,16,256]{3,2,1,0:T(8,128)S(1)}, u32[]{:S(2)}, u32[]{:S(2)}) %collective-permute-start.7) | collective-permute-done | bytes 131104 | tf_op jit(solution)/shard_map/ppermute | solution.py:457
  83.8 0.8 shard_map.69
  84.6 0.0 all-to-all-done.2.parts
  84.6 0.7 shard_map.71
  (4 shorter events, 0.1 us)
Async XLA Ops:
  0.6 0.8 copy-start.2
  1.5 0.7 copy-start.3
  2.2 6.8 %collective-permute-start = (bf16[5,32,128]{2,1,0:T(8,128)(2,1)S(1)}, bf16[5,32,128]{2,1,0:T(8,128)(2,1)S(1)}, u32[]{:S(2)}, u32[]{:S(2)}) collective-permute-start(bf16[5,32,128]{2,1,0:T(8,128)(2,1)S(1)} %get-tuple-element.23), channel_id=1, source_target_pairs={{1,2},{2,1},{3,4},{4,3},{5,6},{6,5},{7,8},{8,7},{9,10},{10,9},{11,... | collective-permute-start | bytes 122888 | tf_op jit(solution)/shard_map/ppermute | solution.py:361
  6.8 0.9 %copy-start.1 = (bf16[3,3,3,256,16]{3,4,2,1,0:T(8,128)(2,1)S(1)}, bf16[3,3,3,256,16]{3,4,2,1,0:T(8,128)(2,1)}, u32[]{:S(2)}) copy-start(bf16[3,3,3,256,16]{3,4,2,1,0:T(8,128)(2,1)} %param.6) | copy-start | bytes 663556
  9.2 7.5 %collective-permute-start.1 = (bf16[15,32,128]{2,1,0:T(8,128)(2,1)S(1)}, bf16[15,32,128]{2,1,0:T(8,128)(2,1)S(1)}, u32[]{:S(2)}, u32[]{:S(2)}) collective-permute-start(bf16[15,32,128]{2,1,0:T(8,128)(2,1)S(1)} %get-tuple-element.24.here), channel_id=1, source_target_pairs={{0,16},{16,0},{32,48},{48,32},{64,80},{80,64},{96,112},{112,96},{1... | collective-permute-start | bytes 368648 | tf_op jit(solution)/shard_map/ppermute | solution.py:379
  16.8 18.6 %copy-start = (bf16[3,3,3,128,256]{4,3,2,1,0:T(8,128)(2,1)S(1)}, bf16[3,3,3,128,256]{4,3,2,1,0:T(8,128)(2,1)}, u32[]{:S(2)}) copy-start(bf16[3,3,3,128,256]{4,3,2,1,0:T(8,128)(2,1)} %param.5) | copy-start | bytes 5308420
  16.8 21.9 %all-to-all-start = ((bf16[16,16,1728]{2,1,0:T(8,128)(2,1)}), bf16[16,16,1728]{2,1,0:T(8,128)(2,1)S(1)}, u32[]{:S(2)}, u32[]{:S(2)}) async-start(bf16[16,16,1728]{2,1,0:T(8,128)(2,1)} %get-tuple-element.26), calls=%async_computation | async-start | bytes 1835008 | tf_op jit(solution)/shard_map/all_to_all | solution.py:387
  24.1 8.2 %collective-permute-start.2 = (bf16[12,32,128]{2,1,0:T(8,128)(2,1)S(1)}, bf16[12,32,128]{2,1,0:T(8,128)(2,1)S(1)}, u32[]{:S(2)}, u32[]{:S(2)}) collective-permute-start(bf16[12,32,128]{2,1,0:T(8,128)(2,1)S(1)} %get-tuple-element.27), channel_id=1, source_target_pairs={{0,32},{16,48},{32,64},{48,80},{64,96},{80,112},{96,128},{112,144}... | collective-permute-start | bytes 294920 | tf_op jit(solution)/shard_map/ppermute | solution.py:390
  27.3 5.0 %collective-permute-start.3 = (bf16[3,32,128]{2,1,0:T(8,128)(2,1)S(1)}, bf16[3,32,128]{2,1,0:T(8,128)(2,1)S(1)}, u32[]{:S(2)}, u32[]{:S(2)}) collective-permute-start(bf16[3,32,128]{2,1,0:T(8,128)(2,1)S(1)} %get-tuple-element.28), channel_id=1, source_target_pairs={{32,0},{48,16},{64,32},{80,48},{96,64},{112,80},{128,96},{144,112}... | collective-permute-start | bytes 73736 | tf_op jit(solution)/shard_map/ppermute | solution.py:391
  32.4 4.2 %collective-permute-start.4 = (bf16[45,32,128]{2,1,0:T(8,128)(2,1)S(1)}, bf16[45,32,128]{2,1,0:T(8,128)(2,1)S(1)}, u32[]{:S(2)}, u32[]{:S(2)}) collective-permute-start(bf16[45,32,128]{2,1,0:T(8,128)(2,1)S(1)} %shard_map.63.own), channel_id=1, source_target_pairs={{0,1},{1,0},{2,3},{3,2},{4,5},{5,4},{6,7},{7,6},{8,9},{9,8},{10,11... | collective-permute-start | bytes 1105928 | tf_op jit(solution)/shard_map/ppermute | solution.py:404
  41.1 18.3 %all-to-all-start.1 = ((bf16[16,7,16,128]{3,2,1,0:T(8,128)(2,1)}), bf16[16,7,16,128]{3,2,1,0:T(8,128)(2,1)S(1)}, u32[]{:S(2)}, u32[]{:S(2)}) async-start(bf16[16,7,16,128]{3,2,1,0:T(8,128)(2,1)} %get-tuple-element.40), calls=%async_computation.1 | async-start | bytes 917504 | tf_op jit(solution)/shard_map/all_to_all | solution.py:430
  47.8 5.7 %collective-permute-start.5 = (bf16[2,10,16,128]{3,2,1,0:T(8,128)(2,1)S(1)}, bf16[2,10,16,128]{3,2,1,0:T(8,128)(2,1)S(1)}, u32[]{:S(2)}, u32[]{:S(2)}) collective-permute-start(bf16[2,10,16,128]{3,2,1,0:T(8,128)(2,1)S(1)} %slice.3), channel_id=1, source_target_pairs={{32,0},{48,16},{64,32},{80,48},{96,64},{112,80},{128,96},{144,112}... | collective-permute-start | bytes 245768 | tf_op jit(solution)/shard_map/ppermute | solution.py:431
  54.6 23.7 %collective-permute-start.6 = (bf16[2,8,16,256]{3,2,1,0:T(8,128)(2,1)S(1)}, bf16[2,8,16,256]{3,2,1,0:T(8,128)(2,1)S(1)}, u32[]{:S(2)}, u32[]{:S(2)}) collective-permute-start(bf16[2,8,16,256]{3,2,1,0:T(8,128)(2,1)S(1)} %get-tuple-element.36._), channel_id=1, source_target_pairs={{0,16},{16,0},{32,48},{48,32},{64,80},{80,64},{96,112},{112,96},{1... | collective-permute-start | bytes 393224 | tf_op jit(solution)/shard_map/ppermute | solution.py:451
  60.1 24.5 %all-to-all-start.2 = ((bf16[16,16,128]{2,1,0:T(8,128)(2,1)}), bf16[16,16,128]{2,1,0:T(8,128)(2,1)S(1)}, u32[]{:S(2)}, u32[]{:S(2)}) async-start(bf16[16,16,128]{2,1,0:T(8,128)(2,1)} %shard_map.70), calls=%async_computation.2 | async-start | bytes 131072 | tf_op jit(solution)/shard_map/all_to_all | solution.py:450
  78.3 5.5 %collective-permute-start.7 = (f32[2,4,16,256]{3,2,1,0:T(8,128)S(1)}, f32[2,4,16,256]{3,2,1,0:T(8,128)S(1)}, u32[]{:S(2)}, u32[]{:S(2)}) collective-permute-start(f32[2,4,16,256]{3,2,1,0:T(8,128)S(1)} %get-tuple-element.38), channel_id=1, source_target_pairs={{0,1},{1,0},{2,3},{3,2},{4,5},{5,4},{6,7},{7,6},{8,9},{9,8},{10,11... | collective-permute-start | bytes 393224 | tf_op jit(solution)/shard_map/ppermute | solution.py:457

commit v7 on v6

--- a/solution.py
+++ b/solution.py
@@ -240,26 +240,38 @@
                     piece = jnp.where(last_band, 0.0, piece)
                 grad[2 * q + fp, r] = piece.astype(BF16)
     turned = grad[:, 1 : 1 + ROWS].reshape(FRAMES * ROWS * 16, 2 * OWN).T
+    blank = jnp.zeros((2 * OWN, 128), BF16)
+    turned = jnp.concatenate([blank, turned, blank], 1)
+    sums = {}
+    for pair in (0, 2, 4):
+        taps = [a for a in range(3) if 0 <= pair - a + 1 <= FRAMES]
+        lhs = [turned[:, (pair - a + 1) * 128 : (pair - a + 3) * 128] for a in taps]
+        lhs = jnp.concatenate(lhs, 0)
+        for b in range(3):
+            tops = [(pair + f) * HIGH + 1 + b for f in range(2)]
+            win = jnp.concatenate([wide[x : x + ROWS] for x in tops], 0)
+            prod = mm(lhs, win.reshape(256, 512))
+            for k, a in enumerate(taps):
+                rows = prod[k * 2 * OWN : (k + 1) * 2 * OWN]
+                sums[a, b] = sums[a, b] + rows if (a, b) in sums else rows
     strips = []
     for a in range(3):
         for b in range(3):
-            tops = [(a + f) * HIGH + 1 + b for f in range(FRAMES)]
-            win = jnp.concatenate([wide[x : x + ROWS] for x in tops], 0)
-            prod = mm(turned, win.reshape(FRAMES * ROWS * 16, 512))
             for c in range(3):
-                piece = prod[:OWN, 128 * c : 128 * c + 128]
-                piece = piece + prod[OWN:, 128 * c + 128 : 128 * c + 256]
+                piece = sums[a, b][:OWN, 128 * c : 128 * c + 128]
+                piece = piece + sums[a, b][OWN:, 128 * c + 128 : 128 * c + 256]
                 strips.append(piece.astype(BF16))
     strips.append(jnp.zeros_like(strips[0]))
     row = lax.broadcasted_iota(jnp.int32, (256, 256), 0)
     col = lax.broadcasted_iota(jnp.int32, (256, 256), 1)
     x, tap, z, e = col // 128, (col // 64) % 2, (col // 4) % 16, col % 4
     order = jnp.where(tap * 128 + 8 * z + 4 * x + e == row, 1.0, 0.0).astype(BF16)
+    pairs = [jnp.concatenate(strips[i : i + 2], 1) for i in range(0, 28, 2)]
+    moved = mm(jnp.concatenate(pairs, 0), order)
     blocks = OWN // 8
     for k in range(7):
-        pairs = [jnp.concatenate(strips[i : i + 2], 1) for i in (4 * k, 4 * k + 2)]
-        pairs = [mm(pair, order).reshape(blocks, 8, 256) for pair in pairs]
-        both = jnp.concatenate(pairs, 1).astype(BF16)
+        both = [moved[i * OWN : (i + 1) * OWN].reshape(blocks, 8, 256) for i in (2 * k, 2 * k + 1)]
+        both = jnp.concatenate(both, 1).astype(BF16)
         for x in range(2):
             parts[x * blocks : (x + 1) * blocks, k] = both[:, :, 128 * x : 128 * x + 128]
 

time: 86 us -> 86 us (level)
  no operation moved by 1% of the time
where the time goes in v7:
time: 86 us; the launch traced here: 85.3 us
  starting transfers between devices  59.4 us (69%)
  waiting for transfers between devices  12.1 us (14%)
  Pallas kernels  10.6 us (12%)
  local copies, waits for them, and re-layouts  2.49 us (3%)
    all_to_all x1, starting transfers between devices, body(): summed = lax.all_to_all(sums, 'tm', 0, 0, axis_index_groups=columns)  18.1 us
    pallas_call x13, Pallas kernels, call(): pl.pallas_call(kernel, out_shape=tuple(out), in_specs=[far if i in idle e...  10.6 us
    all_to_all x1, starting transfers between devices, body(): second = lax.all_to_all(pieces, 'height', 0, 0).reshape(chans, 27 * OWN)  7.31 us
    all_to_all x1, starting transfers between devices, body(): lax.all_to_all(parts, ('tm', 'height'), 0, 0, axis_index_groups=planes)  6.69 us
    ppermute x1, starting transfers between devices, body(): got = lax.ppermute(send, 'tm', blocks)  4.78 us
    ppermute x1, starting transfers between devices, body(): pair = lax.ppermute(here, 'tm', blocks)  4.66 us
    ppermute x1, starting transfers between devices, body(): edge = lax.ppermute(edge, 'height', near_pairs)  4.59 us
    ppermute x1, starting transfers between devices, body(): got = lax.ppermute(send, 'height', siblings)  4.53 us
  transfers between devices with their start and end apart: 11, of which 5 were waited for; matrix products, arithmetic and copies ran while one was open for 0% of the time, Pallas kernels for 9%

profile of v7, /device:TPU:1, one launch (start us, length us, event | category | flops | bytes accessed | tf_op | source)
XLA Modules:
  0.0 85.3 jit_solution(13015622908911392385)
XLA Ops:
  0.6 0.0 copy-start.2
  0.6 0.8 copy-done.2
  1.5 0.0 copy-start.3
  1.5 0.7 copy-done.3
  2.2 4.6 %collective-permute-start = (bf16[5,32,128]{2,1,0:T(8,128)(2,1)S(1)}, bf16[5,32,128]{2,1,0:T(8,128)(2,1)S(1)}, u32[]{:S(2)}, u32[]{:S(2)}) collective-permute-start(bf16[5,32,128]{2,1,0:T(8,128)(2,1)S(1)} %get-tuple-element.23), channel_id=1, source_target_pairs={{1,2},{2,1},{3,4},{4,3},{5,6},{6,5},{7,8},{8,7},{9,10},{10,9},{11,... | collective-permute-start | bytes 122888 | tf_op jit(solution)/shard_map/ppermute | solution.py:373
  6.8 0.0 copy-start.1
  6.8 0.9 %copy-done.1 = bf16[3,3,3,256,16]{3,4,2,1,0:T(8,128)(2,1)S(1)} copy-done((bf16[3,3,3,256,16]{3,4,2,1,0:T(8,128)(2,1)S(1)}, bf16[3,3,3,256,16]{3,4,2,1,0:T(8,128)(2,1)}, u32[]{:S(2)}) %copy-start.1) | copy-done | bytes 221208
  7.8 1.3 %shard_map.60._ = bf16[16,16,1728]{2,1,0:T(8,128)(2,1)} custom-call(bf16[27,16,256]{2,1,0:T(8,128)(2,1)S(1)} %bitcast.8), custom_call_target="tpu_custom_call" | custom-call | flops 28311552 | bytes 1105920 | tf_op jit(solution)/shard_map/pallas_call | solution.py:55
  9.1 0.0 collective-permute-done.edge
  9.1 0.2 shard_map.61
  9.2 4.7 %collective-permute-start.1 = (bf16[15,32,128]{2,1,0:T(8,128)(2,1)S(1)}, bf16[15,32,128]{2,1,0:T(8,128)(2,1)S(1)}, u32[]{:S(2)}, u32[]{:S(2)}) collective-permute-start(bf16[15,32,128]{2,1,0:T(8,128)(2,1)S(1)} %get-tuple-element.24.here), channel_id=1, source_target_pairs={{0,16},{16,0},{32,48},{48,32},{64,80},{80,64},{96,112},{112,96},{1... | collective-permute-start | bytes 368648 | tf_op jit(solution)/shard_map/ppermute | solution.py:391
  13.9 2.8 %collective-permute-done.1.pair = bf16[15,32,128]{2,1,0:T(8,128)(2,1)S(1)} collective-permute-done((bf16[15,32,128]{2,1,0:T(8,128)(2,1)S(1)}, bf16[15,32,128]{2,1,0:T(8,128)(2,1)S(1)}, u32[]{:S(2)}, u32[]{:S(2)}) %collective-permute-start.1) | collective-permute-done | bytes 122912 | tf_op jit(solution)/shard_map/ppermute | solution.py:391
  16.8 0.0 copy-start
  16.8 7.3 %all-to-all-start = ((bf16[16,16,1728]{2,1,0:T(8,128)(2,1)}), bf16[16,16,1728]{2,1,0:T(8,128)(2,1)S(1)}, u32[]{:S(2)}, u32[]{:S(2)}) async-start(bf16[16,16,1728]{2,1,0:T(8,128)(2,1)} %get-tuple-element.26), calls=%async_computation | async-start | bytes 1835008 | tf_op jit(solution)/shard_map/all_to_all | solution.py:399
  24.1 3.2 %collective-permute-start.2 = (bf16[12,32,128]{2,1,0:T(8,128)(2,1)S(1)}, bf16[12,32,128]{2,1,0:T(8,128)(2,1)S(1)}, u32[]{:S(2)}, u32[]{:S(2)}) collective-permute-start(bf16[12,32,128]{2,1,0:T(8,128)(2,1)S(1)} %get-tuple-element.27), channel_id=1, source_target_pairs={{0,32},{16,48},{32,64},{48,80},{64,96},{80,112},{96,128},{112,144}... | collective-permute-start | bytes 294920 | tf_op jit(solution)/shard_map/ppermute | solution.py:402
  27.3 1.3 %collective-permute-start.3 = (bf16[3,32,128]{2,1,0:T(8,128)(2,1)S(1)}, bf16[3,32,128]{2,1,0:T(8,128)(2,1)S(1)}, u32[]{:S(2)}, u32[]{:S(2)}) collective-permute-start(bf16[3,32,128]{2,1,0:T(8,128)(2,1)S(1)} %get-tuple-element.28), channel_id=1, source_target_pairs={{32,0},{48,16},{64,32},{80,48},{96,64},{112,80},{128,96},{144,112}... | collective-permute-start | bytes 73736 | tf_op jit(solution)/shard_map/ppermute | solution.py:403
  28.6 3.7 %collective-permute-done.3.after = bf16[3,32,128]{2,1,0:T(8,128)(2,1)S(1)} collective-permute-done((bf16[3,32,128]{2,1,0:T(8,128)(2,1)S(1)}, bf16[3,32,128]{2,1,0:T(8,128)(2,1)S(1)}, u32[]{:S(2)}, u32[]{:S(2)}) %collective-permute-start.3) | collective-permute-done | bytes 24608 | tf_op jit(solution)/shard_map/ppermute | solution.py:403
  32.3 0.0 collective-permute-done.2.before
  32.3 0.1 shard_map.63.own
  32.4 2.9 %collective-permute-start.4 = (bf16[45,32,128]{2,1,0:T(8,128)(2,1)S(1)}, bf16[45,32,128]{2,1,0:T(8,128)(2,1)S(1)}, u32[]{:S(2)}, u32[]{:S(2)}) collective-permute-start(bf16[45,32,128]{2,1,0:T(8,128)(2,1)S(1)} %shard_map.63.own), channel_id=1, source_target_pairs={{0,1},{1,0},{2,3},{3,2},{4,5},{5,4},{6,7},{7,6},{8,9},{9,8},{10,11... | collective-permute-start | bytes 1105928 | tf_op jit(solution)/shard_map/ppermute | solution.py:416
  35.3 0.0 copy-done
  35.3 1.1 %shard_map.64 = (bf16[3,512,384]{2,1,0:T(8,128)(2,1)S(1)}, bf16[64,3456]{1,0:T(8,128)(2,1)S(1)}) custom-call(bf16[3456,256]{1,0:T(8,128)(2,1)S(1)} %bitcast.7), custom_call_target="tpu_custom_call" | custom-call | flops 339738624 | bytes 3391488 | tf_op jit(solution)/shard_map/pallas_call | solution.py:55
  36.5 0.1 collective-permute-done.4.other
  36.6 2.0 %shard_map.65 = (bf16[72,16,512]{2,1,0:T(8,128)(2,1)S(1)}, bf16[2,18,16,256]{3,2,1,0:T(8,128)(2,1)S(1)}, f32[2,2,2,5,16,128]{5,4,3,2,1,0:T(8,128)S(1)}) custom-call(bf16[45,32,128]{2,1,0:T(8,128)(2,1)S(1)} %shard_map.63.own, bf16[45,32,128]{2,1,0:T(8,128)(2,1)S(1)} %collective-permute-done.4.other, bf16[3,512,384]{2,1,0:T(8,128)(2,1)S(1)} %get-tuple-element.29.filters), custom_call_target="tpu_custom_call" | custom-call | flops 754974720 | bytes 3719168 | tf_op jit(solution)/shard_map/pallas_call | solution.py:55
  38.7 0.0 all-to-all-done
  38.7 2.3 %shard_map.66 = (bf16[4,10,16,128]{3,2,1,0:T(8,128)(2,1)S(1)}, bf16[16,7,16,128]{3,2,1,0:T(8,128)(2,1)}) custom-call(bf16[256,1728]{1,0:T(8,128)(2,1)S(1)} %bitcast.6, bf16[2,18,16,256]{3,2,1,0:T(8,128)(2,1)S(1)} %get-tuple-element.30.ups, f32[2,2,2,5,16,128]{5,4,3,2,1,0:T(8,128)S(1)} %get-tuple-element.31.pre, bf16[72,16,512]{2,1,0:T(8,128)(2,1)S(1)} %get-tuple-element.32.wide), custom_call_target="tpu_custom_call" | custom-call | flops 603979776 | bytes 3309568 | tf_op jit(solution)/shard_map/pallas_call | solution.py:55
  41.0 6.7 %all-to-all-start.1 = ((bf16[16,7,16,128]{3,2,1,0:T(8,128)(2,1)}), bf16[16,7,16,128]{3,2,1,0:T(8,128)(2,1)S(1)}, u32[]{:S(2)}, u32[]{:S(2)}) async-start(bf16[16,7,16,128]{3,2,1,0:T(8,128)(2,1)} %get-tuple-element.40), calls=%async_computation.1 | async-start | bytes 917504 | tf_op jit(solution)/shard_map/all_to_all | solution.py:442
  47.7 1.3 %collective-permute-start.5 = (bf16[2,10,16,128]{3,2,1,0:T(8,128)(2,1)S(1)}, bf16[2,10,16,128]{3,2,1,0:T(8,128)(2,1)S(1)}, u32[]{:S(2)}, u32[]{:S(2)}) collective-permute-start(bf16[2,10,16,128]{3,2,1,0:T(8,128)(2,1)S(1)} %slice.3), channel_id=1, source_target_pairs={{32,0},{48,16},{64,32},{80,48},{96,64},{112,80},{128,96},{144,112}... | collective-permute-start | bytes 245768 | tf_op jit(solution)/shard_map/ppermute | solution.py:443
  49.0 4.4 %collective-permute-done.5.following = bf16[2,10,16,128]{3,2,1,0:T(8,128)(2,1)S(1)} collective-permute-done((bf16[2,10,16,128]{3,2,1,0:T(8,128)(2,1)S(1)}, bf16[2,10,16,128]{3,2,1,0:T(8,128)(2,1)S(1)}, u32[]{:S(2)}, u32[]{:S(2)}) %collective-permute-start.5) | collective-permute-done | bytes 81952 | tf_op jit(solution)/shard_map/ppermute | solution.py:443
  53.4 1.1 %shard_map.67 = (f32[2,8,16,256]{3,2,1,0:T(8,128)S(1)}, bf16[2,8,16,256]{3,2,1,0:T(8,128)(2,1)S(1)}) custom-call(bf16[4,10,16,128]{3,2,1,0:T(8,128)(2,1)S(1)} %get-tuple-element.33.grad, bf16[2,10,16,128]{3,2,1,0:T(8,128)(2,1)S(1)} %collective-permute-done.5.following, bf16[64,3456]{1,0:T(8,128)(2,1)S(1)} %get-tuple-element.34.flat), custom_call_target="tpu_custom_call" | custom-call | flops 603979776 | bytes 1081344 | tf_op jit(solution)/shard_map/pallas_call | solution.py:55
  54.5 4.8 %collective-permute-start.6 = (bf16[2,8,16,256]{3,2,1,0:T(8,128)(2,1)S(1)}, bf16[2,8,16,256]{3,2,1,0:T(8,128)(2,1)S(1)}, u32[]{:S(2)}, u32[]{:S(2)}) collective-permute-start(bf16[2,8,16,256]{3,2,1,0:T(8,128)(2,1)S(1)} %get-tuple-element.36._), channel_id=1, source_target_pairs={{0,16},{16,0},{32,48},{48,32},{64,80},{80,64},{96,112},{112,96},{1... | collective-permute-start | bytes 393224 | tf_op jit(solution)/shard_map/ppermute | solution.py:463
  59.3 0.0 all-to-all-done.1.parts
  59.3 0.8 shard_map.70
  60.1 18.1 %all-to-all-start.2 = ((bf16[16,16,128]{2,1,0:T(8,128)(2,1)}), bf16[16,16,128]{2,1,0:T(8,128)(2,1)S(1)}, u32[]{:S(2)}, u32[]{:S(2)}) async-start(bf16[16,16,128]{2,1,0:T(8,128)(2,1)} %shard_map.70), calls=%async_computation.2 | async-start | bytes 131072 | tf_op jit(solution)/shard_map/all_to_all | solution.py:462
  78.2 0.0 collective-permute-done.6.got
  78.2 4.5 %collective-permute-start.7 = (f32[2,4,16,256]{3,2,1,0:T(8,128)S(1)}, f32[2,4,16,256]{3,2,1,0:T(8,128)S(1)}, u32[]{:S(2)}, u32[]{:S(2)}) collective-permute-start(f32[2,4,16,256]{3,2,1,0:T(8,128)S(1)} %get-tuple-element.38), channel_id=1, source_target_pairs={{0,1},{1,0},{2,3},{3,2},{4,5},{5,4},{6,7},{7,6},{8,9},{9,8},{10,11... | collective-permute-start | bytes 393224 | tf_op jit(solution)/shard_map/ppermute | solution.py:469
  82.8 1.0 %collective-permute-done.7.got = f32[2,4,16,256]{3,2,1,0:T(8,128)S(1)} collective-permute-done((f32[2,4,16,256]{3,2,1,0:T(8,128)S(1)}, f32[2,4,16,256]{3,2,1,0:T(8,128)S(1)}, u32[]{:S(2)}, u32[]{:S(2)}) %collective-permute-start.7) | collective-permute-done | bytes 131104 | tf_op jit(solution)/shard_map/ppermute | solution.py:469
  83.7 0.8 shard_map.69
  84.6 0.0 all-to-all-done.2.parts
  84.6 0.7 shard_map.71
  (4 shorter events, 0.1 us)
Async XLA Ops:
  0.6 0.8 copy-start.2
  1.5 0.7 copy-start.3
  2.2 6.8 %collective-permute-start = (bf16[5,32,128]{2,1,0:T(8,128)(2,1)S(1)}, bf16[5,32,128]{2,1,0:T(8,128)(2,1)S(1)}, u32[]{:S(2)}, u32[]{:S(2)}) collective-permute-start(bf16[5,32,128]{2,1,0:T(8,128)(2,1)S(1)} %get-tuple-element.23), channel_id=1, source_target_pairs={{1,2},{2,1},{3,4},{4,3},{5,6},{6,5},{7,8},{8,7},{9,10},{10,9},{11,... | collective-permute-start | bytes 122888 | tf_op jit(solution)/shard_map/ppermute | solution.py:373
  6.8 0.9 %copy-start.1 = (bf16[3,3,3,256,16]{3,4,2,1,0:T(8,128)(2,1)S(1)}, bf16[3,3,3,256,16]{3,4,2,1,0:T(8,128)(2,1)}, u32[]{:S(2)}) copy-start(bf16[3,3,3,256,16]{3,4,2,1,0:T(8,128)(2,1)} %param.6) | copy-start | bytes 663556
  9.2 7.5 %collective-permute-start.1 = (bf16[15,32,128]{2,1,0:T(8,128)(2,1)S(1)}, bf16[15,32,128]{2,1,0:T(8,128)(2,1)S(1)}, u32[]{:S(2)}, u32[]{:S(2)}) collective-permute-start(bf16[15,32,128]{2,1,0:T(8,128)(2,1)S(1)} %get-tuple-element.24.here), channel_id=1, source_target_pairs={{0,16},{16,0},{32,48},{48,32},{64,80},{80,64},{96,112},{112,96},{1... | collective-permute-start | bytes 368648 | tf_op jit(solution)/shard_map/ppermute | solution.py:391
  16.8 18.6 %copy-start = (bf16[3,3,3,128,256]{4,3,2,1,0:T(8,128)(2,1)S(1)}, bf16[3,3,3,128,256]{4,3,2,1,0:T(8,128)(2,1)}, u32[]{:S(2)}) copy-start(bf16[3,3,3,128,256]{4,3,2,1,0:T(8,128)(2,1)} %param.5) | copy-start | bytes 5308420
  16.8 21.9 %all-to-all-start = ((bf16[16,16,1728]{2,1,0:T(8,128)(2,1)}), bf16[16,16,1728]{2,1,0:T(8,128)(2,1)S(1)}, u32[]{:S(2)}, u32[]{:S(2)}) async-start(bf16[16,16,1728]{2,1,0:T(8,128)(2,1)} %get-tuple-element.26), calls=%async_computation | async-start | bytes 1835008 | tf_op jit(solution)/shard_map/all_to_all | solution.py:399
  24.1 8.2 %collective-permute-start.2 = (bf16[12,32,128]{2,1,0:T(8,128)(2,1)S(1)}, bf16[12,32,128]{2,1,0:T(8,128)(2,1)S(1)}, u32[]{:S(2)}, u32[]{:S(2)}) collective-permute-start(bf16[12,32,128]{2,1,0:T(8,128)(2,1)S(1)} %get-tuple-element.27), channel_id=1, source_target_pairs={{0,32},{16,48},{32,64},{48,80},{64,96},{80,112},{96,128},{112,144}... | collective-permute-start | bytes 294920 | tf_op jit(solution)/shard_map/ppermute | solution.py:402
  27.3 5.0 %collective-permute-start.3 = (bf16[3,32,128]{2,1,0:T(8,128)(2,1)S(1)}, bf16[3,32,128]{2,1,0:T(8,128)(2,1)S(1)}, u32[]{:S(2)}, u32[]{:S(2)}) collective-permute-start(bf16[3,32,128]{2,1,0:T(8,128)(2,1)S(1)} %get-tuple-element.28), channel_id=1, source_target_pairs={{32,0},{48,16},{64,32},{80,48},{96,64},{112,80},{128,96},{144,112}... | collective-permute-start | bytes 73736 | tf_op jit(solution)/shard_map/ppermute | solution.py:403
  32.4 4.2 %collective-permute-start.4 = (bf16[45,32,128]{2,1,0:T(8,128)(2,1)S(1)}, bf16[45,32,128]{2,1,0:T(8,128)(2,1)S(1)}, u32[]{:S(2)}, u32[]{:S(2)}) collective-permute-start(bf16[45,32,128]{2,1,0:T(8,128)(2,1)S(1)} %shard_map.63.own), channel_id=1, source_target_pairs={{0,1},{1,0},{2,3},{3,2},{4,5},{5,4},{6,7},{7,6},{8,9},{9,8},{10,11... | collective-permute-start | bytes 1105928 | tf_op jit(solution)/shard_map/ppermute | solution.py:416
  41.0 18.3 %all-to-all-start.1 = ((bf16[16,7,16,128]{3,2,1,0:T(8,128)(2,1)}), bf16[16,7,16,128]{3,2,1,0:T(8,128)(2,1)S(1)}, u32[]{:S(2)}, u32[]{:S(2)}) async-start(bf16[16,7,16,128]{3,2,1,0:T(8,128)(2,1)} %get-tuple-element.40), calls=%async_computation.1 | async-start | bytes 917504 | tf_op jit(solution)/shard_map/all_to_all | solution.py:442
  47.7 5.7 %collective-permute-start.5 = (bf16[2,10,16,128]{3,2,1,0:T(8,128)(2,1)S(1)}, bf16[2,10,16,128]{3,2,1,0:T(8,128)(2,1)S(1)}, u32[]{:S(2)}, u32[]{:S(2)}) collective-permute-start(bf16[2,10,16,128]{3,2,1,0:T(8,128)(2,1)S(1)} %slice.3), channel_id=1, source_target_pairs={{32,0},{48,16},{64,32},{80,48},{96,64},{112,80},{128,96},{144,112}... | collective-permute-start | bytes 245768 | tf_op jit(solution)/shard_map/ppermute | solution.py:443
  54.5 23.7 %collective-permute-start.6 = (bf16[2,8,16,256]{3,2,1,0:T(8,128)(2,1)S(1)}, bf16[2,8,16,256]{3,2,1,0:T(8,128)(2,1)S(1)}, u32[]{:S(2)}, u32[]{:S(2)}) collective-permute-start(bf16[2,8,16,256]{3,2,1,0:T(8,128)(2,1)S(1)} %get-tuple-element.36._), channel_id=1, source_target_pairs={{0,16},{16,0},{32,48},{48,32},{64,80},{80,64},{96,112},{112,96},{1... | collective-permute-start | bytes 393224 | tf_op jit(solution)/shard_map/ppermute | solution.py:463
  60.1 24.5 %all-to-all-start.2 = ((bf16[16,16,128]{2,1,0:T(8,128)(2,1)}), bf16[16,16,128]{2,1,0:T(8,128)(2,1)S(1)}, u32[]{:S(2)}, u32[]{:S(2)}) async-start(bf16[16,16,128]{2,1,0:T(8,128)(2,1)} %shard_map.70), calls=%async_computation.2 | async-start | bytes 131072 | tf_op jit(solution)/shard_map/all_to_all | solution.py:462
  78.2 5.5 %collective-permute-start.7 = (f32[2,4,16,256]{3,2,1,0:T(8,128)S(1)}, f32[2,4,16,256]{3,2,1,0:T(8,128)S(1)}, u32[]{:S(2)}, u32[]{:S(2)}) collective-permute-start(f32[2,4,16,256]{3,2,1,0:T(8,128)S(1)} %get-tuple-element.38), channel_id=1, source_target_pairs={{0,1},{1,0},{2,3},{3,2},{4,5},{5,4},{6,7},{7,6},{8,9},{9,8},{10,11... | collective-permute-start | bytes 393224 | tf_op jit(solution)/shard_map/ppermute | solution.py:469

commit v8 on v6

--- a/solution.py
+++ b/solution.py
@@ -275,7 +275,7 @@
         halves += [total.reshape(112, 128), blank]
     flat = jnp.concatenate(halves, 0).T
     for i in range(16):
-        z = (i + 8) % 16
+        z = (i + 11) % 16
         rows = [(tap * 64 + z * 4, x) for x in range(2) for tap in range(2)]
         block = [flat[r : r + 4, 128 * x : 128 * x + 128] for r, x in rows]
         out[i] = jnp.concatenate(block, 0).astype(BF16)
@@ -446,7 +446,7 @@
         [parts, send],
         idle=(1,),
     )
-    columns = [[2 * ((i + 8) % lines) + x for i in range(lines)] for x in range(2)]
+    columns = [[2 * ((i + 11) % lines) + x for i in range(lines)] for x in range(2)]
     summed = lax.all_to_all(sums, "tm", 0, 0, axis_index_groups=columns)
     got = lax.ppermute(send, "tm", blocks)
     keep, send = call(

time: 86 us -> 87 us (1.012); the launches traced: 85.4 us -> 85.4 us
  no operation moved by 1% of the time
where the time goes in v8:
time: 87 us; the launch traced here: 85.4 us
  starting transfers between devices  59.4 us (68%)
  waiting for transfers between devices  12.1 us (14%)
  Pallas kernels  10.6 us (12%)
  local copies, waits for them, and re-layouts  2.49 us (3%)
    all_to_all x1, starting transfers between devices, body(): summed = lax.all_to_all(sums, 'tm', 0, 0, axis_index_groups=columns)  18.1 us
    pallas_call x13, Pallas kernels, call(): pl.pallas_call(kernel, out_shape=tuple(out), in_specs=[far if i in idle e...  10.6 us
    all_to_all x1, starting transfers between devices, body(): second = lax.all_to_all(pieces, 'height', 0, 0).reshape(chans, 27 * OWN)  7.31 us
    all_to_all x1, starting transfers between devices, body(): lax.all_to_all(parts, ('tm', 'height'), 0, 0, axis_index_groups=planes)  6.69 us
    ppermute x1, starting transfers between devices, body(): got = lax.ppermute(send, 'tm', blocks)  4.78 us
    ppermute x1, starting transfers between devices, body(): pair = lax.ppermute(here, 'tm', blocks)  4.66 us
    ppermute x1, starting transfers between devices, body(): edge = lax.ppermute(edge, 'height', near_pairs)  4.59 us
    ppermute x1, starting transfers between devices, body(): got = lax.ppermute(send, 'height', siblings)  4.53 us
  transfers between devices with their start and end apart: 11, of which 5 were waited for; matrix products, arithmetic and copies ran while one was open for 0% of the time, Pallas kernels for 9%

profile of v8, /device:TPU:1, one launch (start us, length us, event | category | flops | bytes accessed | tf_op | source)
XLA Modules:
  0.0 85.4 jit_solution(878514436327013997)
XLA Ops:
  0.6 0.0 copy-start.2
  0.6 0.8 copy-done.2
  1.5 0.0 copy-start.3
  1.5 0.7 copy-done.3
  2.2 4.6 %collective-permute-start = (bf16[5,32,128]{2,1,0:T(8,128)(2,1)S(1)}, bf16[5,32,128]{2,1,0:T(8,128)(2,1)S(1)}, u32[]{:S(2)}, u32[]{:S(2)}) collective-permute-start(bf16[5,32,128]{2,1,0:T(8,128)(2,1)S(1)} %get-tuple-element.23), channel_id=1, source_target_pairs={{1,2},{2,1},{3,4},{4,3},{5,6},{6,5},{7,8},{8,7},{9,10},{10,9},{11,... | collective-permute-start | bytes 122888 | tf_op jit(solution)/shard_map/ppermute | solution.py:361
  6.8 0.0 copy-start.1
  6.8 0.9 %copy-done.1 = bf16[3,3,3,256,16]{3,4,2,1,0:T(8,128)(2,1)S(1)} copy-done((bf16[3,3,3,256,16]{3,4,2,1,0:T(8,128)(2,1)S(1)}, bf16[3,3,3,256,16]{3,4,2,1,0:T(8,128)(2,1)}, u32[]{:S(2)}) %copy-start.1) | copy-done | bytes 221208
  7.8 1.3 %shard_map.60._ = bf16[16,16,1728]{2,1,0:T(8,128)(2,1)} custom-call(bf16[27,16,256]{2,1,0:T(8,128)(2,1)S(1)} %bitcast.8), custom_call_target="tpu_custom_call" | custom-call | flops 28311552 | bytes 1105920 | tf_op jit(solution)/shard_map/pallas_call | solution.py:55
  9.1 0.0 collective-permute-done.edge
  9.1 0.2 shard_map.61
  9.2 4.7 %collective-permute-start.1 = (bf16[15,32,128]{2,1,0:T(8,128)(2,1)S(1)}, bf16[15,32,128]{2,1,0:T(8,128)(2,1)S(1)}, u32[]{:S(2)}, u32[]{:S(2)}) collective-permute-start(bf16[15,32,128]{2,1,0:T(8,128)(2,1)S(1)} %get-tuple-element.24.here), channel_id=1, source_target_pairs={{0,16},{16,0},{32,48},{48,32},{64,80},{80,64},{96,112},{112,96},{1... | collective-permute-start | bytes 368648 | tf_op jit(solution)/shard_map/ppermute | solution.py:379
  13.9 2.8 %collective-permute-done.1.pair = bf16[15,32,128]{2,1,0:T(8,128)(2,1)S(1)} collective-permute-done((bf16[15,32,128]{2,1,0:T(8,128)(2,1)S(1)}, bf16[15,32,128]{2,1,0:T(8,128)(2,1)S(1)}, u32[]{:S(2)}, u32[]{:S(2)}) %collective-permute-start.1) | collective-permute-done | bytes 122912 | tf_op jit(solution)/shard_map/ppermute | solution.py:379
  16.8 0.0 copy-start
  16.8 7.3 %all-to-all-start = ((bf16[16,16,1728]{2,1,0:T(8,128)(2,1)}), bf16[16,16,1728]{2,1,0:T(8,128)(2,1)S(1)}, u32[]{:S(2)}, u32[]{:S(2)}) async-start(bf16[16,16,1728]{2,1,0:T(8,128)(2,1)} %get-tuple-element.26), calls=%async_computation | async-start | bytes 1835008 | tf_op jit(solution)/shard_map/all_to_all | solution.py:387
  24.1 3.2 %collective-permute-start.2 = (bf16[12,32,128]{2,1,0:T(8,128)(2,1)S(1)}, bf16[12,32,128]{2,1,0:T(8,128)(2,1)S(1)}, u32[]{:S(2)}, u32[]{:S(2)}) collective-permute-start(bf16[12,32,128]{2,1,0:T(8,128)(2,1)S(1)} %get-tuple-element.27), channel_id=1, source_target_pairs={{0,32},{16,48},{32,64},{48,80},{64,96},{80,112},{96,128},{112,144}... | collective-permute-start | bytes 294920 | tf_op jit(solution)/shard_map/ppermute | solution.py:390
  27.3 1.3 %collective-permute-start.3 = (bf16[3,32,128]{2,1,0:T(8,128)(2,1)S(1)}, bf16[3,32,128]{2,1,0:T(8,128)(2,1)S(1)}, u32[]{:S(2)}, u32[]{:S(2)}) collective-permute-start(bf16[3,32,128]{2,1,0:T(8,128)(2,1)S(1)} %get-tuple-element.28), channel_id=1, source_target_pairs={{32,0},{48,16},{64,32},{80,48},{96,64},{112,80},{128,96},{144,112}... | collective-permute-start | bytes 73736 | tf_op jit(solution)/shard_map/ppermute | solution.py:391
  28.6 3.7 %collective-permute-done.3.after = bf16[3,32,128]{2,1,0:T(8,128)(2,1)S(1)} collective-permute-done((bf16[3,32,128]{2,1,0:T(8,128)(2,1)S(1)}, bf16[3,32,128]{2,1,0:T(8,128)(2,1)S(1)}, u32[]{:S(2)}, u32[]{:S(2)}) %collective-permute-start.3) | collective-permute-done | bytes 24608 | tf_op jit(solution)/shard_map/ppermute | solution.py:391
  32.3 0.0 collective-permute-done.2.before
  32.3 0.1 shard_map.63.own
  32.4 2.9 %collective-permute-start.4 = (bf16[45,32,128]{2,1,0:T(8,128)(2,1)S(1)}, bf16[45,32,128]{2,1,0:T(8,128)(2,1)S(1)}, u32[]{:S(2)}, u32[]{:S(2)}) collective-permute-start(bf16[45,32,128]{2,1,0:T(8,128)(2,1)S(1)} %shard_map.63.own), channel_id=1, source_target_pairs={{0,1},{1,0},{2,3},{3,2},{4,5},{5,4},{6,7},{7,6},{8,9},{9,8},{10,11... | collective-permute-start | bytes 1105928 | tf_op jit(solution)/shard_map/ppermute | solution.py:404
  35.3 0.0 copy-done
  35.3 1.1 %shard_map.64 = (bf16[3,512,384]{2,1,0:T(8,128)(2,1)S(1)}, bf16[64,3456]{1,0:T(8,128)(2,1)S(1)}) custom-call(bf16[3456,256]{1,0:T(8,128)(2,1)S(1)} %bitcast.7), custom_call_target="tpu_custom_call" | custom-call | flops 339738624 | bytes 3391488 | tf_op jit(solution)/shard_map/pallas_call | solution.py:55
  36.5 0.1 collective-permute-done.4.other
  36.6 2.0 %shard_map.65 = (bf16[72,16,512]{2,1,0:T(8,128)(2,1)S(1)}, bf16[2,18,16,256]{3,2,1,0:T(8,128)(2,1)S(1)}, f32[2,2,2,5,16,128]{5,4,3,2,1,0:T(8,128)S(1)}) custom-call(bf16[45,32,128]{2,1,0:T(8,128)(2,1)S(1)} %shard_map.63.own, bf16[45,32,128]{2,1,0:T(8,128)(2,1)S(1)} %collective-permute-done.4.other, bf16[3,512,384]{2,1,0:T(8,128)(2,1)S(1)} %get-tuple-element.29.filters), custom_call_target="tpu_custom_call" | custom-call | flops 754974720 | bytes 3719168 | tf_op jit(solution)/shard_map/pallas_call | solution.py:55
  38.7 0.0 all-to-all-done
  38.7 2.4 %shard_map.66 = (bf16[4,10,16,128]{3,2,1,0:T(8,128)(2,1)S(1)}, bf16[16,7,16,128]{3,2,1,0:T(8,128)(2,1)}) custom-call(bf16[256,1728]{1,0:T(8,128)(2,1)S(1)} %bitcast.6, bf16[2,18,16,256]{3,2,1,0:T(8,128)(2,1)S(1)} %get-tuple-element.30.ups, f32[2,2,2,5,16,128]{5,4,3,2,1,0:T(8,128)S(1)} %get-tuple-element.31.pre, bf16[72,16,512]{2,1,0:T(8,128)(2,1)S(1)} %get-tuple-element.32.wide), custom_call_target="tpu_custom_call" | custom-call | flops 603979776 | bytes 3309568 | tf_op jit(solution)/shard_map/pallas_call | solution.py:55
  41.1 6.7 %all-to-all-start.1 = ((bf16[16,7,16,128]{3,2,1,0:T(8,128)(2,1)}), bf16[16,7,16,128]{3,2,1,0:T(8,128)(2,1)S(1)}, u32[]{:S(2)}, u32[]{:S(2)}) async-start(bf16[16,7,16,128]{3,2,1,0:T(8,128)(2,1)} %get-tuple-element.40), calls=%async_computation.1 | async-start | bytes 917504 | tf_op jit(solution)/shard_map/all_to_all | solution.py:430
  47.8 1.3 %collective-permute-start.5 = (bf16[2,10,16,128]{3,2,1,0:T(8,128)(2,1)S(1)}, bf16[2,10,16,128]{3,2,1,0:T(8,128)(2,1)S(1)}, u32[]{:S(2)}, u32[]{:S(2)}) collective-permute-start(bf16[2,10,16,128]{3,2,1,0:T(8,128)(2,1)S(1)} %slice.3), channel_id=1, source_target_pairs={{32,0},{48,16},{64,32},{80,48},{96,64},{112,80},{128,96},{144,112}... | collective-permute-start | bytes 245768 | tf_op jit(solution)/shard_map/ppermute | solution.py:431
  49.1 4.4 %collective-permute-done.5.following = bf16[2,10,16,128]{3,2,1,0:T(8,128)(2,1)S(1)} collective-permute-done((bf16[2,10,16,128]{3,2,1,0:T(8,128)(2,1)S(1)}, bf16[2,10,16,128]{3,2,1,0:T(8,128)(2,1)S(1)}, u32[]{:S(2)}, u32[]{:S(2)}) %collective-permute-start.5) | collective-permute-done | bytes 81952 | tf_op jit(solution)/shard_map/ppermute | solution.py:431
  53.4 1.1 %shard_map.67 = (f32[2,8,16,256]{3,2,1,0:T(8,128)S(1)}, bf16[2,8,16,256]{3,2,1,0:T(8,128)(2,1)S(1)}) custom-call(bf16[4,10,16,128]{3,2,1,0:T(8,128)(2,1)S(1)} %get-tuple-element.33.grad, bf16[2,10,16,128]{3,2,1,0:T(8,128)(2,1)S(1)} %collective-permute-done.5.following, bf16[64,3456]{1,0:T(8,128)(2,1)S(1)} %get-tuple-element.34.flat), custom_call_target="tpu_custom_call" | custom-call | flops 603979776 | bytes 1081344 | tf_op jit(solution)/shard_map/pallas_call | solution.py:55
  54.6 4.8 %collective-permute-start.6 = (bf16[2,8,16,256]{3,2,1,0:T(8,128)(2,1)S(1)}, bf16[2,8,16,256]{3,2,1,0:T(8,128)(2,1)S(1)}, u32[]{:S(2)}, u32[]{:S(2)}) collective-permute-start(bf16[2,8,16,256]{3,2,1,0:T(8,128)(2,1)S(1)} %get-tuple-element.36._), channel_id=1, source_target_pairs={{0,16},{16,0},{32,48},{48,32},{64,80},{80,64},{96,112},{112,96},{1... | collective-permute-start | bytes 393224 | tf_op jit(solution)/shard_map/ppermute | solution.py:451
  59.3 0.0 all-to-all-done.1.parts
  59.4 0.8 shard_map.70
  60.1 18.1 %all-to-all-start.2 = ((bf16[16,16,128]{2,1,0:T(8,128)(2,1)}), bf16[16,16,128]{2,1,0:T(8,128)(2,1)S(1)}, u32[]{:S(2)}, u32[]{:S(2)}) async-start(bf16[16,16,128]{2,1,0:T(8,128)(2,1)} %shard_map.70), calls=%async_computation.2 | async-start | bytes 131072 | tf_op jit(solution)/shard_map/all_to_all | solution.py:450
  78.2 0.0 collective-permute-done.6.got
  78.3 4.5 %collective-permute-start.7 = (f32[2,4,16,256]{3,2,1,0:T(8,128)S(1)}, f32[2,4,16,256]{3,2,1,0:T(8,128)S(1)}, u32[]{:S(2)}, u32[]{:S(2)}) collective-permute-start(f32[2,4,16,256]{3,2,1,0:T(8,128)S(1)} %get-tuple-element.38), channel_id=1, source_target_pairs={{0,1},{1,0},{2,3},{3,2},{4,5},{5,4},{6,7},{7,6},{8,9},{9,8},{10,11... | collective-permute-start | bytes 393224 | tf_op jit(solution)/shard_map/ppermute | solution.py:457
  82.8 1.0 %collective-permute-done.7.got = f32[2,4,16,256]{3,2,1,0:T(8,128)S(1)} collective-permute-done((f32[2,4,16,256]{3,2,1,0:T(8,128)S(1)}, f32[2,4,16,256]{3,2,1,0:T(8,128)S(1)}, u32[]{:S(2)}, u32[]{:S(2)}) %collective-permute-start.7) | collective-permute-done | bytes 131104 | tf_op jit(solution)/shard_map/ppermute | solution.py:457
  83.8 0.8 shard_map.69
  84.6 0.0 all-to-all-done.2.parts
  84.6 0.7 shard_map.71
  (4 shorter events, 0.1 us)
Async XLA Ops:
  0.6 0.8 copy-start.2
  1.5 0.7 copy-start.3
  2.2 6.8 %collective-permute-start = (bf16[5,32,128]{2,1,0:T(8,128)(2,1)S(1)}, bf16[5,32,128]{2,1,0:T(8,128)(2,1)S(1)}, u32[]{:S(2)}, u32[]{:S(2)}) collective-permute-start(bf16[5,32,128]{2,1,0:T(8,128)(2,1)S(1)} %get-tuple-element.23), channel_id=1, source_target_pairs={{1,2},{2,1},{3,4},{4,3},{5,6},{6,5},{7,8},{8,7},{9,10},{10,9},{11,... | collective-permute-start | bytes 122888 | tf_op jit(solution)/shard_map/ppermute | solution.py:361
  6.8 0.9 %copy-start.1 = (bf16[3,3,3,256,16]{3,4,2,1,0:T(8,128)(2,1)S(1)}, bf16[3,3,3,256,16]{3,4,2,1,0:T(8,128)(2,1)}, u32[]{:S(2)}) copy-start(bf16[3,3,3,256,16]{3,4,2,1,0:T(8,128)(2,1)} %param.6) | copy-start | bytes 663556
  9.2 7.5 %collective-permute-start.1 = (bf16[15,32,128]{2,1,0:T(8,128)(2,1)S(1)}, bf16[15,32,128]{2,1,0:T(8,128)(2,1)S(1)}, u32[]{:S(2)}, u32[]{:S(2)}) collective-permute-start(bf16[15,32,128]{2,1,0:T(8,128)(2,1)S(1)} %get-tuple-element.24.here), channel_id=1, source_target_pairs={{0,16},{16,0},{32,48},{48,32},{64,80},{80,64},{96,112},{112,96},{1... | collective-permute-start | bytes 368648 | tf_op jit(solution)/shard_map/ppermute | solution.py:379
  16.8 18.6 %copy-start = (bf16[3,3,3,128,256]{4,3,2,1,0:T(8,128)(2,1)S(1)}, bf16[3,3,3,128,256]{4,3,2,1,0:T(8,128)(2,1)}, u32[]{:S(2)}) copy-start(bf16[3,3,3,128,256]{4,3,2,1,0:T(8,128)(2,1)} %param.5) | copy-start | bytes 5308420
  16.8 21.9 %all-to-all-start = ((bf16[16,16,1728]{2,1,0:T(8,128)(2,1)}), bf16[16,16,1728]{2,1,0:T(8,128)(2,1)S(1)}, u32[]{:S(2)}, u32[]{:S(2)}) async-start(bf16[16,16,1728]{2,1,0:T(8,128)(2,1)} %get-tuple-element.26), calls=%async_computation | async-start | bytes 1835008 | tf_op jit(solution)/shard_map/all_to_all | solution.py:387
  24.1 8.2 %collective-permute-start.2 = (bf16[12,32,128]{2,1,0:T(8,128)(2,1)S(1)}, bf16[12,32,128]{2,1,0:T(8,128)(2,1)S(1)}, u32[]{:S(2)}, u32[]{:S(2)}) collective-permute-start(bf16[12,32,128]{2,1,0:T(8,128)(2,1)S(1)} %get-tuple-element.27), channel_id=1, source_target_pairs={{0,32},{16,48},{32,64},{48,80},{64,96},{80,112},{96,128},{112,144}... | collective-permute-start | bytes 294920 | tf_op jit(solution)/shard_map/ppermute | solution.py:390
  27.3 5.0 %collective-permute-start.3 = (bf16[3,32,128]{2,1,0:T(8,128)(2,1)S(1)}, bf16[3,32,128]{2,1,0:T(8,128)(2,1)S(1)}, u32[]{:S(2)}, u32[]{:S(2)}) collective-permute-start(bf16[3,32,128]{2,1,0:T(8,128)(2,1)S(1)} %get-tuple-element.28), channel_id=1, source_target_pairs={{32,0},{48,16},{64,32},{80,48},{96,64},{112,80},{128,96},{144,112}... | collective-permute-start | bytes 73736 | tf_op jit(solution)/shard_map/ppermute | solution.py:391
  32.4 4.2 %collective-permute-start.4 = (bf16[45,32,128]{2,1,0:T(8,128)(2,1)S(1)}, bf16[45,32,128]{2,1,0:T(8,128)(2,1)S(1)}, u32[]{:S(2)}, u32[]{:S(2)}) collective-permute-start(bf16[45,32,128]{2,1,0:T(8,128)(2,1)S(1)} %shard_map.63.own), channel_id=1, source_target_pairs={{0,1},{1,0},{2,3},{3,2},{4,5},{5,4},{6,7},{7,6},{8,9},{9,8},{10,11... | collective-permute-start | bytes 1105928 | tf_op jit(solution)/shard_map/ppermute | solution.py:404
  41.1 18.3 %all-to-all-start.1 = ((bf16[16,7,16,128]{3,2,1,0:T(8,128)(2,1)}), bf16[16,7,16,128]{3,2,1,0:T(8,128)(2,1)S(1)}, u32[]{:S(2)}, u32[]{:S(2)}) async-start(bf16[16,7,16,128]{3,2,1,0:T(8,128)(2,1)} %get-tuple-element.40), calls=%async_computation.1 | async-start | bytes 917504 | tf_op jit(solution)/shard_map/all_to_all | solution.py:430
  47.8 5.7 %collective-permute-start.5 = (bf16[2,10,16,128]{3,2,1,0:T(8,128)(2,1)S(1)}, bf16[2,10,16,128]{3,2,1,0:T(8,128)(2,1)S(1)}, u32[]{:S(2)}, u32[]{:S(2)}) collective-permute-start(bf16[2,10,16,128]{3,2,1,0:T(8,128)(2,1)S(1)} %slice.3), channel_id=1, source_target_pairs={{32,0},{48,16},{64,32},{80,48},{96,64},{112,80},{128,96},{144,112}... | collective-permute-start | bytes 245768 | tf_op jit(solution)/shard_map/ppermute | solution.py:431
  54.6 23.7 %collective-permute-start.6 = (bf16[2,8,16,256]{3,2,1,0:T(8,128)(2,1)S(1)}, bf16[2,8,16,256]{3,2,1,0:T(8,128)(2,1)S(1)}, u32[]{:S(2)}, u32[]{:S(2)}) collective-permute-start(bf16[2,8,16,256]{3,2,1,0:T(8,128)(2,1)S(1)} %get-tuple-element.36._), channel_id=1, source_target_pairs={{0,16},{16,0},{32,48},{48,32},{64,80},{80,64},{96,112},{112,96},{1... | collective-permute-start | bytes 393224 | tf_op jit(solution)/shard_map/ppermute | solution.py:451
  60.1 24.5 %all-to-all-start.2 = ((bf16[16,16,128]{2,1,0:T(8,128)(2,1)}), bf16[16,16,128]{2,1,0:T(8,128)(2,1)S(1)}, u32[]{:S(2)}, u32[]{:S(2)}) async-start(bf16[16,16,128]{2,1,0:T(8,128)(2,1)} %shard_map.70), calls=%async_computation.2 | async-start | bytes 131072 | tf_op jit(solution)/shard_map/all_to_all | solution.py:450
  78.3 5.5 %collective-permute-start.7 = (f32[2,4,16,256]{3,2,1,0:T(8,128)S(1)}, f32[2,4,16,256]{3,2,1,0:T(8,128)S(1)}, u32[]{:S(2)}, u32[]{:S(2)}) collective-permute-start(f32[2,4,16,256]{3,2,1,0:T(8,128)S(1)} %get-tuple-element.38), channel_id=1, source_target_pairs={{0,1},{1,0},{2,3},{3,2},{4,5},{5,4},{6,7},{7,6},{8,9},{9,8},{10,11... | collective-permute-start | bytes 393224 | tf_op jit(solution)/shard_map/ppermute | solution.py:457

commit v9 on v6

--- a/solution.py
+++ b/solution.py
@@ -69,7 +69,7 @@
 
 
 def own_channel(place, x, core):
-    return (2 * (place // 8) + core) * 16 + 8 * x + place % 8
+    return (2 * (place >> 3) + core) * 16 + 8 * x + (place & 7)
 
 
 def filter_pieces_kernel(second, out):
@@ -77,7 +77,7 @@
     x = lax.axis_index("tm") % 2
     row = lax.broadcasted_iota(jnp.int32, (chans, 2 * OWN), 0)
     col = lax.broadcasted_iota(jnp.int32, (chans, 2 * OWN), 1)
-    order = jnp.where(own_channel(col % OWN, x, col // OWN) == row, 1.0, 0.0).astype(BF16)
+    order = jnp.where(own_channel(col & (OWN - 1), x, col >> 6) == row, 1.0, 0.0).astype(BF16)
     moved = mm(second[...].reshape(taps * depth, chans), order).astype(BF16)
     moved = moved.reshape(taps, depth, 2 * OWN)
     for place in range(0, len(TAP_ORDER), 2):
@@ -94,7 +94,7 @@
     x, core = lax.axis_index("tm") % 2, lax.axis_index("height") % CORES
     row = lax.broadcasted_iota(jnp.int32, (chans, 2 * OWN), 0)
     col = lax.broadcasted_iota(jnp.int32, (chans, 2 * OWN), 1)
-    pick = jnp.where(own_channel(col % OWN, x, core) == row, 1.0, 0.0).astype(BF16)
+    pick = jnp.where(own_channel(col & (OWN - 1), x, core) == row, 1.0, 0.0).astype(BF16)
     twice = mm(first[...], pick)
     lane = lax.broadcasted_iota(jnp.int32, (128, 2 * OWN), 1)
     for ab in range(9):
@@ -180,12 +180,12 @@
             ext[base + HALF_HIGH - 1, :, lanes] = below[12 + t, subs]
     units = ext.shape[0]
     flat = ext[...].reshape(units * 16, 256)
-    shift = one_hot(units * 16, units * 16, lambda r: jnp.where(r % 16 == 15, -1, r + 1))
+    shift = one_hot(units * 16, units * 16, lambda r: jnp.where((r & 15) == 15, -1, r + 1))
     ups[0] = flat.reshape(units, 16, 256)
     ups[1] = mm(shift, flat).astype(BF16).reshape(units, 16, 256)
 
     def column(r):
-        s, unit, w = r // 128, (r // 16) % 8, 2 * (r % 16) + r // 128 - 1
+        unit, w = (r >> 4) & 7, 2 * (r & 15) + (r >> 7) - 1
         return jnp.where((w >= 0) & (w < 32), unit * 32 + w, -1)
 
     matrix = one_hot(512, 256, column)
@@ -204,6 +204,8 @@
         win = jnp.concatenate([wide[x + 2 : x + 2 + SPAN] for x in tops], 0)
         prod = mm(win.reshape(FRAMES * SPAN * 16, 512), filters[a, :, 4 * OWN :])
         total = total + prod.reshape(FRAMES, SPAN, 16, 2 * OWN)
+    sig = jax.nn.sigmoid(total)
+    total = sig * (1.0 + total * (1.0 - sig))
     for f in range(FRAMES):
         for r in range(SPAN):
             pre[f % 2, r % 2, f // 2, r // 2] = total[f, r]
@@ -229,8 +231,7 @@
     for (fp, ip), act in even.items():
         act = act + jnp.concatenate([blank, odd[fp, ip]], 1)
         x = pre[fp, ip].reshape(32 * HALF, 2 * OWN)
-        sig = jax.nn.sigmoid(x)
-        g = (act * sig * (1.0 + x * (1.0 - sig))).reshape(2, HALF, 16, 2 * OWN)
+        g = (act * x).reshape(2, HALF, 16, 2 * OWN)
         for q in range(2):
             for p in range(HALF):
                 piece, r = g[q, p], 2 * p + ip
@@ -253,7 +254,7 @@
     strips.append(jnp.zeros_like(strips[0]))
     row = lax.broadcasted_iota(jnp.int32, (256, 256), 0)
     col = lax.broadcasted_iota(jnp.int32, (256, 256), 1)
-    x, tap, z, e = col // 128, (col // 64) % 2, (col // 4) % 16, col % 4
+    x, tap, z, e = col >> 7, (col >> 6) & 1, (col >> 2) & 15, col & 3
     order = jnp.where(tap * 128 + 8 * z + 4 * x + e == row, 1.0, 0.0).astype(BF16)
     blocks = OWN // 8
     for k in range(7):
@@ -303,8 +304,8 @@
                     piece = jnp.zeros((OWN, 128), BF16)
                 filters[ab, slot * OWN : (slot + 1) * OWN, jp * 128 : (jp + 1) * 128] = piece
     lane = lax.broadcasted_iota(jnp.int32, (192, 2 * OWN), 1)
-    up = one_hot(192, 192, lambda r: jnp.where(r % 16 == 15, -1, r + 1))
-    down = one_hot(192, 192, lambda r: jnp.where(r % 16 == 0, -1, r - 1))
+    up = one_hot(192, 192, lambda r: jnp.where((r & 15) == 15, -1, r + 1))
+    down = one_hot(192, 192, lambda r: jnp.where((r & 15) == 0, -1, r - 1))
     for f in range(FRAMES + 2):
         src = grad[f] if f < FRAMES else following[f - FRAMES]
         wide[f * SPAN : (f + 1) * SPAN, :, : 2 * OWN] = src
@@ -333,8 +334,8 @@
 
 def join_kernel(kept, got, out, mark):
     total = (kept[...] + got[...]).astype(BF16).reshape(128, 256)
-    low = one_hot(256, 128, lambda r: jnp.where(r % 2 == 0, (r // 32) * 16 + (r % 32) // 2, -1))
-    high = one_hot(256, 128, lambda r: jnp.where(r % 2 == 1, (r // 32) * 16 + (r % 32) // 2, -1))
+    low = one_hot(256, 128, lambda r: jnp.where((r & 1) == 0, (r >> 5) * 16 + ((r & 31) >> 1), -1))
+    high = one_hot(256, 128, lambda r: jnp.where((r & 1) == 1, (r >> 5) * 16 + ((r & 31) >> 1), -1))
     moved = mm(low, total[:, :128]) + mm(high, total[:, 128:])
     out[...] = moved.astype(BF16).reshape(out.shape)
     mark[...] = jnp.zeros_like(mark)

time: 86 us -> 86 us (level)
  no operation moved by 1% of the time
where the time goes in v9:
time: 86 us; the launch traced here: 85.4 us
  starting transfers between devices  59.4 us (69%)
  waiting for transfers between devices  12.1 us (14%)
  Pallas kernels  10.6 us (12%)
  local copies, waits for them, and re-layouts  2.49 us (3%)
    all_to_all x1, starting transfers between devices, body(): summed = lax.all_to_all(sums, 'tm', 0, 0, axis_index_groups=columns)  18.1 us
    pallas_call x13, Pallas kernels, call(): pl.pallas_call(kernel, out_shape=tuple(out), in_specs=[far if i in idle e...  10.6 us
    all_to_all x1, starting transfers between devices, body(): second = lax.all_to_all(pieces, 'height', 0, 0).reshape(chans, 27 * OWN)  7.31 us
    all_to_all x1, starting transfers between devices, body(): lax.all_to_all(parts, ('tm', 'height'), 0, 0, axis_index_groups=planes)  6.69 us
    ppermute x1, starting transfers between devices, body(): got = lax.ppermute(send, 'tm', blocks)  4.78 us
    ppermute x1, starting transfers between devices, body(): pair = lax.ppermute(here, 'tm', blocks)  4.66 us
    ppermute x1, starting transfers between devices, body(): edge = lax.ppermute(edge, 'height', near_pairs)  4.59 us
    ppermute x1, starting transfers between devices, body(): got = lax.ppermute(send, 'height', siblings)  4.54 us
  transfers between devices with their start and end apart: 11, of which 5 were waited for; matrix products, arithmetic and copies ran while one was open for 0% of the time, Pallas kernels for 9%

profile of v9, /device:TPU:1, one launch (start us, length us, event | category | flops | bytes accessed | tf_op | source)
XLA Modules:
  0.0 85.4 jit_solution(711962272506948004)
XLA Ops:
  0.6 0.0 copy-start.2
  0.6 0.8 copy-done.2
  1.5 0.0 copy-start.3
  1.5 0.7 copy-done.3
  2.2 4.6 %collective-permute-start = (bf16[5,32,128]{2,1,0:T(8,128)(2,1)S(1)}, bf16[5,32,128]{2,1,0:T(8,128)(2,1)S(1)}, u32[]{:S(2)}, u32[]{:S(2)}) collective-permute-start(bf16[5,32,128]{2,1,0:T(8,128)(2,1)S(1)} %get-tuple-element.23), channel_id=1, source_target_pairs={{1,2},{2,1},{3,4},{4,3},{5,6},{6,5},{7,8},{8,7},{9,10},{10,9},{11,... | collective-permute-start | bytes 122888 | tf_op jit(solution)/shard_map/ppermute | solution.py:362
  6.8 0.0 copy-start.1
  6.8 0.9 %copy-done.1 = bf16[3,3,3,256,16]{3,4,2,1,0:T(8,128)(2,1)S(1)} copy-done((bf16[3,3,3,256,16]{3,4,2,1,0:T(8,128)(2,1)S(1)}, bf16[3,3,3,256,16]{3,4,2,1,0:T(8,128)(2,1)}, u32[]{:S(2)}) %copy-start.1) | copy-done | bytes 221208
  7.8 1.3 %shard_map.60._ = bf16[16,16,1728]{2,1,0:T(8,128)(2,1)} custom-call(bf16[27,16,256]{2,1,0:T(8,128)(2,1)S(1)} %bitcast.8), custom_call_target="tpu_custom_call" | custom-call | flops 28311552 | bytes 1105920 | tf_op jit(solution)/shard_map/pallas_call | solution.py:55
  9.1 0.0 collective-permute-done.edge
  9.1 0.2 shard_map.61
  9.2 4.7 %collective-permute-start.1 = (bf16[15,32,128]{2,1,0:T(8,128)(2,1)S(1)}, bf16[15,32,128]{2,1,0:T(8,128)(2,1)S(1)}, u32[]{:S(2)}, u32[]{:S(2)}) collective-permute-start(bf16[15,32,128]{2,1,0:T(8,128)(2,1)S(1)} %get-tuple-element.24.here), channel_id=1, source_target_pairs={{0,16},{16,0},{32,48},{48,32},{64,80},{80,64},{96,112},{112,96},{1... | collective-permute-start | bytes 368648 | tf_op jit(solution)/shard_map/ppermute | solution.py:380
  13.9 2.8 %collective-permute-done.1.pair = bf16[15,32,128]{2,1,0:T(8,128)(2,1)S(1)} collective-permute-done((bf16[15,32,128]{2,1,0:T(8,128)(2,1)S(1)}, bf16[15,32,128]{2,1,0:T(8,128)(2,1)S(1)}, u32[]{:S(2)}, u32[]{:S(2)}) %collective-permute-start.1) | collective-permute-done | bytes 122912 | tf_op jit(solution)/shard_map/ppermute | solution.py:380
  16.7 0.0 copy-start
  16.8 7.3 %all-to-all-start = ((bf16[16,16,1728]{2,1,0:T(8,128)(2,1)}), bf16[16,16,1728]{2,1,0:T(8,128)(2,1)S(1)}, u32[]{:S(2)}, u32[]{:S(2)}) async-start(bf16[16,16,1728]{2,1,0:T(8,128)(2,1)} %get-tuple-element.26), calls=%async_computation | async-start | bytes 1835008 | tf_op jit(solution)/shard_map/all_to_all | solution.py:388
  24.1 3.2 %collective-permute-start.2 = (bf16[12,32,128]{2,1,0:T(8,128)(2,1)S(1)}, bf16[12,32,128]{2,1,0:T(8,128)(2,1)S(1)}, u32[]{:S(2)}, u32[]{:S(2)}) collective-permute-start(bf16[12,32,128]{2,1,0:T(8,128)(2,1)S(1)} %get-tuple-element.27), channel_id=1, source_target_pairs={{0,32},{16,48},{32,64},{48,80},{64,96},{80,112},{96,128},{112,144}... | collective-permute-start | bytes 294920 | tf_op jit(solution)/shard_map/ppermute | solution.py:391
  27.3 1.3 %collective-permute-start.3 = (bf16[3,32,128]{2,1,0:T(8,128)(2,1)S(1)}, bf16[3,32,128]{2,1,0:T(8,128)(2,1)S(1)}, u32[]{:S(2)}, u32[]{:S(2)}) collective-permute-start(bf16[3,32,128]{2,1,0:T(8,128)(2,1)S(1)} %get-tuple-element.28), channel_id=1, source_target_pairs={{32,0},{48,16},{64,32},{80,48},{96,64},{112,80},{128,96},{144,112}... | collective-permute-start | bytes 73736 | tf_op jit(solution)/shard_map/ppermute | solution.py:392
  28.6 3.8 %collective-permute-done.3.after = bf16[3,32,128]{2,1,0:T(8,128)(2,1)S(1)} collective-permute-done((bf16[3,32,128]{2,1,0:T(8,128)(2,1)S(1)}, bf16[3,32,128]{2,1,0:T(8,128)(2,1)S(1)}, u32[]{:S(2)}, u32[]{:S(2)}) %collective-permute-start.3) | collective-permute-done | bytes 24608 | tf_op jit(solution)/shard_map/ppermute | solution.py:392
  32.3 0.0 collective-permute-done.2.before
  32.3 0.1 shard_map.63.own
  32.4 2.9 %collective-permute-start.4 = (bf16[45,32,128]{2,1,0:T(8,128)(2,1)S(1)}, bf16[45,32,128]{2,1,0:T(8,128)(2,1)S(1)}, u32[]{:S(2)}, u32[]{:S(2)}) collective-permute-start(bf16[45,32,128]{2,1,0:T(8,128)(2,1)S(1)} %shard_map.63.own), channel_id=1, source_target_pairs={{0,1},{1,0},{2,3},{3,2},{4,5},{5,4},{6,7},{7,6},{8,9},{9,8},{10,11... | collective-permute-start | bytes 1105928 | tf_op jit(solution)/shard_map/ppermute | solution.py:405
  35.3 0.0 copy-done
  35.3 1.1 %shard_map.64 = (bf16[3,512,384]{2,1,0:T(8,128)(2,1)S(1)}, bf16[64,3456]{1,0:T(8,128)(2,1)S(1)}) custom-call(bf16[3456,256]{1,0:T(8,128)(2,1)S(1)} %bitcast.7), custom_call_target="tpu_custom_call" | custom-call | flops 339738624 | bytes 3391488 | tf_op jit(solution)/shard_map/pallas_call | solution.py:55
  36.5 0.2 collective-permute-done.4.other
  36.6 2.1 %shard_map.65 = (bf16[72,16,512]{2,1,0:T(8,128)(2,1)S(1)}, bf16[2,18,16,256]{3,2,1,0:T(8,128)(2,1)S(1)}, f32[2,2,2,5,16,128]{5,4,3,2,1,0:T(8,128)S(1)}) custom-call(bf16[45,32,128]{2,1,0:T(8,128)(2,1)S(1)} %shard_map.63.own, bf16[45,32,128]{2,1,0:T(8,128)(2,1)S(1)} %collective-permute-done.4.other, bf16[3,512,384]{2,1,0:T(8,128)(2,1)S(1)} %get-tuple-element.29.filters), custom_call_target="tpu_custom_call" | custom-call | flops 754974720 | bytes 3719168 | tf_op jit(solution)/shard_map/pallas_call | solution.py:55
  38.7 0.0 all-to-all-done
  38.7 2.4 %shard_map.66 = (bf16[4,10,16,128]{3,2,1,0:T(8,128)(2,1)S(1)}, bf16[16,7,16,128]{3,2,1,0:T(8,128)(2,1)}) custom-call(bf16[256,1728]{1,0:T(8,128)(2,1)S(1)} %bitcast.6, bf16[2,18,16,256]{3,2,1,0:T(8,128)(2,1)S(1)} %get-tuple-element.30.ups, f32[2,2,2,5,16,128]{5,4,3,2,1,0:T(8,128)S(1)} %get-tuple-element.31.pre, bf16[72,16,512]{2,1,0:T(8,128)(2,1)S(1)} %get-tuple-element.32.wide), custom_call_target="tpu_custom_call" | custom-call | flops 603979776 | bytes 3309568 | tf_op jit(solution)/shard_map/pallas_call | solution.py:55
  41.1 6.7 %all-to-all-start.1 = ((bf16[16,7,16,128]{3,2,1,0:T(8,128)(2,1)}), bf16[16,7,16,128]{3,2,1,0:T(8,128)(2,1)S(1)}, u32[]{:S(2)}, u32[]{:S(2)}) async-start(bf16[16,7,16,128]{3,2,1,0:T(8,128)(2,1)} %get-tuple-element.40), calls=%async_computation.1 | async-start | bytes 917504 | tf_op jit(solution)/shard_map/all_to_all | solution.py:431
  47.8 1.3 %collective-permute-start.5 = (bf16[2,10,16,128]{3,2,1,0:T(8,128)(2,1)S(1)}, bf16[2,10,16,128]{3,2,1,0:T(8,128)(2,1)S(1)}, u32[]{:S(2)}, u32[]{:S(2)}) collective-permute-start(bf16[2,10,16,128]{3,2,1,0:T(8,128)(2,1)S(1)} %slice.3), channel_id=1, source_target_pairs={{32,0},{48,16},{64,32},{80,48},{96,64},{112,80},{128,96},{144,112}... | collective-permute-start | bytes 245768 | tf_op jit(solution)/shard_map/ppermute | solution.py:432
  49.1 4.4 %collective-permute-done.5.following = bf16[2,10,16,128]{3,2,1,0:T(8,128)(2,1)S(1)} collective-permute-done((bf16[2,10,16,128]{3,2,1,0:T(8,128)(2,1)S(1)}, bf16[2,10,16,128]{3,2,1,0:T(8,128)(2,1)S(1)}, u32[]{:S(2)}, u32[]{:S(2)}) %collective-permute-start.5) | collective-permute-done | bytes 81952 | tf_op jit(solution)/shard_map/ppermute | solution.py:432
  53.4 1.1 %shard_map.67 = (f32[2,8,16,256]{3,2,1,0:T(8,128)S(1)}, bf16[2,8,16,256]{3,2,1,0:T(8,128)(2,1)S(1)}) custom-call(bf16[4,10,16,128]{3,2,1,0:T(8,128)(2,1)S(1)} %get-tuple-element.33.grad, bf16[2,10,16,128]{3,2,1,0:T(8,128)(2,1)S(1)} %collective-permute-done.5.following, bf16[64,3456]{1,0:T(8,128)(2,1)S(1)} %get-tuple-element.34.flat), custom_call_target="tpu_custom_call" | custom-call | flops 603979776 | bytes 1081344 | tf_op jit(solution)/shard_map/pallas_call | solution.py:55
  54.6 4.8 %collective-permute-start.6 = (bf16[2,8,16,256]{3,2,1,0:T(8,128)(2,1)S(1)}, bf16[2,8,16,256]{3,2,1,0:T(8,128)(2,1)S(1)}, u32[]{:S(2)}, u32[]{:S(2)}) collective-permute-start(bf16[2,8,16,256]{3,2,1,0:T(8,128)(2,1)S(1)} %get-tuple-element.36._), channel_id=1, source_target_pairs={{0,16},{16,0},{32,48},{48,32},{64,80},{80,64},{96,112},{112,96},{1... | collective-permute-start | bytes 393224 | tf_op jit(solution)/shard_map/ppermute | solution.py:452
  59.3 0.0 all-to-all-done.1.parts
  59.3 0.8 shard_map.70
  60.1 18.1 %all-to-all-start.2 = ((bf16[16,16,128]{2,1,0:T(8,128)(2,1)}), bf16[16,16,128]{2,1,0:T(8,128)(2,1)S(1)}, u32[]{:S(2)}, u32[]{:S(2)}) async-start(bf16[16,16,128]{2,1,0:T(8,128)(2,1)} %shard_map.70), calls=%async_computation.2 | async-start | bytes 131072 | tf_op jit(solution)/shard_map/all_to_all | solution.py:451
  78.2 0.0 collective-permute-done.6.got
  78.3 4.5 %collective-permute-start.7 = (f32[2,4,16,256]{3,2,1,0:T(8,128)S(1)}, f32[2,4,16,256]{3,2,1,0:T(8,128)S(1)}, u32[]{:S(2)}, u32[]{:S(2)}) collective-permute-start(f32[2,4,16,256]{3,2,1,0:T(8,128)S(1)} %get-tuple-element.38), channel_id=1, source_target_pairs={{0,1},{1,0},{2,3},{3,2},{4,5},{5,4},{6,7},{7,6},{8,9},{9,8},{10,11... | collective-permute-start | bytes 393224 | tf_op jit(solution)/shard_map/ppermute | solution.py:458
  82.8 1.0 %collective-permute-done.7.got = f32[2,4,16,256]{3,2,1,0:T(8,128)S(1)} collective-permute-done((f32[2,4,16,256]{3,2,1,0:T(8,128)S(1)}, f32[2,4,16,256]{3,2,1,0:T(8,128)S(1)}, u32[]{:S(2)}, u32[]{:S(2)}) %collective-permute-start.7) | collective-permute-done | bytes 131104 | tf_op jit(solution)/shard_map/ppermute | solution.py:458
  83.8 0.8 shard_map.69
  84.6 0.0 all-to-all-done.2.parts
  84.6 0.7 shard_map.71
  (4 shorter events, 0.1 us)
Async XLA Ops:
  0.6 0.8 copy-start.2
  1.5 0.7 copy-start.3
  2.2 6.8 %collective-permute-start = (bf16[5,32,128]{2,1,0:T(8,128)(2,1)S(1)}, bf16[5,32,128]{2,1,0:T(8,128)(2,1)S(1)}, u32[]{:S(2)}, u32[]{:S(2)}) collective-permute-start(bf16[5,32,128]{2,1,0:T(8,128)(2,1)S(1)} %get-tuple-element.23), channel_id=1, source_target_pairs={{1,2},{2,1},{3,4},{4,3},{5,6},{6,5},{7,8},{8,7},{9,10},{10,9},{11,... | collective-permute-start | bytes 122888 | tf_op jit(solution)/shard_map/ppermute | solution.py:362
  6.8 0.9 %copy-start.1 = (bf16[3,3,3,256,16]{3,4,2,1,0:T(8,128)(2,1)S(1)}, bf16[3,3,3,256,16]{3,4,2,1,0:T(8,128)(2,1)}, u32[]{:S(2)}) copy-start(bf16[3,3,3,256,16]{3,4,2,1,0:T(8,128)(2,1)} %param.6) | copy-start | bytes 663556
  9.2 7.5 %collective-permute-start.1 = (bf16[15,32,128]{2,1,0:T(8,128)(2,1)S(1)}, bf16[15,32,128]{2,1,0:T(8,128)(2,1)S(1)}, u32[]{:S(2)}, u32[]{:S(2)}) collective-permute-start(bf16[15,32,128]{2,1,0:T(8,128)(2,1)S(1)} %get-tuple-element.24.here), channel_id=1, source_target_pairs={{0,16},{16,0},{32,48},{48,32},{64,80},{80,64},{96,112},{112,96},{1... | collective-permute-start | bytes 368648 | tf_op jit(solution)/shard_map/ppermute | solution.py:380
  16.7 18.6 %copy-start = (bf16[3,3,3,128,256]{4,3,2,1,0:T(8,128)(2,1)S(1)}, bf16[3,3,3,128,256]{4,3,2,1,0:T(8,128)(2,1)}, u32[]{:S(2)}) copy-start(bf16[3,3,3,128,256]{4,3,2,1,0:T(8,128)(2,1)} %param.5) | copy-start | bytes 5308420
  16.8 21.9 %all-to-all-start = ((bf16[16,16,1728]{2,1,0:T(8,128)(2,1)}), bf16[16,16,1728]{2,1,0:T(8,128)(2,1)S(1)}, u32[]{:S(2)}, u32[]{:S(2)}) async-start(bf16[16,16,1728]{2,1,0:T(8,128)(2,1)} %get-tuple-element.26), calls=%async_computation | async-start | bytes 1835008 | tf_op jit(solution)/shard_map/all_to_all | solution.py:388
  24.1 8.2 %collective-permute-start.2 = (bf16[12,32,128]{2,1,0:T(8,128)(2,1)S(1)}, bf16[12,32,128]{2,1,0:T(8,128)(2,1)S(1)}, u32[]{:S(2)}, u32[]{:S(2)}) collective-permute-start(bf16[12,32,128]{2,1,0:T(8,128)(2,1)S(1)} %get-tuple-element.27), channel_id=1, source_target_pairs={{0,32},{16,48},{32,64},{48,80},{64,96},{80,112},{96,128},{112,144}... | collective-permute-start | bytes 294920 | tf_op jit(solution)/shard_map/ppermute | solution.py:391
  27.3 5.1 %collective-permute-start.3 = (bf16[3,32,128]{2,1,0:T(8,128)(2,1)S(1)}, bf16[3,32,128]{2,1,0:T(8,128)(2,1)S(1)}, u32[]{:S(2)}, u32[]{:S(2)}) collective-permute-start(bf16[3,32,128]{2,1,0:T(8,128)(2,1)S(1)} %get-tuple-element.28), channel_id=1, source_target_pairs={{32,0},{48,16},{64,32},{80,48},{96,64},{112,80},{128,96},{144,112}... | collective-permute-start | bytes 73736 | tf_op jit(solution)/shard_map/ppermute | solution.py:392
  32.4 4.2 %collective-permute-start.4 = (bf16[45,32,128]{2,1,0:T(8,128)(2,1)S(1)}, bf16[45,32,128]{2,1,0:T(8,128)(2,1)S(1)}, u32[]{:S(2)}, u32[]{:S(2)}) collective-permute-start(bf16[45,32,128]{2,1,0:T(8,128)(2,1)S(1)} %shard_map.63.own), channel_id=1, source_target_pairs={{0,1},{1,0},{2,3},{3,2},{4,5},{5,4},{6,7},{7,6},{8,9},{9,8},{10,11... | collective-permute-start | bytes 1105928 | tf_op jit(solution)/shard_map/ppermute | solution.py:405
  41.1 18.3 %all-to-all-start.1 = ((bf16[16,7,16,128]{3,2,1,0:T(8,128)(2,1)}), bf16[16,7,16,128]{3,2,1,0:T(8,128)(2,1)S(1)}, u32[]{:S(2)}, u32[]{:S(2)}) async-start(bf16[16,7,16,128]{3,2,1,0:T(8,128)(2,1)} %get-tuple-element.40), calls=%async_computation.1 | async-start | bytes 917504 | tf_op jit(solution)/shard_map/all_to_all | solution.py:431
  47.8 5.7 %collective-permute-start.5 = (bf16[2,10,16,128]{3,2,1,0:T(8,128)(2,1)S(1)}, bf16[2,10,16,128]{3,2,1,0:T(8,128)(2,1)S(1)}, u32[]{:S(2)}, u32[]{:S(2)}) collective-permute-start(bf16[2,10,16,128]{3,2,1,0:T(8,128)(2,1)S(1)} %slice.3), channel_id=1, source_target_pairs={{32,0},{48,16},{64,32},{80,48},{96,64},{112,80},{128,96},{144,112}... | collective-permute-start | bytes 245768 | tf_op jit(solution)/shard_map/ppermute | solution.py:432
  54.6 23.7 %collective-permute-start.6 = (bf16[2,8,16,256]{3,2,1,0:T(8,128)(2,1)S(1)}, bf16[2,8,16,256]{3,2,1,0:T(8,128)(2,1)S(1)}, u32[]{:S(2)}, u32[]{:S(2)}) collective-permute-start(bf16[2,8,16,256]{3,2,1,0:T(8,128)(2,1)S(1)} %get-tuple-element.36._), channel_id=1, source_target_pairs={{0,16},{16,0},{32,48},{48,32},{64,80},{80,64},{96,112},{112,96},{1... | collective-permute-start | bytes 393224 | tf_op jit(solution)/shard_map/ppermute | solution.py:452
  60.1 24.5 %all-to-all-start.2 = ((bf16[16,16,128]{2,1,0:T(8,128)(2,1)}), bf16[16,16,128]{2,1,0:T(8,128)(2,1)S(1)}, u32[]{:S(2)}, u32[]{:S(2)}) async-start(bf16[16,16,128]{2,1,0:T(8,128)(2,1)} %shard_map.70), calls=%async_computation.2 | async-start | bytes 131072 | tf_op jit(solution)/shard_map/all_to_all | solution.py:451
  78.3 5.5 %collective-permute-start.7 = (f32[2,4,16,256]{3,2,1,0:T(8,128)S(1)}, f32[2,4,16,256]{3,2,1,0:T(8,128)S(1)}, u32[]{:S(2)}, u32[]{:S(2)}) collective-permute-start(f32[2,4,16,256]{3,2,1,0:T(8,128)S(1)} %get-tuple-element.38), channel_id=1, source_target_pairs={{0,1},{1,0},{2,3},{3,2},{4,5},{5,4},{6,7},{7,6},{8,9},{9,8},{10,11... | collective-permute-start | bytes 393224 | tf_op jit(solution)/shard_map/ppermute | solution.py:458

commit v10 on v9

--- a/solution.py
+++ b/solution.py
@@ -320,20 +320,20 @@
             win = jnp.concatenate([wide[x : x + ROWS] for x in tops], 0)
             total = total + mm(win.reshape(FRAMES * ROWS * 16, 4 * OWN), filters[a * 3 + b])
     total = total.reshape(FRAMES, ROWS, 16, 256)
+    even = lax.axis_index("height") % CORES == 0
+    keep[...] = jnp.where(even, total[:, :4], total[:, 4:])
+    send[...] = jnp.where(even, total[:, 4:], total[:, :4])
+
+
+def halve_kernel(kept, got, keep, send):
+    total = kept[...] + got[...]
     first = lax.axis_index("tm") % 2 == 0
     keep[...] = jnp.where(first, total[:2], total[2:])
     send[...] = jnp.where(first, total[2:], total[:2]).astype(BF16)
 
 
-def halve_kernel(kept, got, keep, send):
-    total = kept[...] + got[...].astype(F32)
-    even = lax.axis_index("height") % CORES == 0
-    keep[...] = jnp.where(even, total[:, :4], total[:, 4:])
-    send[...] = jnp.where(even, total[:, 4:], total[:, :4])
-
-
 def join_kernel(kept, got, out, mark):
-    total = (kept[...] + got[...]).astype(BF16).reshape(128, 256)
+    total = (kept[...] + got[...].astype(F32)).astype(BF16).reshape(128, 256)
     low = one_hot(256, 128, lambda r: jnp.where((r & 1) == 0, (r >> 5) * 16 + ((r & 31) >> 1), -1))
     high = one_hot(256, 128, lambda r: jnp.where((r & 1) == 1, (r >> 5) * 16 + ((r & 31) >> 1), -1))
     moved = mm(low, total[:, :128]) + mm(high, total[:, 128:])
@@ -432,7 +432,7 @@
     following = lax.ppermute(grad_pre[:2], "tm", back)
     keep, send = call(
         clip_kernel,
-        [shaped((2, ROWS, 16, 2 * cin), F32), shaped((2, ROWS, 16, 2 * cin), BF16)],
+        [shaped((FRAMES, rows, 16, 2 * cin), F32)] * 2,
         [grad_pre, following, flat],
         scratch=[
             pltpu.VMEM(((FRAMES + 2) * SPAN, 16, 4 * OWN), BF16),
@@ -449,13 +449,13 @@
     )
     columns = [[2 * ((i + 8) % lines) + x for i in range(lines)] for x in range(2)]
     summed = lax.all_to_all(sums, "tm", 0, 0, axis_index_groups=columns)
-    got = lax.ppermute(send, "tm", blocks)
+    got = lax.ppermute(send, "height", siblings)
     keep, send = call(
         halve_kernel,
-        [shaped((2, rows, 16, 2 * cin), F32)] * 2,
+        [shaped((2, rows, 16, 2 * cin), F32), shaped((2, rows, 16, 2 * cin), BF16)],
         [keep, got],
     )
-    got = lax.ppermute(send, "height", siblings)
+    got = lax.ppermute(send, "tm", blocks)
     grad_clip, mark = call(
         join_kernel, [shaped(clip.shape, BF16), shaped((8, 128), F32)], [keep, got]
     )

time: 86 us -> 86.3 us (level)
  starting transfers between devices: 59.4 us -> 58.5 us
    ppermute x1, waiting for transfers between devices: 0.01 us -> 1.64 us  [body(): got = lax.ppermute(send, 'tm', blocks)]
    ppermute x1, starting transfers between devices: 4.54 us -> 3.23 us  [body(): got = lax.ppermute(send, 'height', siblings)]
    ppermute x1, waiting for transfers between devices: 0.96 us -> 0.01 us  [body(): got = lax.ppermute(send, 'height', siblings)]
where the time goes in v10:
time: 86.3 us; the launch traced here: 85.2 us
  starting transfers between devices  58.5 us (68%)
  waiting for transfers between devices  12.7 us (15%)
  Pallas kernels  10.6 us (12%)
  local copies, waits for them, and re-layouts  2.49 us (3%)
    all_to_all x1, starting transfers between devices, body(): summed = lax.all_to_all(sums, 'tm', 0, 0, axis_index_groups=columns)  18.3 us
    pallas_call x13, Pallas kernels, call(): pl.pallas_call(kernel, out_shape=tuple(out), in_specs=[far if i in idle e...  10.6 us
    all_to_all x1, starting transfers between devices, body(): second = lax.all_to_all(pieces, 'height', 0, 0).reshape(chans, 27 * OWN)  7.31 us
    all_to_all x1, starting transfers between devices, body(): lax.all_to_all(parts, ('tm', 'height'), 0, 0, axis_index_groups=planes)  6.69 us
    ppermute x1, starting transfers between devices, body(): got = lax.ppermute(send, 'tm', blocks)  5.06 us
    ppermute x1, starting transfers between devices, body(): pair = lax.ppermute(here, 'tm', blocks)  4.66 us
    ppermute x1, starting transfers between devices, body(): edge = lax.ppermute(edge, 'height', near_pairs)  4.59 us
    ppermute x1, waiting for transfers between devices, body(): following = lax.ppermute(grad_pre[:2], 'tm', back)  4.36 us
  transfers between devices with their start and end apart: 11, of which 5 were waited for; matrix products, arithmetic and copies ran while one was open for 0% of the time, Pallas kernels for 9%

profile of v10, /device:TPU:1, one launch (start us, length us, event | category | flops | bytes accessed | tf_op | source)
XLA Modules:
  0.0 85.2 jit_solution(4399062029904272931)
XLA Ops:
  0.6 0.0 copy-start.2
  0.6 0.8 copy-done.2
  1.5 0.0 copy-start.3
  1.5 0.7 copy-done.3
  2.2 4.6 %collective-permute-start = (bf16[5,32,128]{2,1,0:T(8,128)(2,1)S(1)}, bf16[5,32,128]{2,1,0:T(8,128)(2,1)S(1)}, u32[]{:S(2)}, u32[]{:S(2)}) collective-permute-start(bf16[5,32,128]{2,1,0:T(8,128)(2,1)S(1)} %get-tuple-element.23), channel_id=1, source_target_pairs={{1,2},{2,1},{3,4},{4,3},{5,6},{6,5},{7,8},{8,7},{9,10},{10,9},{11,... | collective-permute-start | bytes 122888 | tf_op jit(solution)/shard_map/ppermute | solution.py:362
  6.8 0.0 copy-start.1
  6.8 0.9 %copy-done.1 = bf16[3,3,3,256,16]{3,4,2,1,0:T(8,128)(2,1)S(1)} copy-done((bf16[3,3,3,256,16]{3,4,2,1,0:T(8,128)(2,1)S(1)}, bf16[3,3,3,256,16]{3,4,2,1,0:T(8,128)(2,1)}, u32[]{:S(2)}) %copy-start.1) | copy-done | bytes 221208
  7.8 1.3 %shard_map.60._ = bf16[16,16,1728]{2,1,0:T(8,128)(2,1)} custom-call(bf16[27,16,256]{2,1,0:T(8,128)(2,1)S(1)} %bitcast.8), custom_call_target="tpu_custom_call" | custom-call | flops 28311552 | bytes 1105920 | tf_op jit(solution)/shard_map/pallas_call | solution.py:55
  9.1 0.0 collective-permute-done.edge
  9.1 0.2 shard_map.61
  9.2 4.7 %collective-permute-start.1 = (bf16[15,32,128]{2,1,0:T(8,128)(2,1)S(1)}, bf16[15,32,128]{2,1,0:T(8,128)(2,1)S(1)}, u32[]{:S(2)}, u32[]{:S(2)}) collective-permute-start(bf16[15,32,128]{2,1,0:T(8,128)(2,1)S(1)} %get-tuple-element.24.here), channel_id=1, source_target_pairs={{0,16},{16,0},{32,48},{48,32},{64,80},{80,64},{96,112},{112,96},{1... | collective-permute-start | bytes 368648 | tf_op jit(solution)/shard_map/ppermute | solution.py:380
  13.9 2.8 %collective-permute-done.1.pair = bf16[15,32,128]{2,1,0:T(8,128)(2,1)S(1)} collective-permute-done((bf16[15,32,128]{2,1,0:T(8,128)(2,1)S(1)}, bf16[15,32,128]{2,1,0:T(8,128)(2,1)S(1)}, u32[]{:S(2)}, u32[]{:S(2)}) %collective-permute-start.1) | collective-permute-done | bytes 122912 | tf_op jit(solution)/shard_map/ppermute | solution.py:380
  16.7 0.0 copy-start
  16.8 7.3 %all-to-all-start = ((bf16[16,16,1728]{2,1,0:T(8,128)(2,1)}), bf16[16,16,1728]{2,1,0:T(8,128)(2,1)S(1)}, u32[]{:S(2)}, u32[]{:S(2)}) async-start(bf16[16,16,1728]{2,1,0:T(8,128)(2,1)} %get-tuple-element.26), calls=%async_computation | async-start | bytes 1835008 | tf_op jit(solution)/shard_map/all_to_all | solution.py:388
  24.1 3.2 %collective-permute-start.2 = (bf16[12,32,128]{2,1,0:T(8,128)(2,1)S(1)}, bf16[12,32,128]{2,1,0:T(8,128)(2,1)S(1)}, u32[]{:S(2)}, u32[]{:S(2)}) collective-permute-start(bf16[12,32,128]{2,1,0:T(8,128)(2,1)S(1)} %get-tuple-element.27), channel_id=1, source_target_pairs={{0,32},{16,48},{32,64},{48,80},{64,96},{80,112},{96,128},{112,144}... | collective-permute-start | bytes 294920 | tf_op jit(solution)/shard_map/ppermute | solution.py:391
  27.3 1.3 %collective-permute-start.3 = (bf16[3,32,128]{2,1,0:T(8,128)(2,1)S(1)}, bf16[3,32,128]{2,1,0:T(8,128)(2,1)S(1)}, u32[]{:S(2)}, u32[]{:S(2)}) collective-permute-start(bf16[3,32,128]{2,1,0:T(8,128)(2,1)S(1)} %get-tuple-element.28), channel_id=1, source_target_pairs={{32,0},{48,16},{64,32},{80,48},{96,64},{112,80},{128,96},{144,112}... | collective-permute-start | bytes 73736 | tf_op jit(solution)/shard_map/ppermute | solution.py:392
  28.6 3.8 %collective-permute-done.3.after = bf16[3,32,128]{2,1,0:T(8,128)(2,1)S(1)} collective-permute-done((bf16[3,32,128]{2,1,0:T(8,128)(2,1)S(1)}, bf16[3,32,128]{2,1,0:T(8,128)(2,1)S(1)}, u32[]{:S(2)}, u32[]{:S(2)}) %collective-permute-start.3) | collective-permute-done | bytes 24608 | tf_op jit(solution)/shard_map/ppermute | solution.py:392
  32.3 0.0 collective-permute-done.2.before
  32.3 0.1 shard_map.63.own
  32.4 2.9 %collective-permute-start.4 = (bf16[45,32,128]{2,1,0:T(8,128)(2,1)S(1)}, bf16[45,32,128]{2,1,0:T(8,128)(2,1)S(1)}, u32[]{:S(2)}, u32[]{:S(2)}) collective-permute-start(bf16[45,32,128]{2,1,0:T(8,128)(2,1)S(1)} %shard_map.63.own), channel_id=1, source_target_pairs={{0,1},{1,0},{2,3},{3,2},{4,5},{5,4},{6,7},{7,6},{8,9},{9,8},{10,11... | collective-permute-start | bytes 1105928 | tf_op jit(solution)/shard_map/ppermute | solution.py:405
  35.3 0.0 copy-done
  35.3 1.1 %shard_map.64 = (bf16[3,512,384]{2,1,0:T(8,128)(2,1)S(1)}, bf16[64,3456]{1,0:T(8,128)(2,1)S(1)}) custom-call(bf16[3456,256]{1,0:T(8,128)(2,1)S(1)} %bitcast.7), custom_call_target="tpu_custom_call" | custom-call | flops 339738624 | bytes 3391488 | tf_op jit(solution)/shard_map/pallas_call | solution.py:55
  36.5 0.2 collective-permute-done.4.other
  36.6 2.1 %shard_map.65 = (bf16[72,16,512]{2,1,0:T(8,128)(2,1)S(1)}, bf16[2,18,16,256]{3,2,1,0:T(8,128)(2,1)S(1)}, f32[2,2,2,5,16,128]{5,4,3,2,1,0:T(8,128)S(1)}) custom-call(bf16[45,32,128]{2,1,0:T(8,128)(2,1)S(1)} %shard_map.63.own, bf16[45,32,128]{2,1,0:T(8,128)(2,1)S(1)} %collective-permute-done.4.other, bf16[3,512,384]{2,1,0:T(8,128)(2,1)S(1)} %get-tuple-element.29.filters), custom_call_target="tpu_custom_call" | custom-call | flops 754974720 | bytes 3719168 | tf_op jit(solution)/shard_map/pallas_call | solution.py:55
  38.7 0.0 all-to-all-done
  38.7 2.4 %shard_map.66 = (bf16[4,10,16,128]{3,2,1,0:T(8,128)(2,1)S(1)}, bf16[16,7,16,128]{3,2,1,0:T(8,128)(2,1)}) custom-call(bf16[256,1728]{1,0:T(8,128)(2,1)S(1)} %bitcast.6, bf16[2,18,16,256]{3,2,1,0:T(8,128)(2,1)S(1)} %get-tuple-element.30.ups, f32[2,2,2,5,16,128]{5,4,3,2,1,0:T(8,128)S(1)} %get-tuple-element.31.pre, bf16[72,16,512]{2,1,0:T(8,128)(2,1)S(1)} %get-tuple-element.32.wide), custom_call_target="tpu_custom_call" | custom-call | flops 603979776 | bytes 3309568 | tf_op jit(solution)/shard_map/pallas_call | solution.py:55
  41.1 6.7 %all-to-all-start.1 = ((bf16[16,7,16,128]{3,2,1,0:T(8,128)(2,1)}), bf16[16,7,16,128]{3,2,1,0:T(8,128)(2,1)S(1)}, u32[]{:S(2)}, u32[]{:S(2)}) async-start(bf16[16,7,16,128]{3,2,1,0:T(8,128)(2,1)} %get-tuple-element.40), calls=%async_computation.1 | async-start | bytes 917504 | tf_op jit(solution)/shard_map/all_to_all | solution.py:431
  47.8 1.3 %collective-permute-start.5 = (bf16[2,10,16,128]{3,2,1,0:T(8,128)(2,1)S(1)}, bf16[2,10,16,128]{3,2,1,0:T(8,128)(2,1)S(1)}, u32[]{:S(2)}, u32[]{:S(2)}) collective-permute-start(bf16[2,10,16,128]{3,2,1,0:T(8,128)(2,1)S(1)} %slice.3), channel_id=1, source_target_pairs={{32,0},{48,16},{64,32},{80,48},{96,64},{112,80},{128,96},{144,112}... | collective-permute-start | bytes 245768 | tf_op jit(solution)/shard_map/ppermute | solution.py:432
  49.1 4.4 %collective-permute-done.5.following = bf16[2,10,16,128]{3,2,1,0:T(8,128)(2,1)S(1)} collective-permute-done((bf16[2,10,16,128]{3,2,1,0:T(8,128)(2,1)S(1)}, bf16[2,10,16,128]{3,2,1,0:T(8,128)(2,1)S(1)}, u32[]{:S(2)}, u32[]{:S(2)}) %collective-permute-start.5) | collective-permute-done | bytes 81952 | tf_op jit(solution)/shard_map/ppermute | solution.py:432
  53.4 1.1 %shard_map.67 = (f32[4,4,16,256]{3,2,1,0:T(8,128)S(1)}, f32[4,4,16,256]{3,2,1,0:T(8,128)S(1)}) custom-call(bf16[4,10,16,128]{3,2,1,0:T(8,128)(2,1)S(1)} %get-tuple-element.33.grad, bf16[2,10,16,128]{3,2,1,0:T(8,128)(2,1)S(1)} %collective-permute-done.5.following, bf16[64,3456]{1,0:T(8,128)(2,1)S(1)} %get-tuple-element.34.flat), custom_call_target="tpu_custom_call" | custom-call | flops 603979776 | bytes 1212416 | tf_op jit(solution)/shard_map/pallas_call | solution.py:55
  54.6 3.2 %collective-permute-start.6 = (f32[4,4,16,256]{3,2,1,0:T(8,128)S(1)}, f32[4,4,16,256]{3,2,1,0:T(8,128)S(1)}, u32[]{:S(2)}, u32[]{:S(2)}) collective-permute-start(f32[4,4,16,256]{3,2,1,0:T(8,128)S(1)} %get-tuple-element.36._), channel_id=1, source_target_pairs={{0,1},{1,0},{2,3},{3,2},{4,5},{5,4},{6,7},{7,6},{8,9},{9,8},{10,11... | collective-permute-start | bytes 786440 | tf_op jit(solution)/shard_map/ppermute | solution.py:452
  57.8 0.0 all-to-all-done.1.parts
  57.8 0.8 shard_map.70
  58.6 18.3 %all-to-all-start.2 = ((bf16[16,16,128]{2,1,0:T(8,128)(2,1)}), bf16[16,16,128]{2,1,0:T(8,128)(2,1)S(1)}, u32[]{:S(2)}, u32[]{:S(2)}) async-start(bf16[16,16,128]{2,1,0:T(8,128)(2,1)} %shard_map.70), calls=%async_computation.2 | async-start | bytes 131072 | tf_op jit(solution)/shard_map/all_to_all | solution.py:451
  76.9 0.0 collective-permute-done.6.got
  76.9 5.1 %collective-permute-start.7 = (bf16[2,4,16,256]{3,2,1,0:T(8,128)(2,1)S(1)}, bf16[2,4,16,256]{3,2,1,0:T(8,128)(2,1)S(1)}, u32[]{:S(2)}, u32[]{:S(2)}) collective-permute-start(bf16[2,4,16,256]{3,2,1,0:T(8,128)(2,1)S(1)} %get-tuple-element.38), channel_id=1, source_target_pairs={{0,16},{16,0},{32,48},{48,32},{64,80},{80,64},{96,112},{112,96},{1... | collective-permute-start | bytes 196616 | tf_op jit(solution)/shard_map/ppermute | solution.py:458
  82.0 1.6 %collective-permute-done.7.got = bf16[2,4,16,256]{3,2,1,0:T(8,128)(2,1)S(1)} collective-permute-done((bf16[2,4,16,256]{3,2,1,0:T(8,128)(2,1)S(1)}, bf16[2,4,16,256]{3,2,1,0:T(8,128)(2,1)S(1)}, u32[]{:S(2)}, u32[]{:S(2)}) %collective-permute-start.7) | collective-permute-done | bytes 65568 | tf_op jit(solution)/shard_map/ppermute | solution.py:458
  83.6 0.8 shard_map.69
  84.4 0.0 all-to-all-done.2.parts
  84.4 0.7 shard_map.71
  (4 shorter events, 0.1 us)
Async XLA Ops:
  0.6 0.8 copy-start.2
  1.5 0.7 copy-start.3
  2.2 6.8 %collective-permute-start = (bf16[5,32,128]{2,1,0:T(8,128)(2,1)S(1)}, bf16[5,32,128]{2,1,0:T(8,128)(2,1)S(1)}, u32[]{:S(2)}, u32[]{:S(2)}) collective-permute-start(bf16[5,32,128]{2,1,0:T(8,128)(2,1)S(1)} %get-tuple-element.23), channel_id=1, source_target_pairs={{1,2},{2,1},{3,4},{4,3},{5,6},{6,5},{7,8},{8,7},{9,10},{10,9},{11,... | collective-permute-start | bytes 122888 | tf_op jit(solution)/shard_map/ppermute | solution.py:362
  6.8 0.9 %copy-start.1 = (bf16[3,3,3,256,16]{3,4,2,1,0:T(8,128)(2,1)S(1)}, bf16[3,3,3,256,16]{3,4,2,1,0:T(8,128)(2,1)}, u32[]{:S(2)}) copy-start(bf16[3,3,3,256,16]{3,4,2,1,0:T(8,128)(2,1)} %param.6) | copy-start | bytes 663556
  9.2 7.5 %collective-permute-start.1 = (bf16[15,32,128]{2,1,0:T(8,128)(2,1)S(1)}, bf16[15,32,128]{2,1,0:T(8,128)(2,1)S(1)}, u32[]{:S(2)}, u32[]{:S(2)}) collective-permute-start(bf16[15,32,128]{2,1,0:T(8,128)(2,1)S(1)} %get-tuple-element.24.here), channel_id=1, source_target_pairs={{0,16},{16,0},{32,48},{48,32},{64,80},{80,64},{96,112},{112,96},{1... | collective-permute-start | bytes 368648 | tf_op jit(solution)/shard_map/ppermute | solution.py:380
  16.7 18.6 %copy-start = (bf16[3,3,3,128,256]{4,3,2,1,0:T(8,128)(2,1)S(1)}, bf16[3,3,3,128,256]{4,3,2,1,0:T(8,128)(2,1)}, u32[]{:S(2)}) copy-start(bf16[3,3,3,128,256]{4,3,2,1,0:T(8,128)(2,1)} %param.5) | copy-start | bytes 5308420
  16.8 21.9 %all-to-all-start = ((bf16[16,16,1728]{2,1,0:T(8,128)(2,1)}), bf16[16,16,1728]{2,1,0:T(8,128)(2,1)S(1)}, u32[]{:S(2)}, u32[]{:S(2)}) async-start(bf16[16,16,1728]{2,1,0:T(8,128)(2,1)} %get-tuple-element.26), calls=%async_computation | async-start | bytes 1835008 | tf_op jit(solution)/shard_map/all_to_all | solution.py:388
  24.1 8.2 %collective-permute-start.2 = (bf16[12,32,128]{2,1,0:T(8,128)(2,1)S(1)}, bf16[12,32,128]{2,1,0:T(8,128)(2,1)S(1)}, u32[]{:S(2)}, u32[]{:S(2)}) collective-permute-start(bf16[12,32,128]{2,1,0:T(8,128)(2,1)S(1)} %get-tuple-element.27), channel_id=1, source_target_pairs={{0,32},{16,48},{32,64},{48,80},{64,96},{80,112},{96,128},{112,144}... | collective-permute-start | bytes 294920 | tf_op jit(solution)/shard_map/ppermute | solution.py:391
  27.3 5.1 %collective-permute-start.3 = (bf16[3,32,128]{2,1,0:T(8,128)(2,1)S(1)}, bf16[3,32,128]{2,1,0:T(8,128)(2,1)S(1)}, u32[]{:S(2)}, u32[]{:S(2)}) collective-permute-start(bf16[3,32,128]{2,1,0:T(8,128)(2,1)S(1)} %get-tuple-element.28), channel_id=1, source_target_pairs={{32,0},{48,16},{64,32},{80,48},{96,64},{112,80},{128,96},{144,112}... | collective-permute-start | bytes 73736 | tf_op jit(solution)/shard_map/ppermute | solution.py:392
  32.4 4.2 %collective-permute-start.4 = (bf16[45,32,128]{2,1,0:T(8,128)(2,1)S(1)}, bf16[45,32,128]{2,1,0:T(8,128)(2,1)S(1)}, u32[]{:S(2)}, u32[]{:S(2)}) collective-permute-start(bf16[45,32,128]{2,1,0:T(8,128)(2,1)S(1)} %shard_map.63.own), channel_id=1, source_target_pairs={{0,1},{1,0},{2,3},{3,2},{4,5},{5,4},{6,7},{7,6},{8,9},{9,8},{10,11... | collective-permute-start | bytes 1105928 | tf_op jit(solution)/shard_map/ppermute | solution.py:405
  41.1 16.7 %all-to-all-start.1 = ((bf16[16,7,16,128]{3,2,1,0:T(8,128)(2,1)}), bf16[16,7,16,128]{3,2,1,0:T(8,128)(2,1)S(1)}, u32[]{:S(2)}, u32[]{:S(2)}) async-start(bf16[16,7,16,128]{3,2,1,0:T(8,128)(2,1)} %get-tuple-element.40), calls=%async_computation.1 | async-start | bytes 917504 | tf_op jit(solution)/shard_map/all_to_all | solution.py:431
  47.8 5.7 %collective-permute-start.5 = (bf16[2,10,16,128]{3,2,1,0:T(8,128)(2,1)S(1)}, bf16[2,10,16,128]{3,2,1,0:T(8,128)(2,1)S(1)}, u32[]{:S(2)}, u32[]{:S(2)}) collective-permute-start(bf16[2,10,16,128]{3,2,1,0:T(8,128)(2,1)S(1)} %slice.3), channel_id=1, source_target_pairs={{32,0},{48,16},{64,32},{80,48},{96,64},{112,80},{128,96},{144,112}... | collective-permute-start | bytes 245768 | tf_op jit(solution)/shard_map/ppermute | solution.py:432
  54.6 22.3 %collective-permute-start.6 = (f32[4,4,16,256]{3,2,1,0:T(8,128)S(1)}, f32[4,4,16,256]{3,2,1,0:T(8,128)S(1)}, u32[]{:S(2)}, u32[]{:S(2)}) collective-permute-start(f32[4,4,16,256]{3,2,1,0:T(8,128)S(1)} %get-tuple-element.36._), channel_id=1, source_target_pairs={{0,1},{1,0},{2,3},{3,2},{4,5},{5,4},{6,7},{7,6},{8,9},{9,8},{10,11... | collective-permute-start | bytes 786440 | tf_op jit(solution)/shard_map/ppermute | solution.py:452
  58.6 25.9 %all-to-all-start.2 = ((bf16[16,16,128]{2,1,0:T(8,128)(2,1)}), bf16[16,16,128]{2,1,0:T(8,128)(2,1)S(1)}, u32[]{:S(2)}, u32[]{:S(2)}) async-start(bf16[16,16,128]{2,1,0:T(8,128)(2,1)} %shard_map.70), calls=%async_computation.2 | async-start | bytes 131072 | tf_op jit(solution)/shard_map/all_to_all | solution.py:451
  76.9 6.7 %collective-permute-start.7 = (bf16[2,4,16,256]{3,2,1,0:T(8,128)(2,1)S(1)}, bf16[2,4,16,256]{3,2,1,0:T(8,128)(2,1)S(1)}, u32[]{:S(2)}, u32[]{:S(2)}) collective-permute-start(bf16[2,4,16,256]{3,2,1,0:T(8,128)(2,1)S(1)} %get-tuple-element.38), channel_id=1, source_target_pairs={{0,16},{16,0},{32,48},{48,32},{64,80},{80,64},{96,112},{112,96},{1... | collective-permute-start | bytes 196616 | tf_op jit(solution)/shard_map/ppermute | solution.py:458
